TPU v7x, 32 devices: a whole 2x2x4 slice. The times are simulated.
32 devices in a mesh: rows: 8 (over y, x, core), tiles: 4 (over z).
Axes of the slice: x: 2, y: 2, z: 4, core: 2. Of those that a mesh axis runs over, the one named last changes fastest.
Arguments:
- embedding: bfloat16 [16384, 256], P('rows'), may hold values from -6 to 6
- start_block: float32 [64, 16384], P(None, ('rows', 'tiles')), may hold values from -4000 to 4000
- start_step: float32 [64, 16384], P(None, ('rows', 'tiles')), may hold values from -4000 to 4000
- rotations: float32 [2, 192, 64], replicated, may hold values from -0.4375 to 0.4375
- neighbour_cols: int32 [128, 48], P('rows', 'tiles'), may hold values from 0 to 127, as said below
- tile_counts: int32 [128], P('rows'), may hold values from 1 to 48, as said below
Outputs:
- block_out: float32 [64, 16384], P(None, ('rows', 'tiles'))
- step_out: float32 [64, 16384], P(None, ('rows', 'tiles'))
Inputs may be any that keep to these rules, and one draw needn't show every extreme that they name: `neighbour_cols`: slot 0 of row block b is b itself; slots 1 to tile_counts[b] - 1 hold distinct blocks c with 0 < |c - b| <= 32; later slots hold b or such blocks and are not used. `tile_counts`: at most the number of blocks c with |c - b| <= 32; 48 in some block of every draw.
All inputs are finite; a program needn't handle non-finite values.
Results may differ from a plain program's by a relative error of at most 0.007.
The roundings to bfloat16 on the way count: a program that leaves them out, or rounds other values in their place, can miss the bound.
Values may be sent and summed in bfloat16 or wider, within the bound.
No kernel may reach another device: no remote copies, remote signals or barrier semaphores. Data moves between devices by JAX's collectives and lax.ppermute only.
A program may use at most 64 MiB of HBM per device.

v0:
```python
import jax
import jax.numpy as jnp
from jax import lax
from jax.sharding import PartitionSpec as P

EMB = 256
K = 64
BR = 128
MAXT = 48
REACH = 2
ITERS = 2


TAU = 6.0
EPS = 1e-06
PRECISE = lax.Precision.HIGHEST


def shifted(value, axis, steps):
    count = lax.axis_size(axis)
    first, last = (max(0, -steps), min(count, count - steps))
    return lax.ppermute(value, axis, [(source, source + steps) for source in range(first, last)])


def normalize_rows(embedding):
    values = embedding.astype(jnp.float32)
    factor = lax.rsqrt(jnp.mean(values * values, axis=1, keepdims=True) + EPS)
    return (values * factor).astype(jnp.bfloat16)


def lobpcg_step(vectors, image, steps, rotation, own_share, total_rows):
    rayleigh = (
        lax.psum(
            jnp.dot(own_share(vectors), own_share(image).T, precision=PRECISE), ("rows", "tiles")
        )
        / total_rows
    )
    resid = image - jnp.dot(rayleigh.T, vectors, precision=PRECISE)
    resid_part = own_share(resid)
    resid_sq = lax.psum(jnp.sum(resid_part * resid_part, axis=1), ("rows", "tiles"))
    resid_rms = jnp.sqrt(resid_sq / total_rows + EPS)
    resid_unit = resid / resid_rms[:, None]
    basis = jnp.concatenate([vectors, resid_unit, steps], axis=0)
    combined = jnp.dot(rotation.T, basis, precision=PRECISE)
    combined_part = own_share(combined)
    combined_sq = lax.psum(jnp.sum(combined_part * combined_part, axis=1), ("rows", "tiles"))
    new_rms = jnp.sqrt(combined_sq / total_rows + EPS)
    new_steps = jnp.dot(rotation[K:].T, basis[K:], precision=PRECISE)
    return (combined / new_rms[:, None], new_steps / new_rms[:, None])


def local(embedding, start_block, start_step, rotations, neighbour_cols, tile_counts):
    tile_devices = lax.axis_size("tiles")
    share_len = start_block.shape[1]
    rows_here = share_len * tile_devices
    total_rows = rows_here * lax.axis_size("rows")
    blocks_here = tile_counts.shape[0]
    slot_span = neighbour_cols.shape[1]
    first_slot = lax.axis_index("tiles") * slot_span
    first_block = (lax.axis_index("rows") - REACH) * blocks_here
    local_cols = neighbour_cols - first_block
    live_slots = jnp.clip(tile_counts - first_slot, 0, slot_span)
    trip_count = jnp.max(live_slots)
    unit_own_rows = normalize_rows(embedding)
    neighbours = []
    for offset in range(-REACH, REACH + 1):
        if offset == 0:
            neighbours.append(unit_own_rows)
        else:
            neighbours.append(shifted(unit_own_rows, "rows", -offset))
    unit_ext = jnp.concatenate(neighbours, axis=0).reshape(-1, BR, EMB)
    unit_own = unit_own_rows.reshape(blocks_here, BR, EMB)
    start_sums = lax.psum(
        (jnp.sum(start_block * start_block, axis=1), jnp.sum(start_step * start_step, axis=1)),
        ("rows", "tiles"),
    )
    block_share = start_block / jnp.sqrt(start_sums[0] / total_rows + EPS)[:, None]
    step_share = start_step / jnp.sqrt(start_sums[1] / total_rows + EPS)[:, None]
    vectors, steps = (
        lax.all_gather(block_share, "tiles", axis=1, tiled=True),
        lax.all_gather(step_share, "tiles", axis=1, tiled=True),
    )
    own_start = lax.axis_index("tiles") * share_len

    def own_share(values):
        return lax.dynamic_slice_in_dim(values, own_start, share_len, 1)

    for iteration in range(ITERS):
        neighbours = []
        for offset in range(-REACH, REACH + 1):
            if offset == 0:
                neighbours.append(vectors)
            else:
                neighbours.append(
                    shifted(vectors.astype(jnp.bfloat16), "rows", -offset).astype(vectors.dtype)
                )
        vec_ext = jnp.concatenate(neighbours, axis=1).reshape(K, -1, BR)

        def add_slot(which_slot, running):
            col_index = lax.dynamic_index_in_dim(local_cols, which_slot, 1, keepdims=False)
            partner = jnp.take(unit_ext, col_index, axis=0)
            scores = jnp.einsum(
                "bie,bje->bij", unit_own, partner, preferred_element_type=jnp.float32
            )
            slot_mask = (which_slot < live_slots).astype(jnp.float32) / (BR * MAXT)
            weights = jnp.exp(scores * (TAU / EMB)) * slot_mask[:, None, None]
            inputs = jnp.take(vec_ext, col_index, axis=1)
            return running + jnp.einsum("bij,kbj->kbi", weights, inputs, precision=PRECISE)

        start_sum = jnp.zeros((K, blocks_here, BR), jnp.float32)
        image = lax.psum(
            lax.fori_loop(0, trip_count, add_slot, start_sum).reshape(K, blocks_here * BR), "tiles"
        )
        vectors, steps = lobpcg_step(
            vectors, image, steps, rotations[iteration], own_share, total_rows
        )
    return (own_share(vectors), own_share(steps))


def solution(mesh):
    return jax.shard_map(
        local,
        mesh=mesh,
        in_specs=(
            P("rows", None),
            P(None, ("rows", "tiles")),
            P(None, ("rows", "tiles")),
            P(),
            P("rows", "tiles"),
            P("rows"),
        ),
        out_specs=(P(None, ("rows", "tiles")), P(None, ("rows", "tiles"))),
        check_vma=False,
    )
```

profile of v0, /device:TPU:0, one launch (start us, length us, event | category | flops | bytes accessed | tf_op | source)
XLA Modules:
  0.0 747.6 jit_solution(9355483298774999050)
XLA Ops:
  8.3 42.0 %psum.70 = f32[64]{0:T(128)S(1)} all-reduce(f32[64]{0:T(128)S(1)} %multiply_reduce_fusion.5), channel_id=1, replica_groups=mesh['rows'=8,'tiles'=4] {'rows','tiles'}, use_global_device_ids=true, to_apply=%region_1.2 | all-reduce | flops 64 | bytes 512 | tf_op jit(solution)/shard_map/psum | solution.py:73
  51.4 15.9 %all_gather.6 = f32[64,2048]{1,0:T(8,128)S(1)} all-gather(f32[64,512]{1,0:T(8,128)S(1)} %broadcast_divide_fusion.4), channel_id=1, replica_groups=mesh['rows'=8,'tiles'=4] {'tiles'}, dimensions={1}, use_global_device_ids=true | all-gather | bytes 655360 | tf_op jit(solution)/shard_map/all_gather | solution.py:80
  67.3 5.0 collective-permute-start
  79.9 5.7 collective-permute-start.4
  94.7 14.6 %collective-permute-done.4 = bf16[2048,256]{1,0:T(8,128)(2,1)S(1)} collective-permute-done((bf16[2048,256]{1,0:T(8,128)(2,1)}, bf16[2048,256]{1,0:T(8,128)(2,1)S(1)}, u32[]{:S(2)}, u32[]{:S(2)}) %collective-permute-start.4) | collective-permute-done | bytes 1048608 | tf_op jit(solution)/shard_map/ppermute | solution.py:22
  109.9 46.1 %collective-permute-done.7 = bf16[2048,256]{1,0:T(8,128)(2,1)S(1)} collective-permute-done((bf16[2048,256]{1,0:T(8,128)(2,1)}, bf16[2048,256]{1,0:T(8,128)(2,1)S(1)}, u32[]{:S(2)}, u32[]{:S(2)}) %collective-permute-start.7) | collective-permute-done | bytes 1048608 | tf_op jit(solution)/shard_map/ppermute | solution.py:22
  158.4 109.5 %while.20 = (s32[]{:T(128)}, f32[64,16,128]{2,0,1:T(8,128)S(1)}, s32[]{:T(128)}, s32[16,12]{0,1:T(8,128)S(1)}, f32[64,80,128]{2,0,1:T(8,128)}, /*index=5*/bf16[8...) while((s32[]{:T(128)}, f32[64,16,128]{2,0,1:T(8,128)S(1)}, ...), condition=%wide.region_5.8_spmd, body=%wide.region_4.7_spmd.sunk | while | flops 336856192 | bytes 8917703 | solution.py:112
  159.1 3.1 gather_fusion
  168.2 3.1 gather_fusion
  177.3 3.1 gather_fusion
  186.4 3.1 gather_fusion
  195.4 3.1 gather_fusion
  204.5 3.1 gather_fusion
  213.6 3.1 gather_fusion
  222.6 3.1 gather_fusion
  231.7 3.1 gather_fusion
  240.8 3.1 gather_fusion
  249.8 3.1 gather_fusion
  258.9 3.1 gather_fusion
  269.0 35.3 %all-reduce.4.cloned.1.call-done = f32[64,2048]{1,0:T(8,128)} async-done(((f32[64,2048]{1,0:T(8,128)}), f32[64,2048]{1,0:T(8,128)}) %all-reduce.4.cloned.1.call-update) | async-done | bytes 524304 | tf_op jit(solution)/shard_map/psum | solution.py:111
  305.4 40.1 %psum.72 = f32[64,64]{1,0:T(8,128)S(1)} all-reduce(f32[64,64]{1,0:T(8,128)S(1)} %fusion.50), channel_id=1, replica_groups=mesh['rows'=8,'tiles'=4] {'rows','tiles'}, use_global_device_ids=true, to_apply=%region_7.0 | all-reduce | flops 4096 | bytes 32768 | tf_op jit(solution)/shard_map/psum | solution.py:33
  347.3 39.5 %all-reduce = (f32[64]{0:T(128)S(1)}, f32[64]{0:T(128)S(1)}) all-reduce(f32[64]{0:T(128)S(1)} %multiply_reduce_fusion.3, f32[64]{0:T(128)S(1)} %multiply_reduce_fusion.4), channel_id=1, replica_groups=mesh['rows'=8,'tiles'=4] {'rows','tiles'}, use_global_device_ids=true, to_apply=%region_11.14 | all-reduce | flops 128 | bytes 1024 | tf_op jit(solution)/shard_map/psum | solution.py:73
  387.0 15.9 %all_gather.7 = f32[64,2048]{1,0:T(8,128)S(1)} all-gather(f32[64,512]{1,0:T(8,128)S(1)} %broadcast_divide_fusion.3), channel_id=1, replica_groups=mesh['rows'=8,'tiles'=4] {'tiles'}, dimensions={1}, use_global_device_ids=true | all-gather | bytes 655360 | tf_op jit(solution)/shard_map/all_gather | solution.py:81
  404.2 39.8 %psum.75 = f32[64]{0:T(128)S(1)} all-reduce(f32[64]{0:T(128)S(1)} %multiply_reduce_fusion.2), channel_id=1, replica_groups=mesh['rows'=8,'tiles'=4] {'rows','tiles'}, use_global_device_ids=true, to_apply=%region_13.16 | all-reduce | flops 64 | bytes 512 | tf_op jit(solution)/shard_map/psum | solution.py:46
  444.1 4.2 collective-permute-start.8
  454.8 10.7 %collective-permute-done.11 = bf16[64,2048]{1,0:T(8,128)(2,1)S(1)} collective-permute-done((bf16[64,2048]{1,0:T(8,128)(2,1)S(1)}, bf16[64,2048]{1,0:T(8,128)(2,1)S(1)}, u32[]{:S(2)}, u32[]{:S(2)}) %collective-permute-start.11) | collective-permute-done | bytes 262176 | tf_op jit(solution)/shard_map/ppermute | solution.py:22
  467.4 109.7 %while.21 = (s32[]{:T(128)}, f32[64,16,128]{2,0,1:T(8,128)S(1)}, s32[]{:T(128)}, s32[16,12]{0,1:T(8,128)S(1)}, f32[64,80,128]{2,0,1:T(8,128)}, /*index=5*/bf16[8...) while((s32[]{:T(128)}, f32[64,16,128]{2,0,1:T(8,128)S(1)}, ...), condition=%wide.region_15.18_spmd, body=%wide.region_14.17_spmd.sunk | while | flops 336856192 | bytes 8917703 | solution.py:112
  468.3 3.1 gather_fusion.2
  579.9 34.8 %all-reduce.6.cloned.1.call-done = f32[64,2048]{1,0:T(8,128)} async-done(((f32[64,2048]{1,0:T(8,128)}), f32[64,2048]{1,0:T(8,128)}) %all-reduce.6.cloned.1.call-update) | async-done | bytes 524304 | tf_op jit(solution)/shard_map/psum | solution.py:111
  615.9 40.1 %psum.77 = f32[64,64]{1,0:T(8,128)S(1)} all-reduce(f32[64,64]{1,0:T(8,128)S(1)} %fusion.47), channel_id=1, replica_groups=mesh['rows'=8,'tiles'=4] {'rows','tiles'}, use_global_device_ids=true, to_apply=%region_17.20 | all-reduce | flops 4096 | bytes 32768 | tf_op jit(solution)/shard_map/psum | solution.py:33
  657.7 39.5 %psum.78 = f32[64]{0:T(128)S(1)} all-reduce(f32[64]{0:T(128)S(1)} %multiply_reduce_fusion.1), channel_id=1, replica_groups=mesh['rows'=8,'tiles'=4] {'rows','tiles'}, use_global_device_ids=true, to_apply=%region_19.22 | all-reduce | flops 64 | bytes 512 | tf_op jit(solution)/shard_map/psum | solution.py:40
  699.3 40.6 %psum.79 = f32[64]{0:T(128)S(1)} all-reduce(f32[64]{0:T(128)S(1)} %multiply_reduce_fusion), channel_id=1, replica_groups=mesh['rows'=8,'tiles'=4] {'rows','tiles'}, use_global_device_ids=true, to_apply=%region_21.24 | all-reduce | flops 64 | bytes 512 | tf_op jit(solution)/shard_map/psum | solution.py:46
  (247 shorter events, 204.4 us)
Async XLA Ops:
  7.2 71.3 %copy-start.1 = (bf16[2048,256]{1,0:T(8,128)(2,1)S(1)}, bf16[2048,256]{1,0:T(8,128)(2,1)}, u32[]{:S(2)}) copy-start(bf16[2048,256]{1,0:T(8,128)(2,1)} %param.14) | copy-start | bytes 3145732
  7.2 78.4 %copy-start.7 = (s32[16]{0:T(128)S(1)}, s32[16]{0:T(128)}, u32[]{:S(2)}) copy-start(s32[16]{0:T(128)} %param.19) | copy-start | bytes 196
  7.2 79.0 %copy-start.6 = (s32[16,12]{1,0:T(8,128)S(1)}, s32[16,12]{1,0:T(8,128)}, u32[]{:S(2)}) copy-start(s32[16,12]{1,0:T(8,128)} %param.18) | copy-start | bytes 2308
  7.2 297.1 %all-reduce.4.cloned.1.call-start = ((), (), s32[]{:S(2)}) async-start(), calls=%async_computation | async-start | bytes 1048576 | tf_op jit(solution)/shard_map/psum | solution.py:111
  67.3 19.0 %collective-permute-start = (bf16[64,2048]{1,0:T(8,128)(2,1)S(1)}, bf16[64,2048]{1,0:T(8,128)(2,1)}, u32[]{:S(2)}, u32[]{:S(2)}) collective-permute-start(bf16[64,2048]{1,0:T(8,128)(2,1)S(1)} %convert_element_type.46), channel_id=1, source_target_pairs={{0,8},{4,12},{8,16},{12,20},{16,24},{20,28},{1,9},{5,13},{9,17},{1... | collective-permute-start | bytes 786440 | tf_op jit(solution)/shard_map/ppermute | solution.py:22
  72.3 16.8 %collective-permute-start.1 = (bf16[64,2048]{1,0:T(8,128)(2,1)S(1)}, bf16[64,2048]{1,0:T(8,128)(2,1)}, u32[]{:S(2)}, u32[]{:S(2)}) collective-permute-start(bf16[64,2048]{1,0:T(8,128)(2,1)S(1)} %convert_element_type.46), channel_id=1, source_target_pairs={{0,4},{4,8},{8,12},{12,16},{16,20},{20,24},{24,28},{1,5},{5,9},{9,... | collective-permute-start | bytes 786440 | tf_op jit(solution)/shard_map/ppermute | solution.py:22
  74.3 17.2 %collective-permute-start.2 = (bf16[64,2048]{1,0:T(8,128)(2,1)S(1)}, bf16[64,2048]{1,0:T(8,128)(2,1)S(1)}, u32[]{:S(2)}, u32[]{:S(2)}) collective-permute-start(bf16[64,2048]{1,0:T(8,128)(2,1)S(1)} %convert_element_type.46), channel_id=1, source_target_pairs={{4,0},{8,4},{12,8},{16,12},{20,16},{24,20},{28,24},{5,1},{9,5},{13... | collective-permute-start | bytes 786440 | tf_op jit(solution)/shard_map/ppermute | solution.py:22
  75.5 17.2 %collective-permute-start.3 = (bf16[64,2048]{1,0:T(8,128)(2,1)S(1)}, bf16[64,2048]{1,0:T(8,128)(2,1)S(1)}, u32[]{:S(2)}, u32[]{:S(2)}) collective-permute-start(bf16[64,2048]{1,0:T(8,128)(2,1)S(1)} %convert_element_type.46), channel_id=1, source_target_pairs={{8,0},{12,4},{16,8},{20,12},{24,16},{28,20},{9,1},{13,5},{17,9},{2... | collective-permute-start | bytes 786440 | tf_op jit(solution)/shard_map/ppermute | solution.py:22
  79.9 29.4 %collective-permute-start.4 = (bf16[2048,256]{1,0:T(8,128)(2,1)}, bf16[2048,256]{1,0:T(8,128)(2,1)S(1)}, u32[]{:S(2)}, u32[]{:S(2)}) collective-permute-start(bf16[2048,256]{1,0:T(8,128)(2,1)} %fusion.26), channel_id=1, source_target_pairs={{0,8},{4,12},{8,16},{12,20},{16,24},{20,28},{1,9},{5,13},{9,17},{1... | collective-permute-start | bytes 3145736 | tf_op jit(solution)/shard_map/ppermute | solution.py:22
  86.3 23.1 %collective-permute-start.5 = (bf16[2048,256]{1,0:T(8,128)(2,1)}, bf16[2048,256]{1,0:T(8,128)(2,1)S(1)}, u32[]{:S(2)}, u32[]{:S(2)}) collective-permute-start(bf16[2048,256]{1,0:T(8,128)(2,1)} %fusion.26), channel_id=1, source_target_pairs={{0,4},{4,8},{8,12},{12,16},{16,20},{20,24},{24,28},{1,5},{5,9},{9,... | collective-permute-start | bytes 3145736 | tf_op jit(solution)/shard_map/ppermute | solution.py:22
  89.1 20.7 %collective-permute-start.6 = (bf16[2048,256]{1,0:T(8,128)(2,1)}, bf16[2048,256]{1,0:T(8,128)(2,1)S(1)}, u32[]{:S(2)}, u32[]{:S(2)}) collective-permute-start(bf16[2048,256]{1,0:T(8,128)(2,1)} %fusion.26), channel_id=1, source_target_pairs={{4,0},{8,4},{12,8},{16,12},{20,16},{24,20},{28,24},{5,1},{9,5},{13... | collective-permute-start | bytes 3145736 | tf_op jit(solution)/shard_map/ppermute | solution.py:22
  91.4 64.6 %collective-permute-start.7 = (bf16[2048,256]{1,0:T(8,128)(2,1)}, bf16[2048,256]{1,0:T(8,128)(2,1)S(1)}, u32[]{:S(2)}, u32[]{:S(2)}) collective-permute-start(bf16[2048,256]{1,0:T(8,128)(2,1)} %fusion.26), channel_id=1, source_target_pairs={{8,0},{12,4},{16,8},{20,12},{24,16},{28,20},{9,1},{13,5},{17,9},{2... | collective-permute-start | bytes 3145736 | tf_op jit(solution)/shard_map/ppermute | solution.py:22
  156.1 2.3 copy-start
  158.4 110.5 %copy-start.4 = (f32[64,512]{1,0:T(8,128)S(1)}, f32[64,512]{1,0:T(8,128)}, u32[]{:S(2)}) copy-start(f32[64,512]{1,0:T(8,128)} %param.16) | copy-start | bytes 393220
  268.8 134.1 %copy-start.5 = (f32[2,192,64]{1,2,0:T(8,128)S(1)}, f32[2,192,64]{1,2,0:T(8,128)}, u32[]{:S(2)}) copy-start(f32[2,192,64]{1,2,0:T(8,128)} %param.17) | copy-start | bytes 294916
  268.8 345.9 %all-reduce.6.cloned.1.call-start = ((), (), s32[]{:S(2)}) async-start(), calls=%async_computation.1 | async-start | bytes 1048576 | tf_op jit(solution)/shard_map/psum | solution.py:111
  386.9 17.1 %copy-start.3 = (f32[64,2048]{1,0:T(8,128)}, f32[64,2048]{1,0:T(8,128)S(1)}, u32[]{:S(2)}) copy-start(f32[64,2048]{1,0:T(8,128)S(1)} %broadcast_divide_fusion.2) | copy-start | bytes 1572868
  402.9 1.2 copy-start.2
  444.1 8.3 %collective-permute-start.8 = (bf16[64,2048]{1,0:T(8,128)(2,1)S(1)}, bf16[64,2048]{1,0:T(8,128)(2,1)S(1)}, u32[]{:S(2)}, u32[]{:S(2)}) collective-permute-start(bf16[64,2048]{1,0:T(8,128)(2,1)S(1)} %get-tuple-element.146), channel_id=1, source_target_pairs={{0,8},{4,12},{8,16},{12,20},{16,24},{20,28},{1,9},{5,13},{9,17},{1... | collective-permute-start | bytes 786440 | tf_op jit(solution)/shard_map/ppermute | solution.py:22
  448.3 4.2 collective-permute-start.9
  449.6 5.1 collective-permute-start.10
  450.9 14.6 %collective-permute-start.11 = (bf16[64,2048]{1,0:T(8,128)(2,1)S(1)}, bf16[64,2048]{1,0:T(8,128)(2,1)S(1)}, u32[]{:S(2)}, u32[]{:S(2)}) collective-permute-start(bf16[64,2048]{1,0:T(8,128)(2,1)S(1)} %get-tuple-element.146), channel_id=1, source_target_pairs={{8,0},{12,4},{16,8},{20,12},{24,16},{28,20},{9,1},{13,5},{17,9},{2... | collective-permute-start | bytes 786440 | tf_op jit(solution)/shard_map/ppermute | solution.py:22
Sparse Core Ops, SparseCore 0:
  268.9 35.2 all-reduce.3
  578.1 36.5 all-reduce.5
where the time goes:
time: 753 us; the launch traced here: 748 us
  blocking collectives  313 us (42%)
  waiting for transfers between devices  144 us (19%)
  local copies, waits for them, and re-layouts  138 us (18%)
  matrix products  80.3 us (11%)
  starting transfers between devices  27.8 us (4%)
  loops' own time  18.7 us (2%)
  between operations  14.5 us (2%)
  other arithmetic  10.8 us (1%)
    psum x2, blocking collectives, local(): lax.psum((jnp.sum(start_block * start_block, axis=1), jnp.sum(start_step...  81.5 us
    psum x2, blocking collectives, lobpcg_step(): lax.psum(jnp.sum(combined_part * combined_part, axis=1), ('rows', 'tiles'))  80.4 us
    psum x2, blocking collectives, lobpcg_step(): lax.psum(jnp.dot(own_share(vectors), own_share(image).T, precision=PRECIS...  80.1 us
    gather x24, local copies, waits for them, and re-layouts, add_slot(): partner = jnp.take(unit_ext, col_index, axis=0)  74.4 us
    ppermute x12, waiting for transfers between devices, shifted(): lax.ppermute(value, axis, [(source, source + steps) for source in range(f...  73.8 us
    psum x2, waiting for transfers between devices, local(): lax.psum(lax.fori_loop(0, trip_count, add_slot, start_sum).reshape(K, blo...  70.1 us
    gather x24, local copies, waits for them, and re-layouts, add_slot(): inputs = jnp.take(vec_ext, col_index, axis=1)  55.7 us
    dot_general x24, matrix products, add_slot(): jnp.einsum('bie,bje->bij', unit_own, partner, preferred_element_type=jnp....  41.3 us
  transfers between devices with their start and end apart: 14, of which 7 were waited for; matrix products, arithmetic and copies ran while one was open for 1% of the time, Pallas kernels for 0%

commit v1 on v0

v1 whole, which is shorter than its diff:
```python
import functools
import math

import jax
import jax.numpy as jnp
from jax import lax
from jax.experimental import pallas as pl
from jax.experimental.pallas import tpu as pltpu
from jax.sharding import PartitionSpec as P

EMB = 256
K = 64
BR = 128
MAXT = 48
REACH = 2
ITERS = 2

TAU = 6.0
EPS = 1e-06
PRECISE = lax.Precision.HIGHEST

WEIGHT = 1.0 / (BR * MAXT)
SIGMA = math.exp(TAU) * WEIGHT
EXP2 = TAU / EMB * math.log2(math.e)
GROUP = 8
SHARDS = 6
F32 = jnp.float32
BF16 = jnp.bfloat16
VMEM = pl.BlockSpec(memory_space=pltpu.VMEM)
SMEM = pl.BlockSpec(memory_space=pltpu.SMEM)


def params():
    return pltpu.CompilerParams(vmem_limit_bytes=48 * 1024 * 1024)


def swapped(value, axis, bits):
    count = lax.axis_size(axis)
    return lax.ppermute(value, axis, [(i, i ^ bits) for i in range(count)])


def rotated(value, axis, steps):
    count = lax.axis_size(axis)
    return lax.ppermute(value, axis, [(i, (i + steps) % count) for i in range(count)])


def other_side(value):
    count = lax.axis_size("rows")
    chips = count // 2
    pairs = []
    for r in range(count):
        chip, core = divmod(r, 2)
        to = (chip + 1) % chips if chip % 2 else (chip - 1) % chips
        pairs.append((r, to * 2 + core))
    return lax.ppermute(value, "rows", pairs)


def chip_halo(value):
    side_a = swapped(value, "rows", 2)
    side_b = other_side(value)
    core = swapped(value, "rows", 1)
    return [
        value, core, side_a, swapped(side_a, "rows", 1), side_b, swapped(side_b, "rows", 1)
    ]


def total_over(value, axis, first):
    count = lax.axis_size(axis)
    bits = first
    while bits < count:
        span = min(4, count // bits)
        value = value + sum(swapped(value, axis, k * bits) for k in range(1, span))
        bits *= span
    return value


def total_over_all(value):
    value = value + swapped(value, "rows", 1)
    value = total_over(value, "rows", 2)
    return total_over(value, "tiles", 1)


def dot_t(a, b):
    return lax.dot_general(a, b, (((1,), (1,)), ((), ())), preferred_element_type=F32)


def unit_of(rows):
    values = rows.astype(F32)
    mean = jnp.sum(values * values, axis=1, keepdims=True) * (1.0 / EMB)
    return (values * lax.rsqrt(mean + EPS)).astype(BF16)


def apply_kernel(blocks, share, devices, *refs):
    meta, items = refs[:2]
    own_emb = refs[2]
    emb = refs[3 : 2 + SHARDS]
    vec = refs[2 + SHARDS : 2 + 2 * SHARDS]
    rest = refs[2 + 2 * SHARDS :]
    own_out, outs = rest[0], rest[1 : 1 + 2 * (devices - 1)]
    diag_out, tiles, unit_own, unit_ext, vec_ext, acc = rest[1 + 2 * (devices - 1) :]
    count, here = meta[0], meta[1]

    @pl.loop(0, blocks)
    def _(b):
        unit_own[b] = unit_of(own_emb[b])

    for i in range(share):
        unit_ext[i] = unit_own[here * share + i]
    for j, ref in enumerate(emb):
        for i in range(share):
            unit_ext[(j + 1) * share + i] = unit_of(ref[pl.ds(i * BR, BR), :])
    for j, ref in enumerate(vec):
        for i in range(share):
            vec_ext[j * share + i] = ref[:, pl.ds(i * BR, BR)]
    acc[...] = jnp.zeros_like(acc)

    rows = lax.broadcasted_iota(jnp.int32, (BR, BR), 0)
    cols = lax.broadcasted_iota(jnp.int32, (BR, BR), 1)
    for i in range(share):
        unit = unit_ext[i]
        weights = jnp.exp2(dot_t(unit, unit) * EXP2)
        on_diag = rows == cols
        diag_out[:, pl.ds(i * BR, BR)] = jnp.sum(
            jnp.where(on_diag, weights, 0.0), axis=0, keepdims=True
        )
        off = jnp.where(on_diag, 0.0, weights).astype(BF16)
        tiles[i] = off
        acc[here * share + i] = jnp.dot(vec_ext[i], off, preferred_element_type=F32)

    @pl.loop(0, (count + GROUP - 1) // GROUP)
    def _(step):
        picked = []
        for g in range(GROUP):
            at = step * GROUP + g
            flat = items[at]
            ext, own = flat // blocks, flat % blocks
            picked.append((ext, own, jnp.where(at < count, own, blocks)))
        scores = [dot_t(unit_ext[ext], unit_own[own]) for ext, own, _ in picked]
        weights = [jnp.exp2(s * EXP2).astype(BF16) for s in scores]
        for g in range(GROUP):
            tiles[share + step * GROUP + g] = weights[g]
        parts = [
            jnp.dot(vec_ext[ext], w, preferred_element_type=F32)
            for (ext, _, _), w in zip(picked, weights)
        ]
        for (_, _, to), part in zip(picked, parts):
            acc[to] += part

    for j in range(devices):
        first = lax.rem(here + j, devices) * share
        for i in range(share):
            part = acc[first + i]
            at = pl.ds(i * BR, BR)
            if j == 0:
                own_out[:, at] = part
            else:
                outs[2 * (j - 1)][:, at] = part[:K].astype(BF16)
                outs[2 * (j - 1) + 1][:, at] = part[K:].astype(BF16)


def again_kernel(blocks, share, devices, *refs):
    meta, items, tiles = refs[:3]
    vec = refs[3 : 3 + SHARDS]
    outs = refs[3 + SHARDS : 3 + SHARDS + devices]
    vec_ext, acc = refs[3 + SHARDS + devices :]
    count, here = meta[0], meta[1]
    for j, ref in enumerate(vec):
        for i in range(share):
            vec_ext[j * share + i] = ref[:, pl.ds(i * BR, BR)]
    acc[...] = jnp.zeros_like(acc)
    for i in range(share):
        acc[here * share + i] = jnp.dot(vec_ext[i], tiles[i], preferred_element_type=F32)

    @pl.loop(0, (count + GROUP - 1) // GROUP)
    def _(step):
        picked = []
        for g in range(GROUP):
            at = step * GROUP + g
            flat = items[at]
            picked.append((flat // blocks, jnp.where(at < count, flat % blocks, blocks)))
        parts = [
            jnp.dot(vec_ext[ext], tiles[share + step * GROUP + g], preferred_element_type=F32)
            for g, (ext, _) in enumerate(picked)
        ]
        for (_, to), part in zip(picked, parts):
            acc[to] += part

    for j in range(devices):
        first = lax.rem(here + j, devices) * share
        for i in range(share):
            outs[j][:, pl.ds(i * BR, BR)] = acc[first + i].astype(outs[j].dtype)


def mul(a, b):
    return jnp.dot(a, b, precision=PRECISE, preferred_element_type=F32)


def step_coefficients(g_vv, g_vs, g_ss, g_vj, g_sj, g_jj, rotation, total):
    eye = (
        lax.broadcasted_iota(jnp.int32, (K, K), 0) == lax.broadcasted_iota(jnp.int32, (K, K), 1)
    )
    m = g_vj * (1.0 / total) + SIGMA * (g_vv * (1.0 / total) - eye.astype(F32))
    resid_sq = (
        jnp.sum(jnp.where(eye, g_jj, 0.0), axis=0, keepdims=True)
        - 2.0 * jnp.sum(m * g_vj, axis=0, keepdims=True)
        + jnp.sum(m * mul(g_vv, m), axis=0, keepdims=True)
    )
    resid_inv = 1.0 / jnp.sqrt(jnp.maximum(resid_sq, 0.0) * (1.0 / total) + EPS)
    on_v, on_resid, on_s = rotation[:K].T, rotation[K : 2 * K].T, rotation[2 * K :].T
    p_j = on_resid * resid_inv
    p_step = -mul(p_j, m.T)
    p_v = jnp.concatenate([on_v + p_step, p_step], axis=0)
    p_s, p_j = jnp.concatenate([on_s, on_s], axis=0), jnp.concatenate([p_j, p_j], axis=0)
    g_v = mul(p_v, g_vv) + mul(p_j, g_vj.T) + mul(p_s, g_vs.T)
    g_s = mul(p_v, g_vs) + mul(p_j, g_sj.T) + mul(p_s, g_ss)
    g_j = mul(p_v, g_vj) + mul(p_j, g_jj) + mul(p_s, g_sj)
    comb_sq = jnp.sum((g_v * p_v + g_s * p_s + g_j * p_j)[:K], axis=1, keepdims=True)
    scale = 1.0 / jnp.sqrt(jnp.maximum(comb_sq, 0.0) * (1.0 / total) + EPS)
    scale = jnp.concatenate([scale, scale], axis=0)
    return scale * p_v, scale * p_s, scale * p_j, scale * g_v, scale * g_s, scale * g_j


def gram_kernel(a_ref, b_ref, j_ref, out_ref):
    x, y, j = a_ref[...], b_ref[...], j_ref[...]
    pairs = ((x, x), (x, y), (y, y), (x, j), (y, j), (j, j))
    for n, (a, b) in enumerate(pairs):
        out_ref[n] = lax.dot_general(
            a, b, (((1,), (1,)), ((), ())), precision=PRECISE, preferred_element_type=F32
        )


def first_kernel(total, g_ref, rot_ref, x_ref, y_ref, j_ref, t_ref, v_out, s_out, part_out, c_out, g_out):
    eye = (
        lax.broadcasted_iota(jnp.int32, (K, K), 0) == lax.broadcasted_iota(jnp.int32, (K, K), 1)
    )
    xx, xy, yy, xj, yj, jj = (g_ref[n] for n in range(6))

    def inv_rms(square, axis):
        picked = jnp.sum(jnp.where(eye, square, 0.0), axis=axis, keepdims=True)
        return 1.0 / jnp.sqrt(picked * (1.0 / total) + EPS)

    x_col, x_row = inv_rms(xx, 1), inv_rms(xx, 0)
    y_col, y_row = inv_rms(yy, 1), inv_rms(yy, 0)
    g_vv, g_vs, g_ss = xx * x_col * x_row, xy * x_col * y_row, yy * y_col * y_row
    g_vj, g_sj, g_jj = xj * x_col * x_row, yj * y_col * x_row, jj * x_col * x_row
    p_v, p_s, p_j, g_v, g_s, g_j = step_coefficients(
        g_vv, g_vs, g_ss, g_vj, g_sj, g_jj, rot_ref[...], total
    )
    new = mul(g_v, p_v.T) + mul(g_s, p_s.T) + mul(g_j, p_j.T)
    g_out[0], g_out[1], g_out[2] = new[:K, :K], new[:K, K:], new[K:, K:]
    p_v, p_j, p_s = p_v * x_row, p_j * x_row, p_s * y_row
    x, y, j, t = x_ref[...], y_ref[...], j_ref[...], t_ref[...]
    both = mul(p_v, x) + mul(p_s, y) + mul(p_j, j)
    v_out[...], s_out[...] = both[:K], both[K:]
    part_out[...] = mul(p_v[:K], j) + mul(p_s[:K], t)
    c_out[...] = p_j[:K]


def second_kernel(v_ref, s_ref, part_ref, c_ref, q_ref, j_out, g_out):
    j = part_ref[...] + mul(c_ref[...], q_ref[...])
    j_out[...] = j
    for n, a in enumerate((v_ref[...], s_ref[...], j)):
        g_out[n] = lax.dot_general(
            a, j, (((1,), (1,)), ((), ())), precision=PRECISE, preferred_element_type=F32
        )


def last_kernel(total, g_ref, h_ref, rot_ref, v_ref, s_ref, j_ref, v_out, s_out):
    p_v, p_s, p_j, _, _, _ = step_coefficients(
        g_ref[0], g_ref[1], g_ref[2], h_ref[0], h_ref[1], h_ref[2], rot_ref[...], total
    )
    both = mul(p_v, v_ref[...]) + mul(p_s, s_ref[...]) + mul(p_j, j_ref[...])
    v_out[...], s_out[...] = both[:K], both[K:]


def call(kernel, outs, *args, smem=0, scratch=(), out_specs=None):
    return pl.pallas_call(
        kernel,
        out_shape=tuple(jax.ShapeDtypeStruct(shape, dtype) for shape, dtype in outs),
        in_specs=[SMEM] * smem + [VMEM] * (len(args) - smem),
        out_specs=tuple(out_specs or [VMEM] * len(outs)),
        scratch_shapes=list(scratch),
        compiler_params=params(),
    )(*args)


def tile_list(cols, counts, here, row, share, devices):
    blocks, span = cols.shape
    flat = blocks * SHARDS * share
    used = []
    for step in range(devices):
        part = cols if step == 0 else rotated(cols, "tiles", step)
        first = lax.rem(here - step + devices, devices) * span
        slot = first + lax.broadcasted_iota(jnp.int32, (blocks, span), 1)
        used.append((part, slot))
    col = jnp.concatenate([part for part, _ in used], axis=1)
    slot = jnp.concatenate([s for _, s in used], axis=1)
    block = row * blocks + lax.broadcasted_iota(jnp.int32, col.shape, 0)
    shard, inner = col // blocks, col % blocks
    other_core = (shard % 2 != row % 2).astype(jnp.int32)
    chip, own_chip = shard // 2, row // 2
    place = other_core + jnp.where(chip == own_chip, 0, jnp.where(chip == own_chip ^ 1, 2, 4))
    mine = (slot < counts[:, None]) & (inner // share == here) & (col != block)
    ext = jnp.where(mine, place * share + inner % share, -1)
    wanted = lax.broadcasted_iota(jnp.int32, (SHARDS * share, blocks, 1), 0)
    mask = jnp.any(ext[None] == wanted, axis=2).astype(F32).reshape(flat)
    index = jnp.arange(flat, dtype=jnp.int32)
    before = (index[:, None] < index[None, :]).astype(F32)
    place = jnp.dot(mask, before).astype(jnp.int32)
    hit = (place[:, None] == index[None, :]) & (mask[:, None] > 0)
    items = jnp.sum(jnp.where(hit, index[:, None], 0), axis=0)
    count = jnp.sum(mask).astype(jnp.int32)
    return jnp.concatenate([items, jnp.zeros((GROUP,), jnp.int32)]), jnp.stack([count, here])


def local(embedding, start_block, start_step, rotations, neighbour_cols, tile_counts):
    devices = lax.axis_size("tiles")
    width = start_block.shape[1]
    share = width // BR
    blocks = tile_counts.shape[0]
    total = width * devices * lax.axis_size("rows")
    here, row = lax.axis_index("tiles"), lax.axis_index("rows")
    flat = blocks * SHARDS * share

    own_emb = lax.dynamic_slice_in_dim(embedding, here * width, width, 0)
    emb = chip_halo(own_emb)
    vec = chip_halo(jnp.concatenate([start_block, start_step], axis=0).astype(BF16))
    items, meta = tile_list(neighbour_cols, tile_counts, here, row, share, devices)

    tiles_shape = ((share + flat + GROUP, BR, BR), BF16)
    outs = call(
        functools.partial(apply_kernel, blocks, share, devices),
        [((2 * K, width), F32)]
        + [((K, width), BF16)] * (2 * (devices - 1))
        + [((1, width), F32), tiles_shape],
        meta,
        items,
        embedding.reshape(blocks, BR, EMB),
        *emb[1:],
        *vec,
        smem=2,
        scratch=[
            pltpu.VMEM((blocks, BR, EMB), BF16),
            pltpu.VMEM((SHARDS * share, BR, EMB), BF16),
            pltpu.VMEM((SHARDS * share, 2 * K, BR), BF16),
            pltpu.VMEM((blocks + 1, 2 * K, BR), F32),
        ],
    )
    own, sent, diag, tiles = outs[0], outs[1:-2], outs[-2], outs[-1]
    diag = diag * WEIGHT - SIGMA

    def collect(own_part, parts, vectors):
        got = own_part
        for n, part in enumerate(parts):
            got = got + rotated(part, "tiles", n + 1).astype(F32)
        return got * WEIGHT + diag * vectors

    image = collect(own[:K], sent[0::2], start_block)
    image_vec = chip_halo(image.astype(BF16))
    step_image = collect(own[K:], sent[1::2], start_step)

    gram = total_over_all(
        call(gram_kernel, [((6, K, K), F32)], start_block, start_step, image)[0]
    )
    vectors, steps, part, coef, gram = call(
        functools.partial(first_kernel, total),
        [((K, width), F32)] * 3 + [((K, K), F32), ((3, K, K), F32)],
        gram,
        rotations[0],
        start_block,
        start_step,
        image,
        step_image,
    )

    outs = call(
        functools.partial(again_kernel, blocks, share, devices),
        [((K, width), F32)] + [((K, width), BF16)] * (devices - 1),
        meta,
        items,
        tiles,
        *image_vec,
        smem=2,
        scratch=[
            pltpu.VMEM((SHARDS * share, K, BR), BF16),
            pltpu.VMEM((blocks + 1, K, BR), F32),
        ],
    )
    twice = collect(outs[0], outs[1:], image)
    image, products = call(
        second_kernel,
        [((K, width), F32), ((3, K, K), F32)],
        vectors,
        steps,
        part,
        coef,
        twice,
    )
    products = total_over_all(products)
    return call(
        functools.partial(last_kernel, total),
        [((K, width), F32)] * 2,
        gram,
        products,
        rotations[1],
        vectors,
        steps,
        image,
    )


def solution(mesh):
    return jax.shard_map(
        local,
        mesh=mesh,
        in_specs=(
            P("rows", None),
            P(None, ("rows", "tiles")),
            P(None, ("rows", "tiles")),
            P(),
            P("rows", "tiles"),
            P("rows"),
        ),
        out_specs=(P(None, ("rows", "tiles")), P(None, ("rows", "tiles"))),
        check_vma=False,
    )
```

time: 753 us -> 130 us (0.17)
  blocking collectives: 313 us -> 0 us
  local copies, waits for them, and re-layouts: 138 us -> 5.25 us
  waiting for transfers between devices: 144 us -> 46.5 us
  matrix products: 80.3 us -> 0.18 us
  Pallas kernels: 0 us -> 24.3 us
  loops' own time: 18.7 us -> 0 us
  starting transfers between devices: 27.8 us -> 46.1 us
  between operations: 14.5 us -> 1.56 us
    psum x7 -> x0, blocking collectives: 282 us -> none  [the longest x2 81.5 us: local(): lax.psum((jnp.sum(start_block * start_block, axis=1), jnp.sum(start_step...]
    gather x48 -> x0, local copies, waits for them, and re-layouts: 130 us -> none  [the longest x24 74.4 us: add_slot(): partner = jnp.take(unit_ext, col_index, axis=0)]
    dot_general x56 -> x1, matrix products: 80.3 us -> 0.18 us  [tile_list(): place = jnp.dot(mask, before).astype(jnp.int32)]
    psum x2 -> x0, waiting for transfers between devices: 70.1 us -> none  [local(): lax.psum(lax.fori_loop(0, trip_count, add_slot, start_sum).reshape(K, blo...]
    all_gather x2 -> x0, blocking collectives: 31.7 us -> none  [the longest x1 15.9 us: local(): lax.all_gather(step_share, 'tiles', axis=1, tiled=True)]
    ppermute x12 -> x41, waiting for transfers between devices: 73.8 us -> 46.5 us  [the longest x26 36.1 us: swapped(): return lax.ppermute(value, axis, [(i, i ^ bits) for i in range(count)])]
    pallas_call x0 -> x6, Pallas kernels: none -> 24.3 us  [call(): pl.pallas_call(kernel, out_shape=tuple((jax.ShapeDtypeStruct(shape, dtype...]
    another operation x2 -> x0, loops' own time: 18.7 us -> none  [local(): lax.fori_loop(0, trip_count, add_slot, start_sum)]
  transfers between devices with their start and end apart: 14 -> 41, of which waited for: 7 -> 16; matrix products, arithmetic and copies ran while one was open for 1% -> 5% of each run, Pallas kernels for 0% -> 5%
where the time goes in v1:
time: 130 us; the launch traced here: 129 us
  waiting for transfers between devices  46.5 us (36%)
  starting transfers between devices  46.1 us (35%)
  Pallas kernels  24.3 us (19%)
  other arithmetic  5.41 us (4%)
  local copies, waits for them, and re-layouts  5.25 us (4%)
  between operations  1.56 us (1%)
    ppermute x26, waiting for transfers between devices, swapped(): return lax.ppermute(value, axis, [(i, i ^ bits) for i in range(count)])  36.1 us
    ppermute x26, starting transfers between devices, swapped(): return lax.ppermute(value, axis, [(i, i ^ bits) for i in range(count)])  24.6 us
    pallas_call x6, Pallas kernels, call(): pl.pallas_call(kernel, out_shape=tuple((jax.ShapeDtypeStruct(shape, dtype...  24.3 us
    ppermute x12, starting transfers between devices, rotated(): lax.ppermute(value, axis, [(i, (i + steps) % count) for i in range(count)])  19 us
    ppermute x12, waiting for transfers between devices, rotated(): lax.ppermute(value, axis, [(i, (i + steps) % count) for i in range(count)])  7.03 us
    ppermute x3, waiting for transfers between devices, other_side(): return lax.ppermute(value, 'rows', pairs)  3.43 us
    unnamed x12, local copies, waits for them, and re-layouts  3.22 us
  transfers between devices with their start and end apart: 41, of which 16 were waited for; matrix products, arithmetic and copies ran while one was open for 5% of the time, Pallas kernels for 5%

profile of v1, /device:TPU:0, one launch (start us, length us, event | category | flops | bytes accessed | tf_op | source)
XLA Modules:
  0.0 129.3 jit_solution(3446512043495094311)
XLA Ops:
  0.7 3.1 %collective-permute-start = (s32[16,12]{1,0:T(8,128)}, s32[16,12]{1,0:T(8,128)S(1)}, u32[]{:S(2)}, u32[]{:S(2)}) collective-permute-start(s32[16,12]{1,0:T(8,128)} %param.10), channel_id=1, source_target_pairs={{0,1},{1,2},{2,3},{3,0},{4,5},{5,6},{6,7},{7,4},{8,9},{9,10},{10,1... | collective-permute-start | bytes 2312 | tf_op jit(solution)/shard_map/ppermute | solution.py:44
  3.7 2.6 %collective-permute-start.1 = (s32[16,12]{1,0:T(8,128)}, s32[16,12]{1,0:T(8,128)S(1)}, u32[]{:S(2)}, u32[]{:S(2)}) collective-permute-start(s32[16,12]{1,0:T(8,128)} %param.10), channel_id=1, source_target_pairs={{0,2},{1,3},{2,0},{3,1},{4,6},{5,7},{6,4},{7,5},{8,10},{9,11},{10,... | collective-permute-start | bytes 2312 | tf_op jit(solution)/shard_map/ppermute | solution.py:44
  8.6 1.6 %collective-permute-start.4 = (bf16[512,256]{1,0:T(8,128)(2,1)S(1)}, bf16[512,256]{1,0:T(8,128)(2,1)S(1)}, u32[]{:S(2)}, u32[]{:S(2)}) collective-permute-start(bf16[512,256]{1,0:T(8,128)(2,1)S(1)} %constant_dynamic-slice_fusion), channel_id=1, source_target_pairs={{0,8},{4,12},{8,0},{12,4},{16,24},{20,28},{24,16},{28,20},{1,9},{5... | collective-permute-start | bytes 786440 | tf_op jit(solution)/shard_map/ppermute | solution.py:39
  10.2 1.5 %collective-permute-start.6 = (bf16[512,256]{1,0:T(8,128)(2,1)S(1)}, bf16[512,256]{1,0:T(8,128)(2,1)S(1)}, u32[]{:S(2)}, u32[]{:S(2)}) collective-permute-start(bf16[512,256]{1,0:T(8,128)(2,1)S(1)} %constant_dynamic-slice_fusion), channel_id=1, source_target_pairs={{0,24},{4,28},{8,16},{12,20},{16,8},{20,12},{24,0},{28,4},{1,25},{... | collective-permute-start | bytes 786440 | tf_op jit(solution)/shard_map/ppermute | solution.py:55
  13.7 1.5 %collective-permute-start.9 = (bf16[128,512]{1,0:T(8,128)(2,1)S(1)}, bf16[128,512]{1,0:T(8,128)(2,1)S(1)}, u32[]{:S(2)}, u32[]{:S(2)}) collective-permute-start(bf16[128,512]{1,0:T(8,128)(2,1)S(1)} %pad_maximum_fusion.refs_8_), channel_id=1, source_target_pairs={{0,8},{4,12},{8,0},{12,4},{16,24},{20,28},{24,16},{28,20},{1,9},{5... | collective-permute-start | bytes 393224 | tf_op jit(solution)/shard_map/ppermute | solution.py:39
  17.4 8.4 %collective-permute-done.9.refs_10_ = bf16[128,512]{1,0:T(8,128)(2,1)S(1)} collective-permute-done((bf16[128,512]{1,0:T(8,128)(2,1)S(1)}, bf16[128,512]{1,0:T(8,128)(2,1)S(1)}, u32[]{:S(2)}, u32[]{:S(2)}) %collective-permute-start.9) | collective-permute-done | bytes 131104 | tf_op jit(solution)/shard_map/ppermute | solution.py:39
  26.5 1.6 %collective-permute-done.11.refs_12_ = bf16[128,512]{1,0:T(8,128)(2,1)S(1)} collective-permute-done((bf16[128,512]{1,0:T(8,128)(2,1)S(1)}, bf16[128,512]{1,0:T(8,128)(2,1)S(1)}, u32[]{:S(2)}, u32[]{:S(2)}) %collective-permute-start.11) | collective-permute-done | bytes 131104 | tf_op jit(solution)/shard_map/ppermute | solution.py:55
  31.2 10.9 %shard_map.77 = (f32[128,512]{1,0:T(8,128)S(1)}, bf16[64,512]{1,0:T(8,128)(2,1)S(1)}, bf16[64,512]{1,0:T(8,128)(2,1)S(1)}, bf16[64,512]{1,0:T(8,128)(2,1)S(1)}, ...) custom-call(s32[2]{0:T(128)S(1)} %pad_add_fusion.1.refs_0_, ...), custom_call_target="tpu_custom_call" | custom-call | tf_op jit(solution)/shard_map/pallas_call | solution.py:277
  42.3 3.6 %collective-permute-start.15 = (bf16[64,512]{1,0:T(8,128)(2,1)S(1)}, bf16[64,512]{1,0:T(8,128)(2,1)S(1)}, u32[]{:S(2)}, u32[]{:S(2)}) collective-permute-start(bf16[64,512]{1,0:T(8,128)(2,1)S(1)} %get-tuple-element.25), channel_id=1, source_target_pairs={{0,3},{1,0},{2,1},{3,2},{4,7},{5,4},{6,5},{7,6},{8,11},{9,8},{10,9... | collective-permute-start | bytes 196616 | tf_op jit(solution)/shard_map/ppermute | solution.py:44
  46.5 1.5 %collective-permute-start.24 = (bf16[64,512]{1,0:T(8,128)(2,1)S(1)}, bf16[64,512]{1,0:T(8,128)(2,1)S(1)}, u32[]{:S(2)}, u32[]{:S(2)}) collective-permute-start(bf16[64,512]{1,0:T(8,128)(2,1)S(1)} %get-tuple-element.28), channel_id=1, source_target_pairs={{0,2},{1,3},{2,0},{3,1},{4,6},{5,7},{6,4},{7,5},{8,10},{9,11},{10,... | collective-permute-start | bytes 196616 | tf_op jit(solution)/shard_map/ppermute | solution.py:44
  48.9 2.0 %collective-permute-start.25 = (bf16[64,512]{1,0:T(8,128)(2,1)S(1)}, bf16[64,512]{1,0:T(8,128)(2,1)S(1)}, u32[]{:S(2)}, u32[]{:S(2)}) collective-permute-start(bf16[64,512]{1,0:T(8,128)(2,1)S(1)} %get-tuple-element.29), channel_id=1, source_target_pairs={{0,3},{1,0},{2,1},{3,2},{4,7},{5,4},{6,5},{7,6},{8,11},{9,8},{10,9... | collective-permute-start | bytes 196616 | tf_op jit(solution)/shard_map/ppermute | solution.py:44
  50.9 2.2 %collective-permute-done.23 = bf16[64,512]{1,0:T(8,128)(2,1)S(1)} collective-permute-done((bf16[64,512]{1,0:T(8,128)(2,1)S(1)}, bf16[64,512]{1,0:T(8,128)(2,1)S(1)}, u32[]{:S(2)}, u32[]{:S(2)}) %collective-permute-start.23) | collective-permute-done | bytes 65568 | tf_op jit(solution)/shard_map/ppermute | solution.py:44
  53.2 3.2 %collective-permute-done.24 = bf16[64,512]{1,0:T(8,128)(2,1)S(1)} collective-permute-done((bf16[64,512]{1,0:T(8,128)(2,1)S(1)}, bf16[64,512]{1,0:T(8,128)(2,1)S(1)}, u32[]{:S(2)}, u32[]{:S(2)}) %collective-permute-start.24) | collective-permute-done | bytes 65568 | tf_op jit(solution)/shard_map/ppermute | solution.py:44
  60.1 1.7 %collective-permute-start.27 = (bf16[64,512]{1,0:T(8,128)(2,1)S(1)}, bf16[64,512]{1,0:T(8,128)(2,1)S(1)}, u32[]{:S(2)}, u32[]{:S(2)}) collective-permute-start(bf16[64,512]{1,0:T(8,128)(2,1)S(1)} %get-tuple-element.42.refs_3_), channel_id=1, source_target_pairs={{0,8},{4,12},{8,0},{12,4},{16,24},{20,28},{24,16},{28,20},{1,9},{5... | collective-permute-start | bytes 196616 | tf_op jit(solution)/shard_map/ppermute | solution.py:39
  62.2 2.8 %collective-permute-done.27.refs_5_ = bf16[64,512]{1,0:T(8,128)(2,1)S(1)} collective-permute-done((bf16[64,512]{1,0:T(8,128)(2,1)S(1)}, bf16[64,512]{1,0:T(8,128)(2,1)S(1)}, u32[]{:S(2)}, u32[]{:S(2)}) %collective-permute-start.27) | collective-permute-done | bytes 65568 | tf_op jit(solution)/shard_map/ppermute | solution.py:39
  65.0 1.9 %collective-permute-done.29.refs_7_ = bf16[64,512]{1,0:T(8,128)(2,1)S(1)} collective-permute-done((bf16[64,512]{1,0:T(8,128)(2,1)S(1)}, bf16[64,512]{1,0:T(8,128)(2,1)S(1)}, u32[]{:S(2)}, u32[]{:S(2)}) %collective-permute-start.29) | collective-permute-done | bytes 65568 | tf_op jit(solution)/shard_map/ppermute | solution.py:55
  67.4 1.7 %collective-permute-start.18 = (f32[6,64,64]{2,1,0:T(8,128)S(1)}, f32[6,64,64]{2,1,0:T(8,128)S(1)}, u32[]{:S(2)}, u32[]{:S(2)}) collective-permute-start(f32[6,64,64]{2,1,0:T(8,128)S(1)} %add.225), channel_id=1, source_target_pairs={{0,16},{4,20},{8,24},{12,28},{16,0},{20,4},{24,8},{28,12},{1,17},{... | collective-permute-start | bytes 294920 | tf_op jit(solution)/shard_map/ppermute | solution.py:39
  71.5 6.2 %shard_map.80 = (f32[64,512]{1,0:T(8,128)S(1)}, bf16[64,512]{1,0:T(8,128)(2,1)S(1)}, bf16[64,512]{1,0:T(8,128)(2,1)S(1)}, bf16[64,512]{1,0:T(8,128)(2,1)S(1)}) custom-call(s32[2]{0:T(128)S(1)} %pad_add_fusion.1.refs_0_, s32[392]{0:T(512)S(1)} %concatenate.44.refs_1_, bf16[396,128,128]{2,1,0:T(8,128)(2,1)} %get-tuple-element.35.refs_2_, ...), custom_call_target="tpu_custom_call" | custom-call | tf_op jit(solution)/shard_map/pallas_call | solution.py:277
  77.7 1.7 %collective-permute-start.31 = (bf16[64,512]{1,0:T(8,128)(2,1)S(1)}, bf16[64,512]{1,0:T(8,128)(2,1)S(1)}, u32[]{:S(2)}, u32[]{:S(2)}) collective-permute-start(bf16[64,512]{1,0:T(8,128)(2,1)S(1)} %get-tuple-element.37), channel_id=1, source_target_pairs={{0,1},{1,2},{2,3},{3,0},{4,5},{5,6},{6,7},{7,4},{8,9},{9,10},{10,1... | collective-permute-start | bytes 196616 | tf_op jit(solution)/shard_map/ppermute | solution.py:44
  82.6 1.9 %collective-permute-start.21 = (f32[6,64,64]{2,1,0:T(8,128)S(1)}, f32[6,64,64]{2,1,0:T(8,128)S(1)}, u32[]{:S(2)}, u32[]{:S(2)}) collective-permute-start(f32[6,64,64]{2,1,0:T(8,128)S(1)} %add_add_fusion.1), channel_id=1, source_target_pairs={{0,2},{1,3},{2,0},{3,1},{4,6},{5,7},{6,4},{7,5},{8,10},{9,11},{10,... | collective-permute-start | bytes 294920 | tf_op jit(solution)/shard_map/ppermute | solution.py:39
  84.6 1.8 %collective-permute-start.22 = (f32[6,64,64]{2,1,0:T(8,128)S(1)}, f32[6,64,64]{2,1,0:T(8,128)S(1)}, u32[]{:S(2)}, u32[]{:S(2)}) collective-permute-start(f32[6,64,64]{2,1,0:T(8,128)S(1)} %add_add_fusion.1), channel_id=1, source_target_pairs={{0,3},{1,2},{2,1},{3,0},{4,7},{5,6},{6,5},{7,4},{8,11},{9,10},{10,... | collective-permute-start | bytes 294920 | tf_op jit(solution)/shard_map/ppermute | solution.py:39
  87.0 6.3 %collective-permute-done.20 = f32[6,64,64]{2,1,0:T(8,128)S(1)} collective-permute-done((f32[6,64,64]{2,1,0:T(8,128)S(1)}, f32[6,64,64]{2,1,0:T(8,128)S(1)}, u32[]{:S(2)}, u32[]{:S(2)}) %collective-permute-start.20) | collective-permute-done | bytes 98336 | tf_op jit(solution)/shard_map/ppermute | solution.py:39
  93.3 7.1 %collective-permute-done.21 = f32[6,64,64]{2,1,0:T(8,128)S(1)} collective-permute-done((f32[6,64,64]{2,1,0:T(8,128)S(1)}, f32[6,64,64]{2,1,0:T(8,128)S(1)}, u32[]{:S(2)}, u32[]{:S(2)}) %collective-permute-start.21) | collective-permute-done | bytes 98336 | tf_op jit(solution)/shard_map/ppermute | solution.py:39
  100.5 2.8 %shard_map.79 = (f32[64,512]{1,0:T(8,128)S(1)}, f32[64,512]{1,0:T(8,128)S(1)}, f32[64,512]{1,0:T(8,128)S(1)}, f32[64,64]{1,0:T(8,128)S(1)}, f32[3,64,64]{2,1,0:T(8,128)S(1)}) custom-call(f32[6,64,64]{2,1,0:T(8,128)S(1)} %add_add_fusion.g_ref, f32[192,64]{1,0:T(8,128)S(1)} %bitcast.8, f32[64,512]{1,0:T(8,128)S(1)} %copy-done.1, f32[64,512]{1,0:T(8,128)S(1)} %copy-done.3, ...), custom_call_target="tpu_custom_call" | custom-call | tf_op jit(solution)/shard_map/pallas_call | solution.py:277
  105.9 1.5 %collective-permute-start.36 = (f32[3,64,64]{2,1,0:T(8,128)S(1)}, f32[3,64,64]{2,1,0:T(8,128)S(1)}, u32[]{:S(2)}, u32[]{:S(2)}) collective-permute-start(f32[3,64,64]{2,1,0:T(8,128)S(1)} %add.240), channel_id=1, source_target_pairs={{0,16},{4,20},{8,24},{12,28},{16,0},{20,4},{24,8},{28,12},{1,17},{... | collective-permute-start | bytes 147464 | tf_op jit(solution)/shard_map/ppermute | solution.py:39
  107.4 1.6 %collective-permute-start.37 = (f32[3,64,64]{2,1,0:T(8,128)S(1)}, f32[3,64,64]{2,1,0:T(8,128)S(1)}, u32[]{:S(2)}, u32[]{:S(2)}) collective-permute-start(f32[3,64,64]{2,1,0:T(8,128)S(1)} %add.240), channel_id=1, source_target_pairs={{0,24},{4,28},{8,16},{12,20},{16,8},{20,12},{24,0},{28,4},{1,25},{... | collective-permute-start | bytes 147464 | tf_op jit(solution)/shard_map/ppermute | solution.py:39
  108.9 2.1 %collective-permute-done.35 = f32[3,64,64]{2,1,0:T(8,128)S(1)} collective-permute-done((f32[3,64,64]{2,1,0:T(8,128)S(1)}, f32[3,64,64]{2,1,0:T(8,128)S(1)}, u32[]{:S(2)}, u32[]{:S(2)}) %collective-permute-start.35) | collective-permute-done | bytes 49184 | tf_op jit(solution)/shard_map/ppermute | solution.py:39
  111.1 1.8 %collective-permute-done.37 = f32[3,64,64]{2,1,0:T(8,128)S(1)} collective-permute-done((f32[3,64,64]{2,1,0:T(8,128)S(1)}, f32[3,64,64]{2,1,0:T(8,128)S(1)}, u32[]{:S(2)}, u32[]{:S(2)}) %collective-permute-start.37) | collective-permute-done | bytes 49184 | tf_op jit(solution)/shard_map/ppermute | solution.py:39
  112.9 4.8 %collective-permute-start.38 = (f32[3,64,64]{2,1,0:T(8,128)S(1)}, f32[3,64,64]{2,1,0:T(8,128)S(1)}, u32[]{:S(2)}, u32[]{:S(2)}) collective-permute-start(f32[3,64,64]{2,1,0:T(8,128)S(1)} %add_add_fusion.3), channel_id=1, source_target_pairs={{0,1},{1,0},{2,3},{3,2},{4,5},{5,4},{6,7},{7,6},{8,9},{9,8},{10,11... | collective-permute-start | bytes 147464 | tf_op jit(solution)/shard_map/ppermute | solution.py:39
  117.7 2.4 %collective-permute-start.40 = (f32[3,64,64]{2,1,0:T(8,128)S(1)}, f32[3,64,64]{2,1,0:T(8,128)S(1)}, u32[]{:S(2)}, u32[]{:S(2)}) collective-permute-start(f32[3,64,64]{2,1,0:T(8,128)S(1)} %add_add_fusion.3), channel_id=1, source_target_pairs={{0,3},{1,2},{2,1},{3,0},{4,7},{5,6},{6,5},{7,4},{8,11},{9,10},{10,... | collective-permute-start | bytes 147464 | tf_op jit(solution)/shard_map/ppermute | solution.py:39
  120.5 5.9 %collective-permute-done.39 = f32[3,64,64]{2,1,0:T(8,128)S(1)} collective-permute-done((f32[3,64,64]{2,1,0:T(8,128)S(1)}, f32[3,64,64]{2,1,0:T(8,128)S(1)}, u32[]{:S(2)}, u32[]{:S(2)}) %collective-permute-start.39) | collective-permute-done | bytes 49184 | tf_op jit(solution)/shard_map/ppermute | solution.py:39
  126.5 2.8 %shard_map.82 = (f32[64,512]{1,0:T(8,128)}, f32[64,512]{1,0:T(8,128)}) custom-call(f32[3,64,64]{2,1,0:T(8,128)S(1)} %get-tuple-element.30.g_ref, f32[3,64,64]{2,1,0:T(8,128)S(1)} %add_add_fusion.2.h_ref, f32[192,64]{1,0:T(8,128)S(1)} %bitcast.9, f32[64,512]{1,0:T(8,128)S(1)} %get-tuple-element.31.v_ref, f32[64,512]{1,0:T(8,128)S(1)} %get-tuple-element.32.s_ref, ...), custom_call_target="tpu_custom_call" | custom-call | tf_op jit(solution)/shard_map/pallas_call | solution.py:277
  (97 shorter events, 25.4 us)
Async XLA Ops:
  0.7 13.0 %collective-permute-start = (s32[16,12]{1,0:T(8,128)}, s32[16,12]{1,0:T(8,128)S(1)}, u32[]{:S(2)}, u32[]{:S(2)}) collective-permute-start(s32[16,12]{1,0:T(8,128)} %param.10), channel_id=1, source_target_pairs={{0,1},{1,2},{2,3},{3,0},{4,5},{5,6},{6,7},{7,4},{8,9},{9,10},{10,1... | collective-permute-start | bytes 2312 | tf_op jit(solution)/shard_map/ppermute | solution.py:44
  3.7 11.5 %collective-permute-start.1 = (s32[16,12]{1,0:T(8,128)}, s32[16,12]{1,0:T(8,128)S(1)}, u32[]{:S(2)}, u32[]{:S(2)}) collective-permute-start(s32[16,12]{1,0:T(8,128)} %param.10), channel_id=1, source_target_pairs={{0,2},{1,3},{2,0},{3,1},{4,6},{5,7},{6,4},{7,5},{8,10},{9,11},{10,... | collective-permute-start | bytes 2312 | tf_op jit(solution)/shard_map/ppermute | solution.py:44
  6.3 9.3 %collective-permute-start.2 = (s32[16,12]{1,0:T(8,128)}, s32[16,12]{1,0:T(8,128)S(1)}, u32[]{:S(2)}, u32[]{:S(2)}) collective-permute-start(s32[16,12]{1,0:T(8,128)} %param.10), channel_id=1, source_target_pairs={{0,3},{1,0},{2,1},{3,2},{4,7},{5,4},{6,5},{7,6},{8,11},{9,8},{10,9... | collective-permute-start | bytes 2312 | tf_op jit(solution)/shard_map/ppermute | solution.py:44
  8.6 17.1 %collective-permute-start.4 = (bf16[512,256]{1,0:T(8,128)(2,1)S(1)}, bf16[512,256]{1,0:T(8,128)(2,1)S(1)}, u32[]{:S(2)}, u32[]{:S(2)}) collective-permute-start(bf16[512,256]{1,0:T(8,128)(2,1)S(1)} %constant_dynamic-slice_fusion), channel_id=1, source_target_pairs={{0,8},{4,12},{8,0},{12,4},{16,24},{20,28},{24,16},{28,20},{1,9},{5... | collective-permute-start | bytes 786440 | tf_op jit(solution)/shard_map/ppermute | solution.py:39
  10.2 16.1 %collective-permute-start.6 = (bf16[512,256]{1,0:T(8,128)(2,1)S(1)}, bf16[512,256]{1,0:T(8,128)(2,1)S(1)}, u32[]{:S(2)}, u32[]{:S(2)}) collective-permute-start(bf16[512,256]{1,0:T(8,128)(2,1)S(1)} %constant_dynamic-slice_fusion), channel_id=1, source_target_pairs={{0,24},{4,28},{8,16},{12,20},{16,8},{20,12},{24,0},{28,4},{1,25},{... | collective-permute-start | bytes 786440 | tf_op jit(solution)/shard_map/ppermute | solution.py:55
  13.7 12.1 %collective-permute-start.9 = (bf16[128,512]{1,0:T(8,128)(2,1)S(1)}, bf16[128,512]{1,0:T(8,128)(2,1)S(1)}, u32[]{:S(2)}, u32[]{:S(2)}) collective-permute-start(bf16[128,512]{1,0:T(8,128)(2,1)S(1)} %pad_maximum_fusion.refs_8_), channel_id=1, source_target_pairs={{0,8},{4,12},{8,0},{12,4},{16,24},{20,28},{24,16},{28,20},{1,9},{5... | collective-permute-start | bytes 393224 | tf_op jit(solution)/shard_map/ppermute | solution.py:39
  15.2 12.9 %collective-permute-start.11 = (bf16[128,512]{1,0:T(8,128)(2,1)S(1)}, bf16[128,512]{1,0:T(8,128)(2,1)S(1)}, u32[]{:S(2)}, u32[]{:S(2)}) collective-permute-start(bf16[128,512]{1,0:T(8,128)(2,1)S(1)} %pad_maximum_fusion.refs_8_), channel_id=1, source_target_pairs={{0,24},{4,28},{8,16},{12,20},{16,8},{20,12},{24,0},{28,4},{1,25},{... | collective-permute-start | bytes 393224 | tf_op jit(solution)/shard_map/ppermute | solution.py:55
  15.7 12.4 %collective-permute-start.8 = (bf16[128,512]{1,0:T(8,128)(2,1)S(1)}, bf16[128,512]{1,0:T(8,128)(2,1)S(1)}, u32[]{:S(2)}, u32[]{:S(2)}) collective-permute-start(bf16[128,512]{1,0:T(8,128)(2,1)S(1)} %pad_maximum_fusion.refs_8_), channel_id=1, source_target_pairs={{0,4},{4,0},{8,12},{12,8},{16,20},{20,16},{24,28},{28,24},{1,5},{5... | collective-permute-start | bytes 393224 | tf_op jit(solution)/shard_map/ppermute | solution.py:39
  42.1 6.8 %collective-permute-start.13 = (bf16[64,512]{1,0:T(8,128)(2,1)S(1)}, bf16[64,512]{1,0:T(8,128)(2,1)S(1)}, u32[]{:S(2)}, u32[]{:S(2)}) collective-permute-start(bf16[64,512]{1,0:T(8,128)(2,1)S(1)} %get-tuple-element.23), channel_id=1, source_target_pairs={{0,1},{1,2},{2,3},{3,0},{4,5},{5,6},{6,7},{7,4},{8,9},{9,10},{10,1... | collective-permute-start | bytes 196616 | tf_op jit(solution)/shard_map/ppermute | solution.py:44
  42.3 8.6 %collective-permute-start.14 = (bf16[64,512]{1,0:T(8,128)(2,1)S(1)}, bf16[64,512]{1,0:T(8,128)(2,1)S(1)}, u32[]{:S(2)}, u32[]{:S(2)}) collective-permute-start(bf16[64,512]{1,0:T(8,128)(2,1)S(1)} %get-tuple-element.24), channel_id=1, source_target_pairs={{0,2},{1,3},{2,0},{3,1},{4,6},{5,7},{6,4},{7,5},{8,10},{9,11},{10,... | collective-permute-start | bytes 196616 | tf_op jit(solution)/shard_map/ppermute | solution.py:44
  42.3 8.6 %collective-permute-start.15 = (bf16[64,512]{1,0:T(8,128)(2,1)S(1)}, bf16[64,512]{1,0:T(8,128)(2,1)S(1)}, u32[]{:S(2)}, u32[]{:S(2)}) collective-permute-start(bf16[64,512]{1,0:T(8,128)(2,1)S(1)} %get-tuple-element.25), channel_id=1, source_target_pairs={{0,3},{1,0},{2,1},{3,2},{4,7},{5,4},{6,5},{7,6},{8,11},{9,8},{10,9... | collective-permute-start | bytes 196616 | tf_op jit(solution)/shard_map/ppermute | solution.py:44
  45.9 7.2 %collective-permute-start.23 = (bf16[64,512]{1,0:T(8,128)(2,1)S(1)}, bf16[64,512]{1,0:T(8,128)(2,1)S(1)}, u32[]{:S(2)}, u32[]{:S(2)}) collective-permute-start(bf16[64,512]{1,0:T(8,128)(2,1)S(1)} %get-tuple-element.27), channel_id=1, source_target_pairs={{0,1},{1,2},{2,3},{3,0},{4,5},{5,6},{6,7},{7,4},{8,9},{9,10},{10,1... | collective-permute-start | bytes 196616 | tf_op jit(solution)/shard_map/ppermute | solution.py:44
  46.5 9.8 %collective-permute-start.24 = (bf16[64,512]{1,0:T(8,128)(2,1)S(1)}, bf16[64,512]{1,0:T(8,128)(2,1)S(1)}, u32[]{:S(2)}, u32[]{:S(2)}) collective-permute-start(bf16[64,512]{1,0:T(8,128)(2,1)S(1)} %get-tuple-element.28), channel_id=1, source_target_pairs={{0,2},{1,3},{2,0},{3,1},{4,6},{5,7},{6,4},{7,5},{8,10},{9,11},{10,... | collective-permute-start | bytes 196616 | tf_op jit(solution)/shard_map/ppermute | solution.py:44
  48.9 7.4 %collective-permute-start.25 = (bf16[64,512]{1,0:T(8,128)(2,1)S(1)}, bf16[64,512]{1,0:T(8,128)(2,1)S(1)}, u32[]{:S(2)}, u32[]{:S(2)}) collective-permute-start(bf16[64,512]{1,0:T(8,128)(2,1)S(1)} %get-tuple-element.29), channel_id=1, source_target_pairs={{0,3},{1,0},{2,1},{3,2},{4,7},{5,4},{6,5},{7,6},{8,11},{9,8},{10,9... | collective-permute-start | bytes 196616 | tf_op jit(solution)/shard_map/ppermute | solution.py:44
  60.0 6.9 %collective-permute-start.16 = (f32[6,64,64]{2,1,0:T(8,128)S(1)}, f32[6,64,64]{2,1,0:T(8,128)S(1)}, u32[]{:S(2)}, u32[]{:S(2)}) collective-permute-start(f32[6,64,64]{2,1,0:T(8,128)S(1)} %shard_map.78), channel_id=1, source_target_pairs={{0,4},{4,0},{8,12},{12,8},{16,20},{20,16},{24,28},{28,24},{1,5},{5... | collective-permute-start | bytes 294920 | tf_op jit(solution)/shard_map/ppermute | solution.py:39
  62.2 6.9 %collective-permute-start.26 = (bf16[64,512]{1,0:T(8,128)(2,1)S(1)}, bf16[64,512]{1,0:T(8,128)(2,1)S(1)}, u32[]{:S(2)}, u32[]{:S(2)}) collective-permute-start(bf16[64,512]{1,0:T(8,128)(2,1)S(1)} %get-tuple-element.42.refs_3_), channel_id=1, source_target_pairs={{0,4},{4,0},{8,12},{12,8},{16,20},{20,16},{24,28},{28,24},{1,5},{5... | collective-permute-start | bytes 196616 | tf_op jit(solution)/shard_map/ppermute | solution.py:39
  65.0 6.4 %collective-permute-start.28 = (bf16[64,512]{1,0:T(8,128)(2,1)S(1)}, bf16[64,512]{1,0:T(8,128)(2,1)S(1)}, u32[]{:S(2)}, u32[]{:S(2)}) collective-permute-start(bf16[64,512]{1,0:T(8,128)(2,1)S(1)} %collective-permute-done.27.refs_5_), channel_id=1, source_target_pairs={{0,4},{4,0},{8,12},{12,8},{16,20},{20,16},{24,28},{28,24},{1,5},{5... | collective-permute-start | bytes 196616 | tf_op jit(solution)/shard_map/ppermute | solution.py:39
  66.9 13.5 %collective-permute-start.17 = (f32[6,64,64]{2,1,0:T(8,128)S(1)}, f32[6,64,64]{2,1,0:T(8,128)S(1)}, u32[]{:S(2)}, u32[]{:S(2)}) collective-permute-start(f32[6,64,64]{2,1,0:T(8,128)S(1)} %add.225), channel_id=1, source_target_pairs={{0,8},{4,12},{8,0},{12,4},{16,24},{20,28},{24,16},{28,20},{1,9},{5... | collective-permute-start | bytes 294920 | tf_op jit(solution)/shard_map/ppermute | solution.py:39
  67.4 14.5 %collective-permute-start.18 = (f32[6,64,64]{2,1,0:T(8,128)S(1)}, f32[6,64,64]{2,1,0:T(8,128)S(1)}, u32[]{:S(2)}, u32[]{:S(2)}) collective-permute-start(f32[6,64,64]{2,1,0:T(8,128)S(1)} %add.225), channel_id=1, source_target_pairs={{0,16},{4,20},{8,24},{12,28},{16,0},{20,4},{24,8},{28,12},{1,17},{... | collective-permute-start | bytes 294920 | tf_op jit(solution)/shard_map/ppermute | solution.py:39
  69.1 12.8 %collective-permute-start.19 = (f32[6,64,64]{2,1,0:T(8,128)S(1)}, f32[6,64,64]{2,1,0:T(8,128)S(1)}, u32[]{:S(2)}, u32[]{:S(2)}) collective-permute-start(f32[6,64,64]{2,1,0:T(8,128)S(1)} %add.225), channel_id=1, source_target_pairs={{0,24},{4,28},{8,16},{12,20},{16,8},{20,12},{24,0},{28,4},{1,25},{... | collective-permute-start | bytes 294920 | tf_op jit(solution)/shard_map/ppermute | solution.py:39
  77.7 6.9 %collective-permute-start.31 = (bf16[64,512]{1,0:T(8,128)(2,1)S(1)}, bf16[64,512]{1,0:T(8,128)(2,1)S(1)}, u32[]{:S(2)}, u32[]{:S(2)}) collective-permute-start(bf16[64,512]{1,0:T(8,128)(2,1)S(1)} %get-tuple-element.37), channel_id=1, source_target_pairs={{0,1},{1,2},{2,3},{3,0},{4,5},{5,6},{6,7},{7,4},{8,9},{9,10},{10,1... | collective-permute-start | bytes 196616 | tf_op jit(solution)/shard_map/ppermute | solution.py:44
  79.4 7.0 %collective-permute-start.32 = (bf16[64,512]{1,0:T(8,128)(2,1)S(1)}, bf16[64,512]{1,0:T(8,128)(2,1)S(1)}, u32[]{:S(2)}, u32[]{:S(2)}) collective-permute-start(bf16[64,512]{1,0:T(8,128)(2,1)S(1)} %get-tuple-element.38), channel_id=1, source_target_pairs={{0,2},{1,3},{2,0},{3,1},{4,6},{5,7},{6,4},{7,5},{8,10},{9,11},{10,... | collective-permute-start | bytes 196616 | tf_op jit(solution)/shard_map/ppermute | solution.py:44
  80.5 6.5 %collective-permute-start.33 = (bf16[64,512]{1,0:T(8,128)(2,1)S(1)}, bf16[64,512]{1,0:T(8,128)(2,1)S(1)}, u32[]{:S(2)}, u32[]{:S(2)}) collective-permute-start(bf16[64,512]{1,0:T(8,128)(2,1)S(1)} %get-tuple-element.39), channel_id=1, source_target_pairs={{0,3},{1,0},{2,1},{3,2},{4,7},{5,4},{6,5},{7,6},{8,11},{9,8},{10,9... | collective-permute-start | bytes 196616 | tf_op jit(solution)/shard_map/ppermute | solution.py:44
  81.9 11.4 %collective-permute-start.20 = (f32[6,64,64]{2,1,0:T(8,128)S(1)}, f32[6,64,64]{2,1,0:T(8,128)S(1)}, u32[]{:S(2)}, u32[]{:S(2)}) collective-permute-start(f32[6,64,64]{2,1,0:T(8,128)S(1)} %add_add_fusion.1), channel_id=1, source_target_pairs={{0,1},{1,0},{2,3},{3,2},{4,5},{5,4},{6,7},{7,6},{8,9},{9,8},{10,11... | collective-permute-start | bytes 294920 | tf_op jit(solution)/shard_map/ppermute | solution.py:39
  82.6 17.8 %collective-permute-start.21 = (f32[6,64,64]{2,1,0:T(8,128)S(1)}, f32[6,64,64]{2,1,0:T(8,128)S(1)}, u32[]{:S(2)}, u32[]{:S(2)}) collective-permute-start(f32[6,64,64]{2,1,0:T(8,128)S(1)} %add_add_fusion.1), channel_id=1, source_target_pairs={{0,2},{1,3},{2,0},{3,1},{4,6},{5,7},{6,4},{7,5},{8,10},{9,11},{10,... | collective-permute-start | bytes 294920 | tf_op jit(solution)/shard_map/ppermute | solution.py:39
  84.6 15.8 %collective-permute-start.22 = (f32[6,64,64]{2,1,0:T(8,128)S(1)}, f32[6,64,64]{2,1,0:T(8,128)S(1)}, u32[]{:S(2)}, u32[]{:S(2)}) collective-permute-start(f32[6,64,64]{2,1,0:T(8,128)S(1)} %add_add_fusion.1), channel_id=1, source_target_pairs={{0,3},{1,2},{2,1},{3,0},{4,7},{5,6},{6,5},{7,4},{8,11},{9,10},{10,... | collective-permute-start | bytes 294920 | tf_op jit(solution)/shard_map/ppermute | solution.py:39
  105.4 5.7 %collective-permute-start.35 = (f32[3,64,64]{2,1,0:T(8,128)S(1)}, f32[3,64,64]{2,1,0:T(8,128)S(1)}, u32[]{:S(2)}, u32[]{:S(2)}) collective-permute-start(f32[3,64,64]{2,1,0:T(8,128)S(1)} %add.240), channel_id=1, source_target_pairs={{0,8},{4,12},{8,0},{12,4},{16,24},{20,28},{24,16},{28,20},{1,9},{5... | collective-permute-start | bytes 147464 | tf_op jit(solution)/shard_map/ppermute | solution.py:39
  105.9 5.2 %collective-permute-start.36 = (f32[3,64,64]{2,1,0:T(8,128)S(1)}, f32[3,64,64]{2,1,0:T(8,128)S(1)}, u32[]{:S(2)}, u32[]{:S(2)}) collective-permute-start(f32[3,64,64]{2,1,0:T(8,128)S(1)} %add.240), channel_id=1, source_target_pairs={{0,16},{4,20},{8,24},{12,28},{16,0},{20,4},{24,8},{28,12},{1,17},{... | collective-permute-start | bytes 147464 | tf_op jit(solution)/shard_map/ppermute | solution.py:39
  107.4 5.5 %collective-permute-start.37 = (f32[3,64,64]{2,1,0:T(8,128)S(1)}, f32[3,64,64]{2,1,0:T(8,128)S(1)}, u32[]{:S(2)}, u32[]{:S(2)}) collective-permute-start(f32[3,64,64]{2,1,0:T(8,128)S(1)} %add.240), channel_id=1, source_target_pairs={{0,24},{4,28},{8,16},{12,20},{16,8},{20,12},{24,0},{28,4},{1,25},{... | collective-permute-start | bytes 147464 | tf_op jit(solution)/shard_map/ppermute | solution.py:39
  112.9 7.6 %collective-permute-start.38 = (f32[3,64,64]{2,1,0:T(8,128)S(1)}, f32[3,64,64]{2,1,0:T(8,128)S(1)}, u32[]{:S(2)}, u32[]{:S(2)}) collective-permute-start(f32[3,64,64]{2,1,0:T(8,128)S(1)} %add_add_fusion.3), channel_id=1, source_target_pairs={{0,1},{1,0},{2,3},{3,2},{4,5},{5,4},{6,7},{7,6},{8,9},{9,8},{10,11... | collective-permute-start | bytes 147464 | tf_op jit(solution)/shard_map/ppermute | solution.py:39
  117.7 8.7 %collective-permute-start.39 = (f32[3,64,64]{2,1,0:T(8,128)S(1)}, f32[3,64,64]{2,1,0:T(8,128)S(1)}, u32[]{:S(2)}, u32[]{:S(2)}) collective-permute-start(f32[3,64,64]{2,1,0:T(8,128)S(1)} %add_add_fusion.3), channel_id=1, source_target_pairs={{0,2},{1,3},{2,0},{3,1},{4,6},{5,7},{6,4},{7,5},{8,10},{9,11},{10,... | collective-permute-start | bytes 147464 | tf_op jit(solution)/shard_map/ppermute | solution.py:39
  117.7 8.7 %collective-permute-start.40 = (f32[3,64,64]{2,1,0:T(8,128)S(1)}, f32[3,64,64]{2,1,0:T(8,128)S(1)}, u32[]{:S(2)}, u32[]{:S(2)}) collective-permute-start(f32[3,64,64]{2,1,0:T(8,128)S(1)} %add_add_fusion.3), channel_id=1, source_target_pairs={{0,3},{1,2},{2,1},{3,0},{4,7},{5,6},{6,5},{7,4},{8,11},{9,10},{10,... | collective-permute-start | bytes 147464 | tf_op jit(solution)/shard_map/ppermute | solution.py:39
  (14 other events, 234.7 us)

commit v2 on v1

v2 whole, which is shorter than its diff:
```python
import functools
import math

import jax
import jax.numpy as jnp
from jax import lax
from jax.experimental import pallas as pl
from jax.experimental.pallas import tpu as pltpu
from jax.sharding import PartitionSpec as P

EMB = 256
K = 64
BR = 128
MAXT = 48
REACH = 2
ITERS = 2

TAU = 6.0
EPS = 1e-06
PRECISE = lax.Precision.HIGHEST

WEIGHT = 1.0 / (BR * MAXT)
SIGMA = math.exp(TAU) * WEIGHT
EXP2 = TAU / EMB * math.log2(math.e)
GROUP = 8
SHARDS = 6
F32 = jnp.float32
BF16 = jnp.bfloat16
VMEM = pl.BlockSpec(memory_space=pltpu.VMEM)
SMEM = pl.BlockSpec(memory_space=pltpu.SMEM)


def swapped(value, axis, bits):
    count = lax.axis_size(axis)
    return lax.ppermute(value, axis, [(i, i ^ bits) for i in range(count)])


def rotated(value, axis, steps):
    count = lax.axis_size(axis)
    return lax.ppermute(value, axis, [(i, (i + steps) % count) for i in range(count)])


def other_side(value):
    count = lax.axis_size("rows")
    chips = count // 2
    pairs = []
    for r in range(count):
        chip, core = divmod(r, 2)
        to = (chip + 1) % chips if chip % 2 else (chip - 1) % chips
        pairs.append((r, to * 2 + core))
    return lax.ppermute(value, "rows", pairs)


def after(value, *others):
    return lax.optimization_barrier((value, *others))[0]


def across(value):
    return swapped(value, "rows", 2), other_side(value), swapped(value, "rows", 1)


def by_core(side_a, side_b):
    return [side_a, swapped(side_a, "rows", 1), side_b, swapped(side_b, "rows", 1)]


def chip_sum_part(value, part):
    rows, tiles = lax.axis_size("rows"), lax.axis_size("tiles")
    if rows // 2 == tiles == 4:
        parts = [value]
        for step in range(1, 4):
            pairs = []
            for r in range(rows):
                for t in range(tiles):
                    along_rows = r % 2 == part
                    to = (r ^ (2 * step), t) if along_rows else (r, (t + step) % tiles)
                    pairs.append((r * tiles + t, to[0] * tiles + to[1]))
            parts.append(lax.ppermute(value, ("rows", "tiles"), pairs))
        return sum(parts)
    if part == 0:
        return value + sum(rotated(value, "tiles", n) for n in range(1, tiles))
    bits = 2
    while bits < rows:
        span = min(4, rows // bits)
        value = value + sum(swapped(value, "rows", k * bits) for k in range(1, span))
        bits *= span
    return value


def dot_t(a, b):
    return lax.dot_general(a, b, (((1,), (1,)), ((), ())), preferred_element_type=F32)


def dot_exact(a, b):
    return lax.dot_general(
        a, b, (((1,), (1,)), ((), ())), precision=PRECISE, preferred_element_type=F32
    )


def unit_of(rows):
    values = rows.astype(F32)
    mean = jnp.sum(values * values, axis=1, keepdims=True) * (1.0 / EMB)
    return (values * lax.rsqrt(mean + EPS)).astype(BF16)


def pack_kernel(meta, emb, block, step, cols, emb_out, vec_out, cols_out, block_buf, step_buf, sems):
    here, width = meta[0], emb_out.shape[0]
    copies = [
        pltpu.make_async_copy(emb.at[pl.ds(here * width, width), :], emb_out, sems.at[0]),
        pltpu.make_async_copy(block, block_buf, sems.at[1]),
        pltpu.make_async_copy(step, step_buf, sems.at[2]),
    ]
    for copy in copies:
        copy.start()
    cols_out[...] = cols[...]
    copies[1].wait()
    vec_out[:K, :] = block_buf[...].astype(BF16)
    copies[2].wait()
    vec_out[K:, :] = step_buf[...].astype(BF16)
    copies[0].wait()


def group_copies(count, first, source, target, sems, body):
    @pl.loop(0, (count + GROUP - 1) // GROUP)
    def _(step):
        at = pl.ds(first + step * GROUP, GROUP)
        body(pltpu.make_async_copy(source.at[at], target.at[at], sems.at[step]))


def build_tiles(blocks, first, items, unit_own, unit_ext, tiles, tiles_out, sems):
    count = items[items.shape[0] - 1]

    @pl.loop(0, (count + GROUP - 1) // GROUP)
    def _(step):
        picked = [items[step * GROUP + g] for g in range(GROUP)]
        scores = [dot_t(unit_ext[f // blocks], unit_own[f % blocks]) for f in picked]
        for g in range(GROUP):
            tiles[first + step * GROUP + g] = jnp.exp2(scores[g] * EXP2).astype(BF16)
        at = pl.ds(first + step * GROUP, GROUP)
        pltpu.make_async_copy(tiles.at[at], tiles_out.at[at], sems.at[step]).start()

    group_copies(count, first, tiles, tiles_out, sems, lambda copy: copy.wait())


def unit_kernel(emb, unit, buf, sems):
    blocks, parts = unit.shape[0], sems.shape[0]
    each = blocks // parts
    copies = [
        pltpu.make_async_copy(
            emb.at[pl.ds(n * each, each)], buf.at[pl.ds(n * each, each)], sems.at[n]
        )
        for n in range(parts)
    ]
    for copy in copies:
        copy.start()
    for n, copy in enumerate(copies):
        copy.wait()

        @pl.loop(n * each, (n + 1) * each)
        def _(b):
            unit[b] = unit_of(buf[b])


def near_kernel(
    blocks, share, meta, items, unit_own, emb_core, diag_out, tiles_out, unit_ext, tiles, sems
):
    here = meta[0]
    for i in range(share):
        unit_ext[i] = unit_own[here * share + i]
        unit_ext[share + i] = unit_of(emb_core[pl.ds(i * BR, BR), :])
    rows = lax.broadcasted_iota(jnp.int32, (BR, BR), 0)
    cols = lax.broadcasted_iota(jnp.int32, (BR, BR), 1)
    for i in range(share):
        unit = unit_ext[i]
        weights = jnp.exp2(dot_t(unit, unit) * EXP2)
        on_diag = rows == cols
        diag_out[:, pl.ds(i * BR, BR)] = (
            jnp.sum(jnp.where(on_diag, weights, 0.0), axis=0, keepdims=True) * WEIGHT - SIGMA
        )
        tiles[i] = jnp.where(on_diag, 0.0, weights).astype(BF16)
    at = pl.ds(0, share)
    copy = pltpu.make_async_copy(tiles.at[at], tiles_out.at[at], sems.at[sems.shape[0] - 1])
    copy.start()
    build_tiles(blocks, share, items, unit_own, unit_ext, tiles, tiles_out, sems)
    copy.wait()


def far_kernel(blocks, share, meta, items, unit_own, *refs):
    emb, (tiles_out, unit_ext, tiles, sems) = refs[:-4], refs[-4:]
    for j, ref in enumerate(emb):
        for i in range(share):
            unit_ext[j * share + i] = unit_of(ref[pl.ds(i * BR, BR), :])
    build_tiles(blocks, 0, items, unit_own, unit_ext, tiles, tiles_out, sems)


def apply_kernel(blocks, share, devices, *refs):
    meta, items, stored = refs[0], refs[1:3], refs[3:5]
    vec, outs = refs[5 : 5 + SHARDS], refs[5 + SHARDS : -6]
    vec_ext, acc, tiles, sems = refs[-6], refs[-5], refs[-4:-2], refs[-2:]
    here = meta[0]
    counts = [ref[ref.shape[0] - 1] for ref in items]
    firsts = (share, 0)
    at = pl.ds(0, share)
    diag_copy = pltpu.make_async_copy(
        stored[0].at[at], tiles[0].at[at], sems[0].at[sems[0].shape[0] - 1]
    )
    diag_copy.start()
    for part in range(2):
        group_copies(
            counts[part], firsts[part], stored[part], tiles[part], sems[part],
            lambda copy: copy.start(),
        )
    for j, ref in enumerate(vec):
        for i in range(share):
            vec_ext[j * share + i] = ref[:, pl.ds(i * BR, BR)]
    acc[...] = jnp.zeros_like(acc)
    diag_copy.wait()
    for i in range(share):
        acc[here * share + i] = jnp.dot(vec_ext[i], tiles[0][i], preferred_element_type=F32)
    for part in range(2):
        count, first, base = counts[part], firsts[part], (0, 2 * share)[part]

        @pl.loop(0, (count + GROUP - 1) // GROUP)
        def _(step):
            group = pl.ds(first + step * GROUP, GROUP)
            pltpu.make_async_copy(
                stored[part].at[group], tiles[part].at[group], sems[part].at[step]
            ).wait()
            picked = []
            for g in range(GROUP):
                at = step * GROUP + g
                flat = items[part][at]
                picked.append(
                    (base + flat // blocks, jnp.where(at < count, flat % blocks, blocks))
                )
            parts = [
                jnp.dot(
                    vec_ext[ext],
                    tiles[part][first + step * GROUP + g],
                    preferred_element_type=F32,
                )
                for g, (ext, _) in enumerate(picked)
            ]
            for (_, to), value in zip(picked, parts):
                acc[to] += value

    for n, out in enumerate(outs):
        rows = pl.ds(n // devices * K, K)
        at_block = lax.rem(here + n % devices, devices) * share
        for i in range(share):
            value = acc[at_block + i, rows, :] * WEIGHT
            out[:, pl.ds(i * BR, BR)] = value.astype(out.dtype)


def summed(parts, diag, vectors):
    value = parts[0][...] + diag[...] * vectors
    for ref in parts[1:]:
        value = value + ref[...].astype(F32)
    return value


def image_kernel(devices, *refs):
    parts, (diag, vec, out, out_half) = refs[:devices], refs[devices:]
    value = summed(parts, diag, vec[...])
    out[...] = value
    out_half[...] = value.astype(BF16)


def mul(a, b):
    return jnp.dot(a, b, precision=PRECISE, preferred_element_type=F32)


def step_coefficients(g_vv, g_vs, g_ss, g_vj, g_sj, g_jj, rotation, total):
    eye = (
        lax.broadcasted_iota(jnp.int32, (K, K), 0) == lax.broadcasted_iota(jnp.int32, (K, K), 1)
    )
    m = g_vj * (1.0 / total) + SIGMA * (g_vv * (1.0 / total) - eye.astype(F32))
    resid_sq = (
        jnp.sum(jnp.where(eye, g_jj, 0.0), axis=0, keepdims=True)
        - 2.0 * jnp.sum(m * g_vj, axis=0, keepdims=True)
        + jnp.sum(m * mul(g_vv, m), axis=0, keepdims=True)
    )
    resid_inv = 1.0 / jnp.sqrt(jnp.maximum(resid_sq, 0.0) * (1.0 / total) + EPS)
    on_v, on_resid, on_s = rotation[:K].T, rotation[K : 2 * K].T, rotation[2 * K :].T
    p_j = on_resid * resid_inv
    p_step = -mul(p_j, m.T)
    p_v = jnp.concatenate([on_v + p_step, p_step], axis=0)
    p_s, p_j = jnp.concatenate([on_s, on_s], axis=0), jnp.concatenate([p_j, p_j], axis=0)
    g_v = mul(p_v, g_vv) + mul(p_j, g_vj.T) + mul(p_s, g_vs.T)
    g_s = mul(p_v, g_vs) + mul(p_j, g_sj.T) + mul(p_s, g_ss)
    g_j = mul(p_v, g_vj) + mul(p_j, g_jj) + mul(p_s, g_sj)
    comb_sq = jnp.sum((g_v * p_v + g_s * p_s + g_j * p_j)[:K], axis=1, keepdims=True)
    scale = 1.0 / jnp.sqrt(jnp.maximum(comb_sq, 0.0) * (1.0 / total) + EPS)
    scale = jnp.concatenate([scale, scale], axis=0)
    return scale * p_v, scale * p_s, scale * p_j, scale * g_v, scale * g_s, scale * g_j


def gram_kernel(x_ref, y_ref, j_ref, out):
    x, y, j = x_ref[...], y_ref[...], j_ref[...]
    for n, (a, b) in enumerate(((x, x), (x, y), (y, y), (x, j), (y, j), (j, j))):
        out[n] = dot_exact(a, b)


def first_kernel(devices, total, rot_ref, x_ref, y_ref, j_ref, diag, gram, *refs):
    parts, outs = refs[:devices], refs[devices:]
    v_out, s_out, part_out, c_out, g_out = outs
    eye = (
        lax.broadcasted_iota(jnp.int32, (K, K), 0) == lax.broadcasted_iota(jnp.int32, (K, K), 1)
    )
    xx, xy, yy, xj, yj, jj = (gram[n] for n in range(6))

    def inv_rms(square, axis):
        picked = jnp.sum(jnp.where(eye, square, 0.0), axis=axis, keepdims=True)
        return 1.0 / jnp.sqrt(picked * (1.0 / total) + EPS)

    x_col, x_row = inv_rms(xx, 1), inv_rms(xx, 0)
    y_col, y_row = inv_rms(yy, 1), inv_rms(yy, 0)
    g_vv, g_vs, g_ss = xx * x_col * x_row, xy * x_col * y_row, yy * y_col * y_row
    g_vj, g_sj, g_jj = xj * x_col * x_row, yj * y_col * x_row, jj * x_col * x_row
    p_v, p_s, p_j, g_v, g_s, g_j = step_coefficients(
        g_vv, g_vs, g_ss, g_vj, g_sj, g_jj, rot_ref[...], total
    )
    new = mul(g_v, p_v.T) + mul(g_s, p_s.T) + mul(g_j, p_j.T)
    g_out[0], g_out[1], g_out[2] = new[:K, :K], new[:K, K:], new[K:, K:]
    p_v, p_j, p_s = p_v * x_row, p_j * x_row, p_s * y_row
    x, y, j = x_ref[...], y_ref[...], j_ref[...]
    t = summed(parts, diag, y)
    both = mul(p_v, x) + mul(p_s, y) + mul(p_j, j)
    v_out[...], s_out[...] = both[:K], both[K:]
    part_out[...] = mul(p_v[:K], j) + mul(p_s[:K], t)
    c_out[...] = p_j[:K]


def second_kernel(devices, v_ref, s_ref, part_ref, c_ref, first_ref, diag, *refs):
    parts, (j_out, out) = refs[:devices], refs[devices:]
    j = part_ref[...] + mul(c_ref[...], summed(parts, diag, first_ref[...]))
    j_out[...] = j
    for n, a in enumerate((v_ref[...], s_ref[...], j)):
        out[n] = dot_exact(a, j)


def last_kernel(total, g_ref, rot_ref, v_ref, s_ref, j_ref, h_ref, v_out, s_out):
    p_v, p_s, p_j, _, _, _ = step_coefficients(
        g_ref[0], g_ref[1], g_ref[2], h_ref[0], h_ref[1], h_ref[2], rot_ref[...], total
    )
    both = mul(p_v, v_ref[...]) + mul(p_s, s_ref[...]) + mul(p_j, j_ref[...])
    v_out[...], s_out[...] = both[:K], both[K:]


def call(kernel, outs, *args, smem=0, hbm=0, scratch=(), us=0.0):
    any_memory = pl.BlockSpec(memory_space=pl.ANY)
    args = [
        pltpu.with_memory_space_constraint(arg, pltpu.HBM) if smem <= n < smem + hbm else arg
        for n, arg in enumerate(args)
    ]
    return pl.pallas_call(
        kernel,
        out_shape=tuple(
            pltpu.HBM(*out[:2]) if len(out) > 2 else jax.ShapeDtypeStruct(*out) for out in outs
        ),
        in_specs=[SMEM] * smem + [any_memory] * hbm + [VMEM] * (len(args) - smem - hbm),
        out_specs=tuple(any_memory if len(out) > 2 else VMEM for out in outs),
        scratch_shapes=list(scratch),
        compiler_params=pltpu.CompilerParams(vmem_limit_bytes=24 * 1024 * 1024),
        cost_estimate=pl.CostEstimate(
            flops=int(us * 1e9), bytes_accessed=0, transcendentals=0
        ),
    )(*args)


def tile_list(cols, counts, here, row, share, devices):
    blocks, span = cols[0].shape
    used = []
    for step, part in enumerate(cols):
        first = lax.rem(here - step + devices, devices) * span
        slot = first + lax.broadcasted_iota(jnp.int32, (blocks, span), 1)
        used.append((part, slot))
    col = jnp.concatenate([part for part, _ in used], axis=1)
    slot = jnp.concatenate([s for _, s in used], axis=1)
    block = row * blocks + lax.broadcasted_iota(jnp.int32, col.shape, 0)
    shard, inner = col // blocks, col % blocks
    other_core = (shard % 2 != row % 2).astype(jnp.int32)
    chip, own_chip = shard // 2, row // 2
    place = other_core + jnp.where(chip == own_chip, 0, jnp.where(chip == own_chip ^ 1, 2, 4))
    mine = (slot < counts[:, None]) & (inner // share == here) & (col != block)
    ext = jnp.where(mine, place * share + inner % share, -1)
    wanted = lax.broadcasted_iota(jnp.int32, (SHARDS * share, blocks, 1), 0)
    mask = jnp.any(ext[None] == wanted, axis=2).astype(F32)
    lists = []
    for part in (mask[: 2 * share], mask[2 * share :]):
        flat = part.size
        part = part.reshape(flat)
        index = jnp.arange(flat, dtype=jnp.int32)
        upto = (index[:, None] <= index[None, :]).astype(F32)
        place = jnp.dot(part, upto).astype(jnp.int32)
        wide = jnp.arange(flat + GROUP + 1, dtype=jnp.int32)[None, :]
        used = part[:, None] > 0
        hit = (place[:, None] == wide + 1) & used
        last = (wide == flat + GROUP) & used
        lists.append(jnp.sum(jnp.where(hit, index[:, None], last.astype(jnp.int32)), axis=0))
    return lists


def local(embedding, start_block, start_step, rotations, neighbour_cols, tile_counts):
    devices = lax.axis_size("tiles")
    width = start_block.shape[1]
    share = width // BR
    blocks = tile_counts.shape[0]
    total = width * devices * lax.axis_size("rows")
    here, row = lax.axis_index("tiles"), lax.axis_index("rows")

    meta = here.reshape(1)
    own_emb, own_vec, cols = call(
        pack_kernel,
        [((width, EMB), BF16), ((2 * K, width), BF16), (neighbour_cols.shape, jnp.int32)],
        meta,
        embedding,
        start_block,
        start_step,
        neighbour_cols,
        smem=1,
        hbm=3,
        scratch=[
            pltpu.VMEM((K, width), F32),
            pltpu.VMEM((K, width), F32),
            pltpu.SemaphoreType.DMA((3,)),
        ],
        us=1.0,
    )
    emb_a, emb_b, emb_core = across(own_emb)
    lists = after(cols, emb_core)
    lists = [lists] + [rotated(lists, "tiles", n) for n in range(1, devices)]
    items = tile_list(lists, tile_counts, here, row, share, devices)
    own_vec = after(own_vec, *lists)
    vec_a, vec_b = swapped(own_vec, "rows", 2), other_side(own_vec)

    (unit_own,) = call(
        unit_kernel,
        [((blocks, BR, EMB), BF16)],
        after(embedding.reshape(blocks, BR, EMB), emb_core),
        hbm=1,
        scratch=[pltpu.VMEM((blocks, BR, EMB), BF16), pltpu.SemaphoreType.DMA((4,))],
        us=1.5,
    )
    near, far = 2 * share * blocks, (SHARDS - 2) * share * blocks
    near_shape, far_shape = (share + near + GROUP, BR, BR), (far + GROUP, BR, BR)
    near_sems = pltpu.SemaphoreType.DMA((near // GROUP + 2,))
    far_sems = pltpu.SemaphoreType.DMA((far // GROUP + 1,))
    diag, tiles_near = call(
        functools.partial(near_kernel, blocks, share),
        [((1, width), F32), (near_shape, BF16, "hbm")],
        meta,
        items[0],
        unit_own,
        emb_core,
        smem=2,
        scratch=[
            pltpu.VMEM((2 * share, BR, EMB), BF16),
            pltpu.VMEM(near_shape, BF16),
            near_sems,
        ],
        us=2.0,
    )
    emb_a, emb_b = after(emb_a, diag), after(emb_b, diag)
    (tiles_far,) = call(
        functools.partial(far_kernel, blocks, share),
        [(far_shape, BF16, "hbm")],
        meta,
        items[1],
        unit_own,
        *by_core(emb_a, emb_b),
        smem=2,
        scratch=[
            pltpu.VMEM(((SHARDS - 2) * share, BR, EMB), BF16),
            pltpu.VMEM(far_shape, BF16),
            far_sems,
        ],
        us=2.0,
    )
    vec_core = swapped(after(own_vec, diag), "rows", 1)
    vec = [own_vec, vec_core, *by_core(after(vec_a, tiles_far), after(vec_b, tiles_far))]

    def applied(halo):
        rows = halo[0].shape[0]
        return call(
            functools.partial(apply_kernel, blocks, share, devices),
            ([((K, width), F32)] + [((K, width), BF16)] * (devices - 1)) * (rows // K),
            meta,
            *items,
            tiles_near,
            tiles_far,
            *halo,
            smem=3,
            hbm=2,
            scratch=[
                pltpu.VMEM((SHARDS * share, rows, BR), BF16),
                pltpu.VMEM((blocks + 1, rows, BR), F32),
                pltpu.VMEM(near_shape, BF16),
                pltpu.VMEM(far_shape, BF16),
                near_sems,
                far_sems,
            ],
            us=2.0,
        )

    def gathered(parts):
        return [parts[0]] + [rotated(part, "tiles", n + 1) for n, part in enumerate(parts[1:])]

    parts = applied(vec)
    parts, step_parts = gathered(parts[:devices]), gathered(parts[devices:])
    image, image_half = call(
        functools.partial(image_kernel, devices),
        [((K, width), F32), ((K, width), BF16)],
        *parts,
        diag,
        start_block,
        us=0.1,
    )
    image_a, image_b, image_core = across(image_half)
    (gram,) = call(
        gram_kernel,
        [((6, K, K), F32)],
        start_block,
        start_step,
        after(image, image_core),
        us=0.8,
    )
    image_vec = [image_half, image_core, *by_core(image_a, image_b)]
    gram = gram + swapped(gram, "rows", 1)
    gram = chip_sum_part(after(gram, image_vec[3]), 0)
    parts = applied(image_vec)
    gram = chip_sum_part(after(gram, parts[0]), 1)
    parts = gathered(parts)
    vectors, steps, part, coef, gram = call(
        functools.partial(first_kernel, devices, total),
        [((K, width), F32)] * 3 + [((K, K), F32), ((3, K, K), F32)],
        rotations[0],
        start_block,
        start_step,
        image,
        diag,
        gram,
        *step_parts,
        us=2.8,
    )
    image, products = call(
        functools.partial(second_kernel, devices),
        [((K, width), F32), ((3, K, K), F32)],
        vectors,
        steps,
        part,
        coef,
        image,
        diag,
        *parts,
        us=0.8,
    )
    products = products + swapped(products, "rows", 1)
    products = chip_sum_part(chip_sum_part(products, 0), 1)
    return call(
        functools.partial(last_kernel, total),
        [((K, width), F32)] * 2,
        gram,
        rotations[1],
        vectors,
        steps,
        image,
        products,
        us=2.8,
    )


def solution(mesh):
    return jax.shard_map(
        local,
        mesh=mesh,
        in_specs=(
            P("rows", None),
            P(None, ("rows", "tiles")),
            P(None, ("rows", "tiles")),
            P(),
            P("rows", "tiles"),
            P("rows"),
        ),
        out_specs=(P(None, ("rows", "tiles")), P(None, ("rows", "tiles"))),
        check_vma=False,
    )
```

time: 130 us -> 107 us (0.82)
  waiting for transfers between devices: 46.5 us -> 28.2 us
  other arithmetic: 5.41 us -> 1.39 us
  local copies, waits for them, and re-layouts: 5.25 us -> 1.26 us
  starting transfers between devices: 46.1 us -> 48.9 us
  Pallas kernels: 24.3 us -> 25.7 us
    ppermute x26 -> x14, waiting for transfers between devices: 36.1 us -> 4.39 us  [swapped(): return lax.ppermute(value, axis, [(i, i ^ bits) for i in range(count)])]
    ppermute x26 -> x14, starting transfers between devices: 24.6 us -> 3.64 us  [swapped(): return lax.ppermute(value, axis, [(i, i ^ bits) for i in range(count)])]
    ppermute x0 -> x12, waiting for transfers between devices: none -> 17.1 us  [chip_sum_part(): parts.append(lax.ppermute(value, ('rows', 'tiles'), pairs))]
    ppermute x0 -> x12, starting transfers between devices: none -> 14.8 us  [chip_sum_part(): parts.append(lax.ppermute(value, ('rows', 'tiles'), pairs))]
    ppermute x3, starting transfers between devices: 2.44 us -> 7.75 us  [other_side(): return lax.ppermute(value, 'rows', pairs)]
    ppermute x12, starting transfers between devices: 19 us -> 22.7 us  [rotated(): lax.ppermute(value, axis, [(i, (i + steps) % count) for i in range(count)])]
    unnamed x12, local copies, waits for them, and re-layouts: 3.22 us -> 0.89 us
    ppermute x12, waiting for transfers between devices: 7.03 us -> 4.88 us  [rotated(): lax.ppermute(value, axis, [(i, (i + steps) % count) for i in range(count)])]
  transfers between devices with their start and end apart: 41 -> 41, of which waited for: 16 -> 18; matrix products, arithmetic and copies ran while one was open for 5% -> 2% of each run, Pallas kernels for 5% -> 16%
where the time goes in v2:
time: 107 us
  starting transfers between devices  48.9 us (46%)
  waiting for transfers between devices  28.2 us (26%)
  Pallas kernels  25.7 us (24%)
  other arithmetic  1.39 us (1%)
  local copies, waits for them, and re-layouts  1.26 us (1%)
    pallas_call x11, Pallas kernels, call(): pl.pallas_call(kernel, out_shape=tuple((pltpu.HBM(*out[:2]) if len(out) >...  25.7 us
    ppermute x12, starting transfers between devices, rotated(): lax.ppermute(value, axis, [(i, (i + steps) % count) for i in range(count)])  22.7 us
    ppermute x12, waiting for transfers between devices, chip_sum_part(): parts.append(lax.ppermute(value, ('rows', 'tiles'), pairs))  17.1 us
    ppermute x12, starting transfers between devices, chip_sum_part(): parts.append(lax.ppermute(value, ('rows', 'tiles'), pairs))  14.8 us
    ppermute x3, starting transfers between devices, other_side(): return lax.ppermute(value, 'rows', pairs)  7.75 us
    ppermute x12, waiting for transfers between devices, rotated(): lax.ppermute(value, axis, [(i, (i + steps) % count) for i in range(count)])  4.88 us
    ppermute x14, waiting for transfers between devices, swapped(): return lax.ppermute(value, axis, [(i, i ^ bits) for i in range(count)])  4.39 us
    ppermute x14, starting transfers between devices, swapped(): return lax.ppermute(value, axis, [(i, i ^ bits) for i in range(count)])  3.64 us
  transfers between devices with their start and end apart: 41, of which 18 were waited for; matrix products, arithmetic and copies ran while one was open for 2% of the time, Pallas kernels for 16%

profile of v2, /device:TPU:0, one launch (start us, length us, event | category | flops | bytes accessed | tf_op | source)
XLA Modules:
  0.0 106.8 jit_solution(16198413902893499132)
XLA Ops:
  3.0 3.5 %collective-permute-start.6 = (bf16[512,256]{1,0:T(8,128)(2,1)S(1)}, bf16[512,256]{1,0:T(8,128)(2,1)S(1)}, u32[]{:S(2)}, u32[]{:S(2)}) collective-permute-start(bf16[512,256]{1,0:T(8,128)(2,1)S(1)} %get-tuple-element.40), channel_id=1, source_target_pairs={{0,24},{4,28},{8,16},{12,20},{16,8},{20,12},{24,0},{28,4},{1,25},{... | collective-permute-start | bytes 786440 | tf_op jit(solution)/shard_map/ppermute | solution.py:51
  7.2 1.6 %collective-permute-start.1 = (s32[16,12]{1,0:T(8,128)S(1)}, s32[16,12]{1,0:T(8,128)S(1)}, u32[]{:S(2)}, u32[]{:S(2)}) collective-permute-start(s32[16,12]{1,0:T(8,128)S(1)} %get-tuple-element.41), channel_id=1, source_target_pairs={{0,1},{1,2},{2,3},{3,0},{4,5},{5,6},{6,7},{7,4},{8,9},{9,10},{10,1... | collective-permute-start | bytes 2312 | tf_op jit(solution)/shard_map/ppermute | solution.py:40
  8.8 2.6 %collective-permute-start.2 = (s32[16,12]{1,0:T(8,128)S(1)}, s32[16,12]{1,0:T(8,128)S(1)}, u32[]{:S(2)}, u32[]{:S(2)}) collective-permute-start(s32[16,12]{1,0:T(8,128)S(1)} %get-tuple-element.41), channel_id=1, source_target_pairs={{0,2},{1,3},{2,0},{3,1},{4,6},{5,7},{6,4},{7,5},{8,10},{9,11},{10,... | collective-permute-start | bytes 2312 | tf_op jit(solution)/shard_map/ppermute | solution.py:40
  11.4 1.3 %collective-permute-start.3 = (s32[16,12]{1,0:T(8,128)S(1)}, s32[16,12]{1,0:T(8,128)S(1)}, u32[]{:S(2)}, u32[]{:S(2)}) collective-permute-start(s32[16,12]{1,0:T(8,128)S(1)} %get-tuple-element.41), channel_id=1, source_target_pairs={{0,3},{1,0},{2,1},{3,2},{4,7},{5,4},{6,5},{7,6},{8,11},{9,8},{10,9... | collective-permute-start | bytes 2312 | tf_op jit(solution)/shard_map/ppermute | solution.py:40
  12.7 2.7 %shard_map.78.unit_own = bf16[16,128,256]{2,1,0:T(8,128)(2,1)S(1)} custom-call(bf16[16,128,256]{2,1,0:T(8,128)(2,1)} %bitcast.14), custom_call_target="tpu_custom_call" | custom-call | flops 1500000000 | tf_op jit(solution)/shard_map/pallas_call | solution.py:355
  16.1 1.5 %collective-permute-start.11 = (bf16[128,512]{1,0:T(8,128)(2,1)S(1)}, bf16[128,512]{1,0:T(8,128)(2,1)S(1)}, u32[]{:S(2)}, u32[]{:S(2)}) collective-permute-start(bf16[128,512]{1,0:T(8,128)(2,1)S(1)} %get-tuple-element.49.refs_5_), channel_id=1, source_target_pairs={{0,24},{4,28},{8,16},{12,20},{16,8},{20,12},{24,0},{28,4},{1,25},{... | collective-permute-start | bytes 393224 | tf_op jit(solution)/shard_map/ppermute | solution.py:51
  18.7 3.6 %shard_map.79 = (f32[1,512]{1,0:T(1,128)S(1)}, bf16[140,128,128]{2,1,0:T(8,128)(2,1)}) custom-call(s32[1]{0:T(128)} %bitcast.1.meta.refs_0_, s32[137]{0:T(256)S(1)} %select_reduce_fusion.1.items.refs_1_, bf16[16,128,256]{2,1,0:T(8,128)(2,1)S(1)} %shard_map.78.unit_own, bf16[512,256]{1,0:T(8,128)(2,1)S(1)} %collective-permute-done.emb_core), custom_call_target="tpu_custom_call" | custom-call | flops 2000000000 | tf_op jit(solution)/shard_map/pallas_call | solution.py:355
  24.2 2.9 %shard_map.80.refs_4_ = bf16[264,128,128]{2,1,0:T(8,128)(2,1)} custom-call(s32[1]{0:T(128)} %bitcast.1.meta.refs_0_, s32[265]{0:T(512)S(1)} %select_reduce_fusion.items.refs_2_, bf16[16,128,256]{2,1,0:T(8,128)(2,1)S(1)} %shard_map.78.unit_own, bf16[512,256]{1,0:T(8,128)(2,1)S(1)} %collective-permute-done.4.refs_0_, ...), custom_call_target="tpu_custom_call" | custom-call | flops 2000000000 | tf_op jit(solution)/shard_map/pallas_call | solution.py:355
  29.4 4.3 %shard_map.81 = (f32[64,512]{1,0:T(8,128)S(1)}, bf16[64,512]{1,0:T(8,128)(2,1)S(1)}, bf16[64,512]{1,0:T(8,128)(2,1)S(1)}, bf16[64,512]{1,0:T(8,128)(2,1)S(1)}, f...) custom-call(s32[1]{0:T(128)} %bitcast.1.meta.refs_0_, ...), custom_call_target="tpu_custom_call" | custom-call | flops 2000000000 | tf_op jit(solution)/shard_map/pallas_call | solution.py:355
  34.1 1.9 %collective-permute-start.14 = (bf16[64,512]{1,0:T(8,128)(2,1)S(1)}, bf16[64,512]{1,0:T(8,128)(2,1)S(1)}, u32[]{:S(2)}, u32[]{:S(2)}) collective-permute-start(bf16[64,512]{1,0:T(8,128)(2,1)S(1)} %get-tuple-element.54), channel_id=1, source_target_pairs={{0,2},{1,3},{2,0},{3,1},{4,6},{5,7},{6,4},{7,5},{8,10},{9,11},{10,... | collective-permute-start | bytes 196616 | tf_op jit(solution)/shard_map/ppermute | solution.py:40
  36.0 1.6 %collective-permute-start.15 = (bf16[64,512]{1,0:T(8,128)(2,1)S(1)}, bf16[64,512]{1,0:T(8,128)(2,1)S(1)}, u32[]{:S(2)}, u32[]{:S(2)}) collective-permute-start(bf16[64,512]{1,0:T(8,128)(2,1)S(1)} %get-tuple-element.55), channel_id=1, source_target_pairs={{0,3},{1,0},{2,1},{3,2},{4,7},{5,4},{6,5},{7,6},{8,11},{9,8},{10,9... | collective-permute-start | bytes 196616 | tf_op jit(solution)/shard_map/ppermute | solution.py:40
  37.6 2.9 %collective-permute-done.13.refs_1_ = bf16[64,512]{1,0:T(8,128)(2,1)S(1)} collective-permute-done((bf16[64,512]{1,0:T(8,128)(2,1)S(1)}, bf16[64,512]{1,0:T(8,128)(2,1)S(1)}, u32[]{:S(2)}, u32[]{:S(2)}) %collective-permute-start.13) | collective-permute-done | bytes 65568 | tf_op jit(solution)/shard_map/ppermute | solution.py:40
  40.5 1.9 %collective-permute-done.14.refs_2_ = bf16[64,512]{1,0:T(8,128)(2,1)S(1)} collective-permute-done((bf16[64,512]{1,0:T(8,128)(2,1)S(1)}, bf16[64,512]{1,0:T(8,128)(2,1)S(1)}, u32[]{:S(2)}, u32[]{:S(2)}) %collective-permute-start.14) | collective-permute-done | bytes 65568 | tf_op jit(solution)/shard_map/ppermute | solution.py:40
  42.8 2.7 %collective-permute-start.23 = (bf16[64,512]{1,0:T(8,128)(2,1)S(1)}, bf16[64,512]{1,0:T(8,128)(2,1)S(1)}, u32[]{:S(2)}, u32[]{:S(2)}) collective-permute-start(bf16[64,512]{1,0:T(8,128)(2,1)S(1)} %get-tuple-element.57.refs_5_), channel_id=1, source_target_pairs={{0,24},{4,28},{8,16},{12,20},{16,8},{20,12},{24,0},{28,4},{1,25},{... | collective-permute-start | bytes 196616 | tf_op jit(solution)/shard_map/ppermute | solution.py:51
  47.5 1.8 %collective-permute-done.23.refs_9_ = bf16[64,512]{1,0:T(8,128)(2,1)S(1)} collective-permute-done((bf16[64,512]{1,0:T(8,128)(2,1)S(1)}, bf16[64,512]{1,0:T(8,128)(2,1)S(1)}, u32[]{:S(2)}, u32[]{:S(2)}) %collective-permute-start.23) | collective-permute-done | bytes 65568 | tf_op jit(solution)/shard_map/ppermute | solution.py:51
  49.9 1.4 %collective-permute-start.21 = (f32[6,64,64]{2,1,0:T(8,128)S(1)}, f32[6,64,64]{2,1,0:T(8,128)S(1)}, u32[]{:S(2)}, u32[]{:S(2)}) collective-permute-start(f32[6,64,64]{2,1,0:T(8,128)S(1)} %add.204), channel_id=1, source_target_pairs={{0,16},{1,17},{2,18},{3,19},{4,6},{5,7},{6,4},{7,5},{8,24},{9,25},... | collective-permute-start | bytes 294920 | tf_op jit(solution)/shard_map/ppermute | solution.py:77
  51.4 1.6 %collective-permute-start.22 = (f32[6,64,64]{2,1,0:T(8,128)S(1)}, f32[6,64,64]{2,1,0:T(8,128)S(1)}, u32[]{:S(2)}, u32[]{:S(2)}) collective-permute-start(f32[6,64,64]{2,1,0:T(8,128)S(1)} %add.204), channel_id=1, source_target_pairs={{0,24},{1,25},{2,26},{3,27},{4,7},{5,4},{6,5},{7,6},{8,16},{9,17},... | collective-permute-start | bytes 294920 | tf_op jit(solution)/shard_map/ppermute | solution.py:77
  53.0 4.0 %shard_map.84 = (f32[64,512]{1,0:T(8,128)S(1)}, bf16[64,512]{1,0:T(8,128)(2,1)S(1)}, bf16[64,512]{1,0:T(8,128)(2,1)S(1)}, bf16[64,512]{1,0:T(8,128)(2,1)S(1)}) custom-call(s32[1]{0:T(128)} %bitcast.1.meta.refs_0_, s32[137]{0:T(256)S(1)} %select_reduce_fusion.1.items.refs_1_, s32[265]{0:T(512)S(1)} %select_reduce_fusion.items.refs_2_, ...), custom_call_target="tpu_custom_call" | custom-call | flops 2000000000 | tf_op jit(solution)/shard_map/pallas_call | solution.py:355
  58.0 1.4 %collective-permute-start.25 = (f32[6,64,64]{2,1,0:T(8,128)S(1)}, f32[6,64,64]{2,1,0:T(8,128)S(1)}, u32[]{:S(2)}, u32[]{:S(2)}) collective-permute-start(f32[6,64,64]{2,1,0:T(8,128)S(1)} %add_add_fusion.1), channel_id=1, source_target_pairs={{0,1},{1,2},{2,3},{3,0},{4,12},{5,13},{6,14},{7,15},{8,9},{9,10},{... | collective-permute-start | bytes 294920 | tf_op jit(solution)/shard_map/ppermute | solution.py:77
  59.4 1.5 %collective-permute-start.26 = (f32[6,64,64]{2,1,0:T(8,128)S(1)}, f32[6,64,64]{2,1,0:T(8,128)S(1)}, u32[]{:S(2)}, u32[]{:S(2)}) collective-permute-start(f32[6,64,64]{2,1,0:T(8,128)S(1)} %add_add_fusion.1), channel_id=1, source_target_pairs={{0,2},{1,3},{2,0},{3,1},{4,20},{5,21},{6,22},{7,23},{8,10},{9,11},... | collective-permute-start | bytes 294920 | tf_op jit(solution)/shard_map/ppermute | solution.py:77
  63.0 1.5 %collective-permute-start.29 = (bf16[64,512]{1,0:T(8,128)(2,1)S(1)}, bf16[64,512]{1,0:T(8,128)(2,1)S(1)}, u32[]{:S(2)}, u32[]{:S(2)}) collective-permute-start(bf16[64,512]{1,0:T(8,128)(2,1)S(1)} %get-tuple-element.64), channel_id=1, source_target_pairs={{0,2},{1,3},{2,0},{3,1},{4,6},{5,7},{6,4},{7,5},{8,10},{9,11},{10,... | collective-permute-start | bytes 196616 | tf_op jit(solution)/shard_map/ppermute | solution.py:40
  67.0 5.4 %collective-permute-done.26 = f32[6,64,64]{2,1,0:T(8,128)S(1)} collective-permute-done((f32[6,64,64]{2,1,0:T(8,128)S(1)}, f32[6,64,64]{2,1,0:T(8,128)S(1)}, u32[]{:S(2)}, u32[]{:S(2)}) %collective-permute-start.26) | collective-permute-done | bytes 98336 | tf_op jit(solution)/shard_map/ppermute | solution.py:77
  72.4 3.0 %collective-permute-start.31 = (bf16[64,512]{1,0:T(8,128)(2,1)S(1)}, bf16[64,512]{1,0:T(8,128)(2,1)S(1)}, u32[]{:S(2)}, u32[]{:S(2)}) collective-permute-start(bf16[64,512]{1,0:T(8,128)(2,1)S(1)} %get-tuple-element.71), channel_id=1, source_target_pairs={{0,1},{1,2},{2,3},{3,0},{4,5},{5,6},{6,7},{7,4},{8,9},{9,10},{10,1... | collective-permute-start | bytes 196616 | tf_op jit(solution)/shard_map/ppermute | solution.py:40
  75.4 3.5 %collective-permute-start.32 = (bf16[64,512]{1,0:T(8,128)(2,1)S(1)}, bf16[64,512]{1,0:T(8,128)(2,1)S(1)}, u32[]{:S(2)}, u32[]{:S(2)}) collective-permute-start(bf16[64,512]{1,0:T(8,128)(2,1)S(1)} %get-tuple-element.72), channel_id=1, source_target_pairs={{0,2},{1,3},{2,0},{3,1},{4,6},{5,7},{6,4},{7,5},{8,10},{9,11},{10,... | collective-permute-start | bytes 196616 | tf_op jit(solution)/shard_map/ppermute | solution.py:40
  78.9 2.9 %collective-permute-start.33 = (bf16[64,512]{1,0:T(8,128)(2,1)S(1)}, bf16[64,512]{1,0:T(8,128)(2,1)S(1)}, u32[]{:S(2)}, u32[]{:S(2)}) collective-permute-start(bf16[64,512]{1,0:T(8,128)(2,1)S(1)} %get-tuple-element.73), channel_id=1, source_target_pairs={{0,3},{1,0},{2,1},{3,2},{4,7},{5,4},{6,5},{7,6},{8,11},{9,8},{10,9... | collective-permute-start | bytes 196616 | tf_op jit(solution)/shard_map/ppermute | solution.py:40
  81.9 2.8 %shard_map.85 = (f32[64,512]{1,0:T(8,128)S(1)}, f32[64,512]{1,0:T(8,128)S(1)}, f32[64,512]{1,0:T(8,128)S(1)}, f32[64,64]{1,0:T(8,128)S(1)}, f32[3,64,64]{2,1,0:T(8,128)S(1)}) custom-call(f32[192,64]{1,0:T(8,128)S(1)} %bitcast.11, f32[64,512]{1,0:T(8,128)S(1)} %copy-done, f32[64,512]{1,0:T(8,128)S(1)} %copy-done.1, ...), custom_call_target="tpu_custom_call" | custom-call | flops 2800000000 | tf_op jit(solution)/shard_map/pallas_call | solution.py:355
  86.8 1.4 %collective-permute-start.35 = (f32[3,64,64]{2,1,0:T(8,128)S(1)}, f32[3,64,64]{2,1,0:T(8,128)S(1)}, u32[]{:S(2)}, u32[]{:S(2)}) collective-permute-start(f32[3,64,64]{2,1,0:T(8,128)S(1)} %add.211), channel_id=1, source_target_pairs={{0,8},{1,9},{2,10},{3,11},{4,5},{5,6},{6,7},{7,4},{8,0},{9,1},{10,... | collective-permute-start | bytes 147464 | tf_op jit(solution)/shard_map/ppermute | solution.py:77
  92.8 1.7 %collective-permute-done.37 = f32[3,64,64]{2,1,0:T(8,128)S(1)} collective-permute-done((f32[3,64,64]{2,1,0:T(8,128)S(1)}, f32[3,64,64]{2,1,0:T(8,128)S(1)}, u32[]{:S(2)}, u32[]{:S(2)}) %collective-permute-start.37) | collective-permute-done | bytes 49184 | tf_op jit(solution)/shard_map/ppermute | solution.py:77
  94.6 3.8 %collective-permute-start.39 = (f32[3,64,64]{2,1,0:T(8,128)S(1)}, f32[3,64,64]{2,1,0:T(8,128)S(1)}, u32[]{:S(2)}, u32[]{:S(2)}) collective-permute-start(f32[3,64,64]{2,1,0:T(8,128)S(1)} %add_add_fusion.3), channel_id=1, source_target_pairs={{0,2},{1,3},{2,0},{3,1},{4,20},{5,21},{6,22},{7,23},{8,10},{9,11},... | collective-permute-start | bytes 147464 | tf_op jit(solution)/shard_map/ppermute | solution.py:77
  98.6 2.6 %collective-permute-done.38 = f32[3,64,64]{2,1,0:T(8,128)S(1)} collective-permute-done((f32[3,64,64]{2,1,0:T(8,128)S(1)}, f32[3,64,64]{2,1,0:T(8,128)S(1)}, u32[]{:S(2)}, u32[]{:S(2)}) %collective-permute-start.38) | collective-permute-done | bytes 49184 | tf_op jit(solution)/shard_map/ppermute | solution.py:77
  101.1 2.1 %collective-permute-done.39 = f32[3,64,64]{2,1,0:T(8,128)S(1)} collective-permute-done((f32[3,64,64]{2,1,0:T(8,128)S(1)}, f32[3,64,64]{2,1,0:T(8,128)S(1)}, u32[]{:S(2)}, u32[]{:S(2)}) %collective-permute-start.39) | collective-permute-done | bytes 49184 | tf_op jit(solution)/shard_map/ppermute | solution.py:77
  104.0 2.8 %shard_map.87 = (f32[64,512]{1,0:T(8,128)}, f32[64,512]{1,0:T(8,128)}) custom-call(f32[3,64,64]{2,1,0:T(8,128)S(1)} %get-tuple-element.66.g_ref, f32[192,64]{1,0:T(8,128)S(1)} %bitcast.12, f32[64,512]{1,0:T(8,128)S(1)} %get-tuple-element.67.v_ref, f32[64,512]{1,0:T(8,128)S(1)} %get-tuple-element.68.s_ref, f32[64,512]{1,0:T(8,128)S(1)} %get-tuple-element.74.j_ref, ...), custom_call_target="tpu_custom_call" | custom-call | flops 2800000000 | tf_op jit(solution)/shard_map/pallas_call | solution.py:355
  (104 shorter events, 25.5 us)
Async XLA Ops:
  2.4 4.7 %collective-permute-start = (bf16[512,256]{1,0:T(8,128)(2,1)S(1)}, bf16[512,256]{1,0:T(8,128)(2,1)S(1)}, u32[]{:S(2)}, u32[]{:S(2)}) collective-permute-start(bf16[512,256]{1,0:T(8,128)(2,1)S(1)} %get-tuple-element.40), channel_id=1, source_target_pairs={{0,4},{4,0},{8,12},{12,8},{16,20},{20,16},{24,28},{28,24},{1,5},{5... | collective-permute-start | bytes 786440 | tf_op jit(solution)/shard_map/ppermute | solution.py:35
  3.0 19.3 %collective-permute-start.6 = (bf16[512,256]{1,0:T(8,128)(2,1)S(1)}, bf16[512,256]{1,0:T(8,128)(2,1)S(1)}, u32[]{:S(2)}, u32[]{:S(2)}) collective-permute-start(bf16[512,256]{1,0:T(8,128)(2,1)S(1)} %get-tuple-element.40), channel_id=1, source_target_pairs={{0,24},{4,28},{8,16},{12,20},{16,8},{20,12},{24,0},{28,4},{1,25},{... | collective-permute-start | bytes 786440 | tf_op jit(solution)/shard_map/ppermute | solution.py:51
  6.5 15.9 %collective-permute-start.4 = (bf16[512,256]{1,0:T(8,128)(2,1)S(1)}, bf16[512,256]{1,0:T(8,128)(2,1)S(1)}, u32[]{:S(2)}, u32[]{:S(2)}) collective-permute-start(bf16[512,256]{1,0:T(8,128)(2,1)S(1)} %get-tuple-element.40), channel_id=1, source_target_pairs={{0,8},{4,12},{8,0},{12,4},{16,24},{20,28},{24,16},{28,20},{1,9},{5... | collective-permute-start | bytes 786440 | tf_op jit(solution)/shard_map/ppermute | solution.py:35
  7.2 8.2 %collective-permute-start.1 = (s32[16,12]{1,0:T(8,128)S(1)}, s32[16,12]{1,0:T(8,128)S(1)}, u32[]{:S(2)}, u32[]{:S(2)}) collective-permute-start(s32[16,12]{1,0:T(8,128)S(1)} %get-tuple-element.41), channel_id=1, source_target_pairs={{0,1},{1,2},{2,3},{3,0},{4,5},{5,6},{6,7},{7,4},{8,9},{9,10},{10,1... | collective-permute-start | bytes 2312 | tf_op jit(solution)/shard_map/ppermute | solution.py:40
  8.8 6.6 %collective-permute-start.2 = (s32[16,12]{1,0:T(8,128)S(1)}, s32[16,12]{1,0:T(8,128)S(1)}, u32[]{:S(2)}, u32[]{:S(2)}) collective-permute-start(s32[16,12]{1,0:T(8,128)S(1)} %get-tuple-element.41), channel_id=1, source_target_pairs={{0,2},{1,3},{2,0},{3,1},{4,6},{5,7},{6,4},{7,5},{8,10},{9,11},{10,... | collective-permute-start | bytes 2312 | tf_op jit(solution)/shard_map/ppermute | solution.py:40
  11.4 4.0 %collective-permute-start.3 = (s32[16,12]{1,0:T(8,128)S(1)}, s32[16,12]{1,0:T(8,128)S(1)}, u32[]{:S(2)}, u32[]{:S(2)}) collective-permute-start(s32[16,12]{1,0:T(8,128)S(1)} %get-tuple-element.41), channel_id=1, source_target_pairs={{0,3},{1,0},{2,1},{3,2},{4,7},{5,4},{6,5},{7,6},{8,11},{9,8},{10,9... | collective-permute-start | bytes 2312 | tf_op jit(solution)/shard_map/ppermute | solution.py:40
  16.1 11.1 %collective-permute-start.11 = (bf16[128,512]{1,0:T(8,128)(2,1)S(1)}, bf16[128,512]{1,0:T(8,128)(2,1)S(1)}, u32[]{:S(2)}, u32[]{:S(2)}) collective-permute-start(bf16[128,512]{1,0:T(8,128)(2,1)S(1)} %get-tuple-element.49.refs_5_), channel_id=1, source_target_pairs={{0,24},{4,28},{8,16},{12,20},{16,8},{20,12},{24,0},{28,4},{1,25},{... | collective-permute-start | bytes 393224 | tf_op jit(solution)/shard_map/ppermute | solution.py:51
  17.6 10.5 %collective-permute-start.9 = (bf16[128,512]{1,0:T(8,128)(2,1)S(1)}, bf16[128,512]{1,0:T(8,128)(2,1)S(1)}, u32[]{:S(2)}, u32[]{:S(2)}) collective-permute-start(bf16[128,512]{1,0:T(8,128)(2,1)S(1)} %get-tuple-element.49.refs_5_), channel_id=1, source_target_pairs={{0,8},{4,12},{8,0},{12,4},{16,24},{20,28},{24,16},{28,20},{1,9},{5... | collective-permute-start | bytes 393224 | tf_op jit(solution)/shard_map/ppermute | solution.py:35
  23.2 4.9 %collective-permute-start.8 = (bf16[128,512]{1,0:T(8,128)(2,1)S(1)}, bf16[128,512]{1,0:T(8,128)(2,1)S(1)}, u32[]{:S(2)}, u32[]{:S(2)}) collective-permute-start(bf16[128,512]{1,0:T(8,128)(2,1)S(1)} %get-tuple-element.49.refs_5_), channel_id=1, source_target_pairs={{0,4},{4,0},{8,12},{12,8},{16,20},{20,16},{24,28},{28,24},{1,5},{5... | collective-permute-start | bytes 393224 | tf_op jit(solution)/shard_map/ppermute | solution.py:35
  33.7 6.8 %collective-permute-start.13 = (bf16[64,512]{1,0:T(8,128)(2,1)S(1)}, bf16[64,512]{1,0:T(8,128)(2,1)S(1)}, u32[]{:S(2)}, u32[]{:S(2)}) collective-permute-start(bf16[64,512]{1,0:T(8,128)(2,1)S(1)} %get-tuple-element.53), channel_id=1, source_target_pairs={{0,1},{1,2},{2,3},{3,0},{4,5},{5,6},{6,7},{7,4},{8,9},{9,10},{10,1... | collective-permute-start | bytes 196616 | tf_op jit(solution)/shard_map/ppermute | solution.py:40
  34.1 8.3 %collective-permute-start.14 = (bf16[64,512]{1,0:T(8,128)(2,1)S(1)}, bf16[64,512]{1,0:T(8,128)(2,1)S(1)}, u32[]{:S(2)}, u32[]{:S(2)}) collective-permute-start(bf16[64,512]{1,0:T(8,128)(2,1)S(1)} %get-tuple-element.54), channel_id=1, source_target_pairs={{0,2},{1,3},{2,0},{3,1},{4,6},{5,7},{6,4},{7,5},{8,10},{9,11},{10,... | collective-permute-start | bytes 196616 | tf_op jit(solution)/shard_map/ppermute | solution.py:40
  36.0 6.4 %collective-permute-start.15 = (bf16[64,512]{1,0:T(8,128)(2,1)S(1)}, bf16[64,512]{1,0:T(8,128)(2,1)S(1)}, u32[]{:S(2)}, u32[]{:S(2)}) collective-permute-start(bf16[64,512]{1,0:T(8,128)(2,1)S(1)} %get-tuple-element.55), channel_id=1, source_target_pairs={{0,3},{1,0},{2,1},{3,2},{4,7},{5,4},{6,5},{7,6},{8,11},{9,8},{10,9... | collective-permute-start | bytes 196616 | tf_op jit(solution)/shard_map/ppermute | solution.py:40
  42.6 5.0 %collective-permute-start.18 = (bf16[64,512]{1,0:T(8,128)(2,1)S(1)}, bf16[64,512]{1,0:T(8,128)(2,1)S(1)}, u32[]{:S(2)}, u32[]{:S(2)}) collective-permute-start(bf16[64,512]{1,0:T(8,128)(2,1)S(1)} %get-tuple-element.57.refs_5_), channel_id=1, source_target_pairs={{0,8},{4,12},{8,0},{12,4},{16,24},{20,28},{24,16},{28,20},{1,9},{5... | collective-permute-start | bytes 196616 | tf_op jit(solution)/shard_map/ppermute | solution.py:35
  42.8 6.6 %collective-permute-start.23 = (bf16[64,512]{1,0:T(8,128)(2,1)S(1)}, bf16[64,512]{1,0:T(8,128)(2,1)S(1)}, u32[]{:S(2)}, u32[]{:S(2)}) collective-permute-start(bf16[64,512]{1,0:T(8,128)(2,1)S(1)} %get-tuple-element.57.refs_5_), channel_id=1, source_target_pairs={{0,24},{4,28},{8,16},{12,20},{16,8},{20,12},{24,0},{28,4},{1,25},{... | collective-permute-start | bytes 196616 | tf_op jit(solution)/shard_map/ppermute | solution.py:51
  49.4 7.6 %collective-permute-start.20 = (f32[6,64,64]{2,1,0:T(8,128)S(1)}, f32[6,64,64]{2,1,0:T(8,128)S(1)}, u32[]{:S(2)}, u32[]{:S(2)}) collective-permute-start(f32[6,64,64]{2,1,0:T(8,128)S(1)} %add.204), channel_id=1, source_target_pairs={{0,8},{1,9},{2,10},{3,11},{4,5},{5,6},{6,7},{7,4},{8,0},{9,1},{10,... | collective-permute-start | bytes 294920 | tf_op jit(solution)/shard_map/ppermute | solution.py:77
  49.9 7.1 %collective-permute-start.21 = (f32[6,64,64]{2,1,0:T(8,128)S(1)}, f32[6,64,64]{2,1,0:T(8,128)S(1)}, u32[]{:S(2)}, u32[]{:S(2)}) collective-permute-start(f32[6,64,64]{2,1,0:T(8,128)S(1)} %add.204), channel_id=1, source_target_pairs={{0,16},{1,17},{2,18},{3,19},{4,6},{5,7},{6,4},{7,5},{8,24},{9,25},... | collective-permute-start | bytes 294920 | tf_op jit(solution)/shard_map/ppermute | solution.py:77
  51.4 6.6 %collective-permute-start.22 = (f32[6,64,64]{2,1,0:T(8,128)S(1)}, f32[6,64,64]{2,1,0:T(8,128)S(1)}, u32[]{:S(2)}, u32[]{:S(2)}) collective-permute-start(f32[6,64,64]{2,1,0:T(8,128)S(1)} %add.204), channel_id=1, source_target_pairs={{0,24},{1,25},{2,26},{3,27},{4,7},{5,4},{6,5},{7,6},{8,16},{9,17},... | collective-permute-start | bytes 294920 | tf_op jit(solution)/shard_map/ppermute | solution.py:77
  58.0 7.7 %collective-permute-start.25 = (f32[6,64,64]{2,1,0:T(8,128)S(1)}, f32[6,64,64]{2,1,0:T(8,128)S(1)}, u32[]{:S(2)}, u32[]{:S(2)}) collective-permute-start(f32[6,64,64]{2,1,0:T(8,128)S(1)} %add_add_fusion.1), channel_id=1, source_target_pairs={{0,1},{1,2},{2,3},{3,0},{4,12},{5,13},{6,14},{7,15},{8,9},{9,10},{... | collective-permute-start | bytes 294920 | tf_op jit(solution)/shard_map/ppermute | solution.py:77
  59.4 13.0 %collective-permute-start.26 = (f32[6,64,64]{2,1,0:T(8,128)S(1)}, f32[6,64,64]{2,1,0:T(8,128)S(1)}, u32[]{:S(2)}, u32[]{:S(2)}) collective-permute-start(f32[6,64,64]{2,1,0:T(8,128)S(1)} %add_add_fusion.1), channel_id=1, source_target_pairs={{0,2},{1,3},{2,0},{3,1},{4,20},{5,21},{6,22},{7,23},{8,10},{9,11},... | collective-permute-start | bytes 294920 | tf_op jit(solution)/shard_map/ppermute | solution.py:77
  60.9 14.5 %collective-permute-start.27 = (f32[6,64,64]{2,1,0:T(8,128)S(1)}, f32[6,64,64]{2,1,0:T(8,128)S(1)}, u32[]{:S(2)}, u32[]{:S(2)}) collective-permute-start(f32[6,64,64]{2,1,0:T(8,128)S(1)} %add_add_fusion.1), channel_id=1, source_target_pairs={{0,3},{1,0},{2,1},{3,2},{4,28},{5,29},{6,30},{7,31},{8,11},{9,8},{... | collective-permute-start | bytes 294920 | tf_op jit(solution)/shard_map/ppermute | solution.py:77
  62.0 16.9 %collective-permute-start.28 = (bf16[64,512]{1,0:T(8,128)(2,1)S(1)}, bf16[64,512]{1,0:T(8,128)(2,1)S(1)}, u32[]{:S(2)}, u32[]{:S(2)}) collective-permute-start(bf16[64,512]{1,0:T(8,128)(2,1)S(1)} %get-tuple-element.63), channel_id=1, source_target_pairs={{0,1},{1,2},{2,3},{3,0},{4,5},{5,6},{6,7},{7,4},{8,9},{9,10},{10,1... | collective-permute-start | bytes 196616 | tf_op jit(solution)/shard_map/ppermute | solution.py:40
  63.0 18.8 %collective-permute-start.29 = (bf16[64,512]{1,0:T(8,128)(2,1)S(1)}, bf16[64,512]{1,0:T(8,128)(2,1)S(1)}, u32[]{:S(2)}, u32[]{:S(2)}) collective-permute-start(bf16[64,512]{1,0:T(8,128)(2,1)S(1)} %get-tuple-element.64), channel_id=1, source_target_pairs={{0,2},{1,3},{2,0},{3,1},{4,6},{5,7},{6,4},{7,5},{8,10},{9,11},{10,... | collective-permute-start | bytes 196616 | tf_op jit(solution)/shard_map/ppermute | solution.py:40
  65.7 16.2 %collective-permute-start.30 = (bf16[64,512]{1,0:T(8,128)(2,1)S(1)}, bf16[64,512]{1,0:T(8,128)(2,1)S(1)}, u32[]{:S(2)}, u32[]{:S(2)}) collective-permute-start(bf16[64,512]{1,0:T(8,128)(2,1)S(1)} %get-tuple-element.65), channel_id=1, source_target_pairs={{0,3},{1,0},{2,1},{3,2},{4,7},{5,4},{6,5},{7,6},{8,11},{9,8},{10,9... | collective-permute-start | bytes 196616 | tf_op jit(solution)/shard_map/ppermute | solution.py:40
  72.4 12.3 %collective-permute-start.31 = (bf16[64,512]{1,0:T(8,128)(2,1)S(1)}, bf16[64,512]{1,0:T(8,128)(2,1)S(1)}, u32[]{:S(2)}, u32[]{:S(2)}) collective-permute-start(bf16[64,512]{1,0:T(8,128)(2,1)S(1)} %get-tuple-element.71), channel_id=1, source_target_pairs={{0,1},{1,2},{2,3},{3,0},{4,5},{5,6},{6,7},{7,4},{8,9},{9,10},{10,1... | collective-permute-start | bytes 196616 | tf_op jit(solution)/shard_map/ppermute | solution.py:40
  75.4 9.3 %collective-permute-start.32 = (bf16[64,512]{1,0:T(8,128)(2,1)S(1)}, bf16[64,512]{1,0:T(8,128)(2,1)S(1)}, u32[]{:S(2)}, u32[]{:S(2)}) collective-permute-start(bf16[64,512]{1,0:T(8,128)(2,1)S(1)} %get-tuple-element.72), channel_id=1, source_target_pairs={{0,2},{1,3},{2,0},{3,1},{4,6},{5,7},{6,4},{7,5},{8,10},{9,11},{10,... | collective-permute-start | bytes 196616 | tf_op jit(solution)/shard_map/ppermute | solution.py:40
  78.9 5.8 %collective-permute-start.33 = (bf16[64,512]{1,0:T(8,128)(2,1)S(1)}, bf16[64,512]{1,0:T(8,128)(2,1)S(1)}, u32[]{:S(2)}, u32[]{:S(2)}) collective-permute-start(bf16[64,512]{1,0:T(8,128)(2,1)S(1)} %get-tuple-element.73), channel_id=1, source_target_pairs={{0,3},{1,0},{2,1},{3,2},{4,7},{5,4},{6,5},{7,6},{8,11},{9,8},{10,9... | collective-permute-start | bytes 196616 | tf_op jit(solution)/shard_map/ppermute | solution.py:40
  86.8 4.7 %collective-permute-start.35 = (f32[3,64,64]{2,1,0:T(8,128)S(1)}, f32[3,64,64]{2,1,0:T(8,128)S(1)}, u32[]{:S(2)}, u32[]{:S(2)}) collective-permute-start(f32[3,64,64]{2,1,0:T(8,128)S(1)} %add.211), channel_id=1, source_target_pairs={{0,8},{1,9},{2,10},{3,11},{4,5},{5,6},{6,7},{7,4},{8,0},{9,1},{10,... | collective-permute-start | bytes 147464 | tf_op jit(solution)/shard_map/ppermute | solution.py:77
  88.2 4.6 %collective-permute-start.36 = (f32[3,64,64]{2,1,0:T(8,128)S(1)}, f32[3,64,64]{2,1,0:T(8,128)S(1)}, u32[]{:S(2)}, u32[]{:S(2)}) collective-permute-start(f32[3,64,64]{2,1,0:T(8,128)S(1)} %add.211), channel_id=1, source_target_pairs={{0,16},{1,17},{2,18},{3,19},{4,6},{5,7},{6,4},{7,5},{8,24},{9,25},... | collective-permute-start | bytes 147464 | tf_op jit(solution)/shard_map/ppermute | solution.py:77
  89.0 5.5 %collective-permute-start.37 = (f32[3,64,64]{2,1,0:T(8,128)S(1)}, f32[3,64,64]{2,1,0:T(8,128)S(1)}, u32[]{:S(2)}, u32[]{:S(2)}) collective-permute-start(f32[3,64,64]{2,1,0:T(8,128)S(1)} %add.211), channel_id=1, source_target_pairs={{0,24},{1,25},{2,26},{3,27},{4,7},{5,4},{6,5},{7,6},{8,16},{9,17},... | collective-permute-start | bytes 147464 | tf_op jit(solution)/shard_map/ppermute | solution.py:77
  94.6 6.6 %collective-permute-start.38 = (f32[3,64,64]{2,1,0:T(8,128)S(1)}, f32[3,64,64]{2,1,0:T(8,128)S(1)}, u32[]{:S(2)}, u32[]{:S(2)}) collective-permute-start(f32[3,64,64]{2,1,0:T(8,128)S(1)} %add_add_fusion.3), channel_id=1, source_target_pairs={{0,1},{1,2},{2,3},{3,0},{4,12},{5,13},{6,14},{7,15},{8,9},{9,10},{... | collective-permute-start | bytes 147464 | tf_op jit(solution)/shard_map/ppermute | solution.py:77
  94.6 8.6 %collective-permute-start.39 = (f32[3,64,64]{2,1,0:T(8,128)S(1)}, f32[3,64,64]{2,1,0:T(8,128)S(1)}, u32[]{:S(2)}, u32[]{:S(2)}) collective-permute-start(f32[3,64,64]{2,1,0:T(8,128)S(1)} %add_add_fusion.3), channel_id=1, source_target_pairs={{0,2},{1,3},{2,0},{3,1},{4,20},{5,21},{6,22},{7,23},{8,10},{9,11},... | collective-permute-start | bytes 147464 | tf_op jit(solution)/shard_map/ppermute | solution.py:77
  98.4 5.5 %collective-permute-start.40 = (f32[3,64,64]{2,1,0:T(8,128)S(1)}, f32[3,64,64]{2,1,0:T(8,128)S(1)}, u32[]{:S(2)}, u32[]{:S(2)}) collective-permute-start(f32[3,64,64]{2,1,0:T(8,128)S(1)} %add_add_fusion.3), channel_id=1, source_target_pairs={{0,3},{1,0},{2,1},{3,2},{4,28},{5,29},{6,30},{7,31},{8,11},{9,8},{... | collective-permute-start | bytes 147464 | tf_op jit(solution)/shard_map/ppermute | solution.py:77
  (14 other events, 85.1 us)

commit v3 on v2

v3 whole, which is shorter than its diff:
```python
import functools
import math

import jax
import jax.numpy as jnp
from jax import lax
from jax.experimental import pallas as pl
from jax.experimental.pallas import tpu as pltpu
from jax.sharding import PartitionSpec as P

EMB = 256
K = 64
BR = 128
MAXT = 48
REACH = 2
ITERS = 2

TAU = 6.0
EPS = 1e-06
PRECISE = lax.Precision.HIGHEST

WEIGHT = 1.0 / (BR * MAXT)
SIGMA = math.exp(TAU) * WEIGHT
EXP2 = TAU / EMB * math.log2(math.e)
GROUP = 8
SHARDS = 6
F32 = jnp.float32
BF16 = jnp.bfloat16
VMEM = pl.BlockSpec(memory_space=pltpu.VMEM)
SMEM = pl.BlockSpec(memory_space=pltpu.SMEM)


def swapped(value, axis, bits):
    count = lax.axis_size(axis)
    return lax.ppermute(value, axis, [(i, i ^ bits) for i in range(count)])


def rotated(value, axis, steps):
    count = lax.axis_size(axis)
    return lax.ppermute(value, axis, [(i, (i + steps) % count) for i in range(count)])


def other_side(value):
    count = lax.axis_size("rows")
    chips = count // 2
    pairs = []
    for r in range(count):
        chip, core = divmod(r, 2)
        to = (chip + 1) % chips if chip % 2 else (chip - 1) % chips
        pairs.append((r, to * 2 + core))
    return lax.ppermute(value, "rows", pairs)


def after(value, *others):
    return lax.optimization_barrier((value, *others))[0]


def across(value):
    return swapped(value, "rows", 2), other_side(value), swapped(value, "rows", 1)


def by_core(side_a, side_b):
    return [side_a, swapped(side_a, "rows", 1), side_b, swapped(side_b, "rows", 1)]


def sum_tiles(value):
    return value + sum(rotated(value, "tiles", n) for n in range(1, lax.axis_size("tiles")))


def sum_rows(value):
    rows, bits = lax.axis_size("rows"), 2
    while bits < rows:
        span = min(4, rows // bits)
        value = value + sum(swapped(value, "rows", k * bits) for k in range(1, span))
        bits *= span
    return value


def sum_chips(value, part):
    rows, tiles = lax.axis_size("rows"), lax.axis_size("tiles")
    if rows // 2 != tiles or tiles != 4:
        total = (sum_tiles if part else sum_rows)(value)
        return total, total
    parts = [value]
    for step in range(1, 4):
        pairs = []
        for r in range(rows):
            for t in range(tiles):
                along_rows = r % 2 == part
                to = (r ^ (2 * step), t) if along_rows else (r, (t + step) % tiles)
                pairs.append((r * tiles + t, to[0] * tiles + to[1]))
        parts.append(lax.ppermute(value, ("rows", "tiles"), pairs))
    return sum(parts), parts[1]


def after_list(values, other):
    return [after(values[0], other), *values[1:]]


def dot_t(a, b):
    return lax.dot_general(a, b, (((1,), (1,)), ((), ())), preferred_element_type=F32)


def dot_exact(a, b):
    return lax.dot_general(
        a, b, (((1,), (1,)), ((), ())), precision=PRECISE, preferred_element_type=F32
    )


def unit_of(rows):
    values = rows.astype(F32)
    mean = jnp.sum(values * values, axis=1, keepdims=True) * (1.0 / EMB)
    return (values * lax.rsqrt(mean + EPS)).astype(BF16)


def pack_kernel(meta, emb, block, step, cols, emb_out, vec_out, cols_out, block_buf, step_buf, sems):
    here, width = meta[0], emb_out.shape[0]
    copies = [
        pltpu.make_async_copy(emb.at[pl.ds(here * width, width), :], emb_out, sems.at[0]),
        pltpu.make_async_copy(block, block_buf, sems.at[1]),
        pltpu.make_async_copy(step, step_buf, sems.at[2]),
    ]
    for copy in copies:
        copy.start()
    cols_out[...] = cols[...]
    copies[1].wait()
    vec_out[:K, :] = block_buf[...].astype(BF16)
    copies[2].wait()
    vec_out[K:, :] = step_buf[...].astype(BF16)
    copies[0].wait()


def group_copies(count, first, source, target, sems, body):
    @pl.loop(0, (count + GROUP - 1) // GROUP)
    def _(step):
        at = pl.ds(first + step * GROUP, GROUP)
        body(pltpu.make_async_copy(source.at[at], target.at[at], sems.at[step]))


def build_tiles(blocks, first, items, unit_own, unit_ext, tiles, stored=None, sems=None):
    count = items[items.shape[0] - 1]

    @pl.loop(0, (count + GROUP - 1) // GROUP)
    def _(step):
        picked = [items[step * GROUP + g] for g in range(GROUP)]
        scores = [dot_t(unit_ext[f // blocks], unit_own[f % blocks]) for f in picked]
        for g in range(GROUP):
            tiles[first + step * GROUP + g] = jnp.exp2(scores[g] * EXP2).astype(BF16)
        if stored is not None:
            at = pl.ds(first + step * GROUP, GROUP)
            pltpu.make_async_copy(tiles.at[at], stored.at[at], sems.at[step]).start()


def unit_kernel(emb, unit, buf, sems):
    blocks, parts = unit.shape[0], sems.shape[0]
    each = blocks // parts
    copies = [
        pltpu.make_async_copy(
            emb.at[pl.ds(n * each, each)], buf.at[pl.ds(n * each, each)], sems.at[n]
        )
        for n in range(parts)
    ]
    for copy in copies:
        copy.start()
    for n, copy in enumerate(copies):
        copy.wait()

        @pl.loop(n * each, (n + 1) * each)
        def _(b):
            unit[b] = unit_of(buf[b])


def near_kernel(
    blocks, share, meta, items, unit_own, emb_core, diag_out, stored, unit_ext, tiles, sems
):
    here = meta[0]
    for i in range(share):
        unit_ext[i] = unit_own[here * share + i]
        unit_ext[share + i] = unit_of(emb_core[pl.ds(i * BR, BR), :])
    rows = lax.broadcasted_iota(jnp.int32, (BR, BR), 0)
    cols = lax.broadcasted_iota(jnp.int32, (BR, BR), 1)
    for i in range(share):
        unit = unit_ext[i]
        weights = jnp.exp2(dot_t(unit, unit) * EXP2)
        on_diag = rows == cols
        diag_out[:, pl.ds(i * BR, BR)] = (
            jnp.sum(jnp.where(on_diag, weights, 0.0), axis=0, keepdims=True) * WEIGHT - SIGMA
        )
        tiles[i] = jnp.where(on_diag, 0.0, weights).astype(BF16)
    at = pl.ds(0, share)
    copy = pltpu.make_async_copy(tiles.at[at], stored.at[at], sems.at[sems.shape[0] - 1])
    copy.start()
    build_tiles(blocks, share, items, unit_own, unit_ext, tiles, stored, sems)
    count = items[items.shape[0] - 1]
    group_copies(count, share, tiles, stored, sems, lambda copy: copy.wait())
    copy.wait()


def apply_tiles(blocks, share, devices, here, items, tiles, vec, outs, vec_ext, acc):
    for j, ref in enumerate(vec):
        for i in range(share):
            vec_ext[j * share + i] = ref[:, pl.ds(i * BR, BR)]
    acc[...] = jnp.zeros_like(acc)
    for i in range(share):
        acc[here * share + i] = jnp.dot(vec_ext[i], tiles[0][i], preferred_element_type=F32)
    for part in range(2):
        count, first, base = items[part][items[part].shape[0] - 1], (share, 0)[part], (0, 2 * share)[part]

        @pl.loop(0, (count + GROUP - 1) // GROUP)
        def _(step):
            picked = []
            for g in range(GROUP):
                at = step * GROUP + g
                flat = items[part][at]
                picked.append(
                    (base + flat // blocks, jnp.where(at < count, flat % blocks, blocks))
                )
            parts = [
                jnp.dot(
                    vec_ext[ext],
                    tiles[part][first + step * GROUP + g],
                    preferred_element_type=F32,
                )
                for g, (ext, _) in enumerate(picked)
            ]
            for (_, to), value in zip(picked, parts):
                acc[to] += value

    for n, out in enumerate(outs):
        rows = pl.ds(n // devices * K, K)
        at_block = lax.rem(here + n % devices, devices) * share
        for i in range(share):
            value = acc[at_block + i, rows, :] * WEIGHT
            out[:, pl.ds(i * BR, BR)] = value.astype(out.dtype)


def far_kernel(blocks, share, devices, *refs):
    meta, items, stored, unit_own = refs[0], refs[1:3], refs[3], refs[4]
    emb, vec = refs[5 : 3 + SHARDS], refs[3 + SHARDS : 3 + 2 * SHARDS]
    outs, (near, far, unit_ext, vec_ext, acc, sems) = refs[3 + 2 * SHARDS : -6], refs[-6:]
    count, at = items[0][items[0].shape[0] - 1], pl.ds(0, share)
    copy = pltpu.make_async_copy(stored.at[at], near.at[at], sems.at[sems.shape[0] - 1])
    copy.start()
    group_copies(count, share, stored, near, sems, lambda copy: copy.start())
    for j, ref in enumerate(emb):
        for i in range(share):
            unit_ext[j * share + i] = unit_of(ref[pl.ds(i * BR, BR), :])
    build_tiles(blocks, 0, items[1], unit_own, unit_ext, far)
    copy.wait()
    group_copies(count, share, stored, near, sems, lambda copy: copy.wait())
    apply_tiles(blocks, share, devices, meta[0], items, (near, far), vec, outs, vec_ext, acc)


def apply_kernel(blocks, share, devices, *refs):
    meta, items, tiles = refs[0], refs[1:3], refs[3:5]
    vec, outs, (vec_ext, acc) = refs[5 : 5 + SHARDS], refs[5 + SHARDS : -2], refs[-2:]
    apply_tiles(blocks, share, devices, meta[0], items, tiles, vec, outs, vec_ext, acc)


def summed(parts, diag, vectors):
    value = parts[0][...] + diag[...] * vectors
    for ref in parts[1:]:
        value = value + ref[...].astype(F32)
    return value


def image_kernel(devices, *refs):
    parts, (diag, vec, out, out_half) = refs[:devices], refs[devices:]
    value = summed(parts, diag, vec[...])
    out[...] = value
    out_half[...] = value.astype(BF16)


def mul(a, b):
    return jnp.dot(a, b, precision=PRECISE, preferred_element_type=F32)


def eye_mask(n):
    shape = (n, n)
    return lax.broadcasted_iota(jnp.int32, shape, 0) == lax.broadcasted_iota(jnp.int32, shape, 1)


def as_row(column):
    return jnp.sum(jnp.where(eye_mask(K), column, 0.0), axis=0, keepdims=True)


def step_coefficients(g_vv, g_vs, g_ss, g_jv, g_js, g_jj, rotation, total):
    m_t = g_jv * (1.0 / total) + SIGMA * (g_vv * (1.0 / total) - eye_mask(K).astype(F32))
    resid_sq = (
        jnp.sum(jnp.where(eye_mask(K), g_jj, 0.0), axis=1, keepdims=True)
        - 2.0 * jnp.sum(m_t * g_jv, axis=1, keepdims=True)
        + jnp.sum(m_t * mul(m_t, g_vv), axis=1, keepdims=True)
    )
    resid_inv = 1.0 / jnp.sqrt(jnp.maximum(resid_sq, 0.0) * (1.0 / total) + EPS)
    on_v, on_resid, on_s = rotation[:K].T, rotation[K : 2 * K].T, rotation[2 * K :].T
    p_j = on_resid * as_row(resid_inv)
    p_step = -mul(p_j, m_t)
    coef = jnp.concatenate(
        [
            jnp.concatenate([on_v + p_step, on_s, p_j], axis=1),
            jnp.concatenate([p_step, on_s, p_j], axis=1),
        ],
        axis=0,
    )
    gram = jnp.concatenate(
        [
            jnp.concatenate([g_vv, g_vs, g_jv.T], axis=1),
            jnp.concatenate([g_vs.T, g_ss, g_js.T], axis=1),
            jnp.concatenate([g_jv, g_js, g_jj], axis=1),
        ],
        axis=0,
    )
    on_gram = mul(coef, gram)
    comb_sq = jnp.sum(on_gram[:K] * coef[:K], axis=1, keepdims=True)
    scale = 1.0 / jnp.sqrt(jnp.maximum(comb_sq, 0.0) * (1.0 / total) + EPS)
    return coef, on_gram, jnp.concatenate([scale, scale], axis=0)


def gram_kernel(devices, meta, x_ref, y_ref, j_ref, diag, *refs):
    parts, (rows, keep, send) = refs[:devices], refs[devices:]
    rows[:K, :] = x_ref[...]
    rows[K : 2 * K, :] = y_ref[...]
    rows[2 * K : 3 * K, :] = j_ref[...]
    rows[3 * K :, :] = summed(parts, diag, y_ref[...])
    g = dot_exact(rows[...], rows[...])
    packed = jnp.concatenate(
        [
            g[:K, : 2 * K],
            jnp.concatenate([g[K : 2 * K, K : 2 * K], g[3 * K :, 3 * K :]], axis=1),
            g[: 3 * K, 2 * K :],
        ],
        axis=0,
    )
    half = keep.shape[0]
    keep[...] = jnp.where(meta[1] == 0, packed[:half], packed[half:])
    send[...] = jnp.where(meta[1] == 0, packed[half:], packed[:half])


def first_kernel(total, meta, rot_ref, rows, mine, other, new_out, part_out, coef_out, g_out, l_out):
    packed = jnp.concatenate(
        [
            jnp.where(meta[1] == 0, mine[...], other[...]),
            jnp.where(meta[1] == 0, other[...], mine[...]),
        ],
        axis=0,
    )
    xx, xy = packed[:K, :K], packed[:K, K:]
    yy, tt = packed[K : 2 * K, :K], packed[K : 2 * K, K:]
    xj, xt = packed[2 * K : 3 * K, :K], packed[2 * K : 3 * K, K:]
    yj, yt = packed[3 * K : 4 * K, :K], packed[3 * K : 4 * K, K:]
    jj, jt = packed[4 * K :, :K], packed[4 * K :, K:]

    def inv_rms(square):
        picked = jnp.sum(jnp.where(eye_mask(K), square, 0.0), axis=1, keepdims=True)
        return 1.0 / jnp.sqrt(picked * (1.0 / total) + EPS)

    x_col, y_col = inv_rms(xx), inv_rms(yy)
    x_row, y_row = as_row(x_col), as_row(y_col)
    coef, on_gram, scale = step_coefficients(
        xx * x_col * x_row,
        xy * x_col * y_row,
        yy * y_col * y_row,
        xj.T * x_col * x_row,
        yj.T * x_col * y_row,
        jj * x_col * x_row,
        rot_ref[...],
        total,
    )
    coef = scale * coef
    g_out[...] = dot_exact(scale * on_gram, coef)
    coef = coef * jnp.concatenate([x_row, y_row, x_row], axis=1)
    coef_out[...] = coef
    new_out[...] = mul(coef, rows[: 3 * K, :])
    known = coef[:K, : 2 * K]
    part_out[...] = mul(known, rows[2 * K :, :])
    j_t = jnp.concatenate(
        [
            jnp.concatenate([xj.T, yj.T, jj, jt], axis=1),
            jnp.concatenate([xt.T, yt.T, jt.T, tt], axis=1),
        ],
        axis=0,
    )
    l_out[...] = mul(known, j_t)


def twice_kernel(devices, rows, diag, *refs):
    parts, (q_out, out) = refs[:devices], refs[devices:]
    q = summed(parts, diag, rows[2 * K : 3 * K, :])
    q_out[...] = q
    g = dot_exact(q, rows[...])
    out[:K, :] = g[:, : 2 * K]
    out[K : 2 * K, :] = g[:, 2 * K :]
    qq = dot_exact(q, q)
    out[2 * K :, :K] = qq[: K // 2]
    out[2 * K :, K:] = qq[K // 2 :]


def image_again_kernel(part, coef, q, out):
    out[...] = part[...] + mul(coef[:K, 2 * K :], q[...])


def last_kernel(total, rot_ref, new, j_ref, coef_ref, g_ref, l_ref, h_ref, v_out, s_out):
    coef, gram = coef_ref[...], g_ref[...]
    q_xy, q_jt = h_ref[:K, :], h_ref[K : 2 * K, :]
    qq = jnp.concatenate([h_ref[2 * K :, :K], h_ref[2 * K :, K:]], axis=0)
    q_all = jnp.concatenate([q_xy, q_jt, qq], axis=1)
    image = mul(coef[:K, 2 * K :], q_all)
    on_rows = l_ref[...] + image[:, : 4 * K]
    on_q = dot_exact(coef[:K, : 2 * K], q_jt) + image[:, 4 * K :]
    j_new = dot_exact(on_rows[:, : 3 * K], coef)
    g_jj = dot_exact(jnp.concatenate([on_rows[:, 2 * K :], on_q], axis=1), coef[:K])
    coef, _, scale = step_coefficients(
        gram[:K, :K],
        gram[:K, K:],
        gram[K:, K:],
        j_new[:, :K],
        j_new[:, K:],
        g_jj,
        rot_ref[...],
        total,
    )
    both = scale * mul(coef, jnp.concatenate([new[...], j_ref[...]], axis=0))
    v_out[...], s_out[...] = both[:K], both[K:]


def call(kernel, outs, *args, smem=0, hbm=0, scratch=(), us=0.0):
    any_memory = pl.BlockSpec(memory_space=pl.ANY)
    args = [
        pltpu.with_memory_space_constraint(arg, pltpu.HBM) if smem <= n < smem + hbm else arg
        for n, arg in enumerate(args)
    ]
    return pl.pallas_call(
        kernel,
        out_shape=tuple(
            pltpu.HBM(*out[:2]) if len(out) > 2 else jax.ShapeDtypeStruct(*out) for out in outs
        ),
        in_specs=[SMEM] * smem + [any_memory] * hbm + [VMEM] * (len(args) - smem - hbm),
        out_specs=tuple(any_memory if len(out) > 2 else VMEM for out in outs),
        scratch_shapes=list(scratch),
        compiler_params=pltpu.CompilerParams(vmem_limit_bytes=16 * 1024 * 1024),
        cost_estimate=pl.CostEstimate(
            flops=int(us * 1e9), bytes_accessed=0, transcendentals=0
        ),
    )(*args)


def tile_list(cols, counts, here, row, share, devices):
    blocks, span = cols.shape[0], cols.shape[1] // devices
    slot = jnp.concatenate(
        [
            (here ^ n) * span + lax.broadcasted_iota(jnp.int32, (blocks, span), 1)
            for n in range(devices)
        ],
        axis=1,
    )
    col = cols
    block = row * blocks + lax.broadcasted_iota(jnp.int32, col.shape, 0)
    shard, inner = col // blocks, col % blocks
    other_core = (shard % 2 != row % 2).astype(jnp.int32)
    chip, own_chip = shard // 2, row // 2
    place = other_core + jnp.where(chip == own_chip, 0, jnp.where(chip == own_chip ^ 1, 2, 4))
    mine = (slot < counts[:, None]) & (inner // share == here) & (col != block)
    ext = jnp.where(mine, place * share + inner % share, -1)
    wanted = lax.broadcasted_iota(jnp.int32, (SHARDS * share, blocks, 1), 0)
    mask = jnp.any(ext[None] == wanted, axis=2).astype(F32)
    lists = []
    for part in (mask[: 2 * share], mask[2 * share :]):
        flat = part.size
        part = part.reshape(flat)
        index = jnp.arange(flat, dtype=jnp.int32)
        upto = (index[:, None] <= index[None, :]).astype(F32)
        place = jnp.dot(part, upto).astype(jnp.int32)
        wide = jnp.arange(flat + GROUP + 1, dtype=jnp.int32)[None, :]
        used = part[:, None] > 0
        hit = (place[:, None] == wide + 1) & used
        last = (wide == flat + GROUP) & used
        lists.append(jnp.sum(jnp.where(hit, index[:, None], last.astype(jnp.int32)), axis=0))
    return lists


def local(embedding, start_block, start_step, rotations, neighbour_cols, tile_counts):
    devices = lax.axis_size("tiles")
    width = start_block.shape[1]
    share = width // BR
    blocks = tile_counts.shape[0]
    total = width * devices * lax.axis_size("rows")
    here, row = lax.axis_index("tiles"), lax.axis_index("rows")

    meta = jnp.stack([here, row % 2])
    own_emb, own_vec, cols = call(
        pack_kernel,
        [((width, EMB), BF16), ((2 * K, width), BF16), (neighbour_cols.shape, jnp.int32)],
        meta,
        embedding,
        start_block,
        start_step,
        neighbour_cols,
        smem=1,
        hbm=3,
        scratch=[
            pltpu.VMEM((K, width), F32),
            pltpu.VMEM((K, width), F32),
            pltpu.SemaphoreType.DMA((3,)),
        ],
        us=1.0,
    )
    emb_a, emb_b, emb_core = across(own_emb)
    lists = after(cols, emb_core)
    bits = 1
    while bits < devices:
        lists = jnp.concatenate([lists, swapped(lists, "tiles", bits)], axis=1)
        bits *= 2
    items = tile_list(lists, tile_counts, here, row, share, devices)
    own_vec = after(own_vec, emb_core)
    vec_a, vec_b, vec_core = across(own_vec)
    (unit_own,) = call(
        unit_kernel,
        [((blocks, BR, EMB), BF16)],
        after(embedding.reshape(blocks, BR, EMB), emb_core),
        hbm=1,
        scratch=[pltpu.VMEM((blocks, BR, EMB), BF16), pltpu.SemaphoreType.DMA((4,))],
        us=2.6,
    )
    near, far = 2 * share * blocks, (SHARDS - 2) * share * blocks
    near_shape, far_shape = (share + near + GROUP, BR, BR), (far + GROUP, BR, BR)
    near_sems = pltpu.SemaphoreType.DMA((near // GROUP + 2,))
    diag, tiles_near = call(
        functools.partial(near_kernel, blocks, share),
        [((1, width), F32), (near_shape, BF16, "hbm")],
        meta,
        items[0],
        unit_own,
        emb_core,
        smem=2,
        scratch=[
            pltpu.VMEM((2 * share, BR, EMB), BF16),
            pltpu.VMEM(near_shape, BF16),
            near_sems,
        ],
        us=2.0,
    )
    emb_a, emb_b, vec_a, vec_b = (after(side, diag) for side in (emb_a, emb_b, vec_a, vec_b))
    parts = call(
        functools.partial(far_kernel, blocks, share, devices),
        ([((K, width), F32)] + [((K, width), BF16)] * (devices - 1)) * 2
        + [(near_shape, BF16), (far_shape, BF16)],
        meta,
        *items,
        tiles_near,
        unit_own,
        *by_core(emb_a, emb_b),
        own_vec,
        vec_core,
        *by_core(vec_a, vec_b),
        smem=3,
        hbm=1,
        scratch=[
            pltpu.VMEM(((SHARDS - 2) * share, BR, EMB), BF16),
            pltpu.VMEM((SHARDS * share, 2 * K, BR), BF16),
            pltpu.VMEM((blocks + 1, 2 * K, BR), F32),
            near_sems,
        ],
        us=5.0,
    )
    parts, tiles_near, tiles_far = parts[:-2], parts[-2], parts[-1]

    def applied(halo):
        return call(
            functools.partial(apply_kernel, blocks, share, devices),
            [((K, width), F32)] + [((K, width), BF16)] * (devices - 1),
            meta,
            *items,
            tiles_near,
            tiles_far,
            *halo,
            smem=3,
            scratch=[
                pltpu.VMEM((SHARDS * share, K, BR), BF16),
                pltpu.VMEM((blocks + 1, K, BR), F32),
            ],
            us=3.0,
        )

    def gathered(parts):
        return [parts[0]] + [rotated(part, "tiles", n + 1) for n, part in enumerate(parts[1:])]

    parts, step_parts = gathered(parts[:devices]), gathered(parts[devices:])
    image, image_half = call(
        functools.partial(image_kernel, devices),
        [((K, width), F32), ((K, width), BF16)],
        *after_list(parts, step_parts[1]),
        diag,
        start_block,
        us=0.1,
    )
    image_a, image_b, image_core = across(image_half)
    half = 5 * K // 2
    rows, keep, send = call(
        functools.partial(gram_kernel, devices),
        [((4 * K, width), F32)] + [((half, 2 * K), F32)] * 2,
        meta,
        start_block,
        start_step,
        after(image, image_core),
        diag,
        *step_parts,
        smem=1,
        us=1.0,
    )
    image_vec = [image_half, image_core, *by_core(after(image_a, keep), after(image_b, keep))]
    gram = keep + swapped(send, "rows", 1)
    parts = gathered(applied(image_vec))
    gram = sum_rows(after(gram, parts[1]))
    twice, products = call(
        functools.partial(twice_kernel, devices),
        [((K, width), F32), ((half, 2 * K), F32)],
        rows,
        diag,
        *parts,
        us=0.8,
    )
    products = products + swapped(products, "rows", 1)
    gram = sum_tiles(after(gram, products))
    products, _ = sum_chips(products, 0)
    products, _ = sum_chips(products, 1)
    new, part, coef, gram, known = call(
        functools.partial(first_kernel, total),
        [
            ((2 * K, width), F32),
            ((K, width), F32),
            ((2 * K, 3 * K), F32),
            ((2 * K, 2 * K), F32),
            ((K, 4 * K), F32),
        ],
        meta,
        rotations[0],
        rows,
        gram,
        swapped(gram, "rows", 1),
        smem=1,
        us=0.0,
    )
    (image,) = call(image_again_kernel, [((K, width), F32)], part, coef, twice, us=0.0)
    return call(
        functools.partial(last_kernel, total),
        [((K, width), F32)] * 2,
        rotations[1],
        new,
        image,
        coef,
        gram,
        known,
        products,
        us=2.5,
    )


def solution(mesh):
    return jax.shard_map(
        local,
        mesh=mesh,
        in_specs=(
            P("rows", None),
            P(None, ("rows", "tiles")),
            P(None, ("rows", "tiles")),
            P(),
            P("rows", "tiles"),
            P("rows"),
        ),
        out_specs=(P(None, ("rows", "tiles")), P(None, ("rows", "tiles"))),
        check_vma=False,
    )
```

time: 107 us -> 90.3 us (0.84)
  waiting for transfers between devices: 28.2 us -> 16.6 us
  starting transfers between devices: 48.9 us -> 44 us
  Pallas kernels: 25.7 us -> 24.5 us
    ppermute x12 -> x6, waiting for transfers between devices: 17.1 us -> 0.25 us  [sum_chips(): parts.append(lax.ppermute(value, ('rows', 'tiles'), pairs))]
    ppermute x14 -> x20, starting transfers between devices: 3.64 us -> 12.1 us  [swapped(): return lax.ppermute(value, axis, [(i, i ^ bits) for i in range(count)])]
    ppermute x12 -> x6, starting transfers between devices: 14.8 us -> 7.46 us  [sum_chips(): parts.append(lax.ppermute(value, ('rows', 'tiles'), pairs))]
    ppermute x12, starting transfers between devices: 22.7 us -> 18.3 us  [rotated(): lax.ppermute(value, axis, [(i, (i + steps) % count) for i in range(count)])]
    ppermute x12, waiting for transfers between devices: 4.88 us -> 9.08 us  [rotated(): lax.ppermute(value, axis, [(i, (i + steps) % count) for i in range(count)])]
    ppermute x3, starting transfers between devices: 7.75 us -> 6.15 us  [other_side(): return lax.ppermute(value, 'rows', pairs)]
    pallas_call x11, Pallas kernels: 25.7 us -> 24.5 us  [call(): pl.pallas_call(kernel, out_shape=tuple((pltpu.HBM(*out[:2]) if len(out) >...]
    ppermute x14 -> x20, waiting for transfers between devices: 4.39 us -> 5.57 us  [swapped(): return lax.ppermute(value, axis, [(i, i ^ bits) for i in range(count)])]
where the time goes in v3:
time: 90.3 us; the launch traced here: 89.2 us
  starting transfers between devices  44 us (49%)
  Pallas kernels  24.5 us (27%)
  waiting for transfers between devices  16.6 us (18%)
  other arithmetic  1.47 us (2%)
  local copies, waits for them, and re-layouts  1.27 us (1%)
  between operations  1.01 us (1%)
    pallas_call x11, Pallas kernels, call(): pl.pallas_call(kernel, out_shape=tuple((pltpu.HBM(*out[:2]) if len(out) >...  24.5 us
    ppermute x12, starting transfers between devices, rotated(): lax.ppermute(value, axis, [(i, (i + steps) % count) for i in range(count)])  18.3 us
    ppermute x20, starting transfers between devices, swapped(): return lax.ppermute(value, axis, [(i, i ^ bits) for i in range(count)])  12.1 us
    ppermute x12, waiting for transfers between devices, rotated(): lax.ppermute(value, axis, [(i, (i + steps) % count) for i in range(count)])  9.08 us
    ppermute x6, starting transfers between devices, sum_chips(): parts.append(lax.ppermute(value, ('rows', 'tiles'), pairs))  7.46 us
    ppermute x3, starting transfers between devices, other_side(): return lax.ppermute(value, 'rows', pairs)  6.15 us
    ppermute x20, waiting for transfers between devices, swapped(): return lax.ppermute(value, axis, [(i, i ^ bits) for i in range(count)])  5.57 us
  transfers between devices with their start and end apart: 41, of which 18 were waited for; matrix products, arithmetic and copies ran while one was open for 2% of the time, Pallas kernels for 16%

profile of v3, /device:TPU:0, one launch (start us, length us, event | category | flops | bytes accessed | tf_op | source)
XLA Modules:
  0.0 89.2 jit_solution(17277037943784141515)
XLA Ops:
  1.4 1.6 %shard_map.77 = (bf16[512,256]{1,0:T(8,128)(2,1)S(1)}, bf16[128,512]{1,0:T(8,128)(2,1)S(1)}, s32[16,12]{1,0:T(8,128)S(1)}) custom-call(s32[2]{0:T(128)S(1)} %pad_add_fusion.2.meta.refs_0_, bf16[2048,256]{1,0:T(8,128)(2,1)} %emb.1, f32[64,512]{1,0:T(8,128)} %x_ref.1, f32[64,512]{1,0:T(8,128)} %y_ref.1, s32[16,12]{1,0:T(8,128)S(1)} %copy-done.2), custom_call_target="tpu_custom_call" | custom-call | flops 1000000000 | tf_op jit(solution)/shard_map/pallas_call | solution.py:432
  3.6 3.5 %collective-permute-start.5 = (bf16[512,256]{1,0:T(8,128)(2,1)S(1)}, bf16[512,256]{1,0:T(8,128)(2,1)S(1)}, u32[]{:S(2)}, u32[]{:S(2)}) collective-permute-start(bf16[512,256]{1,0:T(8,128)(2,1)S(1)} %get-tuple-element.47), channel_id=1, source_target_pairs={{0,24},{4,28},{8,16},{12,20},{16,8},{20,12},{24,0},{28,4},{1,25},{... | collective-permute-start | bytes 786440 | tf_op jit(solution)/shard_map/ppermute | solution.py:51
  7.8 1.6 %collective-permute-start.1 = (s32[16,12]{1,0:T(8,128)S(1)}, s32[16,12]{1,0:T(8,128)S(1)}, u32[]{:S(2)}, u32[]{:S(2)}) collective-permute-start(s32[16,12]{1,0:T(8,128)S(1)} %get-tuple-element.48), channel_id=1, source_target_pairs={{0,1},{1,0},{2,3},{3,2},{4,5},{5,4},{6,7},{7,6},{8,9},{9,8},{10,11... | collective-permute-start | bytes 2312 | tf_op jit(solution)/shard_map/ppermute | solution.py:35
  9.4 1.4 %collective-permute-start.10 = (bf16[128,512]{1,0:T(8,128)(2,1)S(1)}, bf16[128,512]{1,0:T(8,128)(2,1)S(1)}, u32[]{:S(2)}, u32[]{:S(2)}) collective-permute-start(bf16[128,512]{1,0:T(8,128)(2,1)S(1)} %get-tuple-element.55.refs_9_), channel_id=1, source_target_pairs={{0,24},{4,28},{8,16},{12,20},{16,8},{20,12},{24,0},{28,4},{1,25},{... | collective-permute-start | bytes 393224 | tf_op jit(solution)/shard_map/ppermute | solution.py:51
  11.6 2.6 %collective-permute-start.2 = (s32[16,24]{1,0:T(8,128)S(1)}, s32[16,24]{1,0:T(8,128)S(1)}, u32[]{:S(2)}, u32[]{:S(2)}) collective-permute-start(s32[16,24]{1,0:T(8,128)S(1)} %pad_add_fusion), channel_id=1, source_target_pairs={{0,2},{1,3},{2,0},{3,1},{4,6},{5,7},{6,4},{7,5},{8,10},{9,11},{10,... | collective-permute-start | bytes 4616 | tf_op jit(solution)/shard_map/ppermute | solution.py:35
  14.2 2.7 %shard_map.78.unit_own.refs_4_ = bf16[16,128,256]{2,1,0:T(8,128)(2,1)S(1)} custom-call(bf16[16,128,256]{2,1,0:T(8,128)(2,1)} %bitcast.15), custom_call_target="tpu_custom_call" | custom-call | flops 2600000000 | tf_op jit(solution)/shard_map/pallas_call | solution.py:432
  18.1 4.2 %shard_map.79 = (f32[1,512]{1,0:T(1,128)S(1)}, bf16[140,128,128]{2,1,0:T(8,128)(2,1)}) custom-call(s32[2]{0:T(128)S(1)} %pad_add_fusion.2.meta.refs_0_, s32[137]{0:T(256)S(1)} %select_reduce_fusion.1.items.refs_1_, bf16[16,128,256]{2,1,0:T(8,128)(2,1)S(1)} %shard_map.78.unit_own.refs_4_, bf16[512,256]{1,0:T(8,128)(2,1)S(1)} %collective-permute-done.emb_core), custom_call_target="tpu_custom_call" | custom-call | flops 2000000000 | tf_op jit(solution)/shard_map/pallas_call | solution.py:432
  23.2 2.3 %collective-permute-done.8.refs_11_ = bf16[128,512]{1,0:T(8,128)(2,1)S(1)} collective-permute-done((bf16[128,512]{1,0:T(8,128)(2,1)S(1)}, bf16[128,512]{1,0:T(8,128)(2,1)S(1)}, u32[]{:S(2)}, u32[]{:S(2)}) %collective-permute-start.8) | collective-permute-done | bytes 131104 | tf_op jit(solution)/shard_map/ppermute | solution.py:35
  26.9 5.8 %shard_map.80 = (f32[64,512]{1,0:T(8,128)S(1)}, bf16[64,512]{1,0:T(8,128)(2,1)S(1)}, bf16[64,512]{1,0:T(8,128)(2,1)S(1)}, bf16[64,512]{1,0:T(8,128)(2,1)S(1)}, f...) custom-call(s32[2]{0:T(128)S(1)} %pad_add_fusion.2.meta.refs_0_, ...), custom_call_target="tpu_custom_call" | custom-call | flops 5000000000 | tf_op jit(solution)/shard_map/pallas_call | solution.py:432
  33.6 1.3 %collective-permute-start.13 = (bf16[64,512]{1,0:T(8,128)(2,1)S(1)}, bf16[64,512]{1,0:T(8,128)(2,1)S(1)}, u32[]{:S(2)}, u32[]{:S(2)}) collective-permute-start(bf16[64,512]{1,0:T(8,128)(2,1)S(1)} %get-tuple-element.61), channel_id=1, source_target_pairs={{0,1},{1,2},{2,3},{3,0},{4,5},{5,6},{6,7},{7,4},{8,9},{9,10},{10,1... | collective-permute-start | bytes 196616 | tf_op jit(solution)/shard_map/ppermute | solution.py:40
  35.0 2.1 %collective-permute-start.14 = (bf16[64,512]{1,0:T(8,128)(2,1)S(1)}, bf16[64,512]{1,0:T(8,128)(2,1)S(1)}, u32[]{:S(2)}, u32[]{:S(2)}) collective-permute-start(bf16[64,512]{1,0:T(8,128)(2,1)S(1)} %get-tuple-element.62), channel_id=1, source_target_pairs={{0,2},{1,3},{2,0},{3,1},{4,6},{5,7},{6,4},{7,5},{8,10},{9,11},{10,... | collective-permute-start | bytes 196616 | tf_op jit(solution)/shard_map/ppermute | solution.py:40
  37.1 1.8 %collective-permute-start.15 = (bf16[64,512]{1,0:T(8,128)(2,1)S(1)}, bf16[64,512]{1,0:T(8,128)(2,1)S(1)}, u32[]{:S(2)}, u32[]{:S(2)}) collective-permute-start(bf16[64,512]{1,0:T(8,128)(2,1)S(1)} %get-tuple-element.63), channel_id=1, source_target_pairs={{0,3},{1,0},{2,1},{3,2},{4,7},{5,4},{6,5},{7,6},{8,11},{9,8},{10,9... | collective-permute-start | bytes 196616 | tf_op jit(solution)/shard_map/ppermute | solution.py:40
  39.0 1.4 %collective-permute-done.13.refs_1_ = bf16[64,512]{1,0:T(8,128)(2,1)S(1)} collective-permute-done((bf16[64,512]{1,0:T(8,128)(2,1)S(1)}, bf16[64,512]{1,0:T(8,128)(2,1)S(1)}, u32[]{:S(2)}, u32[]{:S(2)}) %collective-permute-start.13) | collective-permute-done | bytes 65568 | tf_op jit(solution)/shard_map/ppermute | solution.py:40
  40.4 1.9 %collective-permute-done.14.refs_2_ = bf16[64,512]{1,0:T(8,128)(2,1)S(1)} collective-permute-done((bf16[64,512]{1,0:T(8,128)(2,1)S(1)}, bf16[64,512]{1,0:T(8,128)(2,1)S(1)}, u32[]{:S(2)}, u32[]{:S(2)}) %collective-permute-start.14) | collective-permute-done | bytes 65568 | tf_op jit(solution)/shard_map/ppermute | solution.py:40
  43.3 3.4 %collective-permute-start.18 = (bf16[64,512]{1,0:T(8,128)(2,1)S(1)}, bf16[64,512]{1,0:T(8,128)(2,1)S(1)}, u32[]{:S(2)}, u32[]{:S(2)}) collective-permute-start(bf16[64,512]{1,0:T(8,128)(2,1)S(1)} %get-tuple-element.69), channel_id=1, source_target_pairs={{0,3},{1,0},{2,1},{3,2},{4,7},{5,4},{6,5},{7,6},{8,11},{9,8},{10,9... | collective-permute-start | bytes 196616 | tf_op jit(solution)/shard_map/ppermute | solution.py:40
  46.7 1.2 %collective-permute-start.22 = (bf16[64,512]{1,0:T(8,128)(2,1)S(1)}, bf16[64,512]{1,0:T(8,128)(2,1)S(1)}, u32[]{:S(2)}, u32[]{:S(2)}) collective-permute-start(bf16[64,512]{1,0:T(8,128)(2,1)S(1)} %get-tuple-element.65.refs_5_), channel_id=1, source_target_pairs={{0,24},{4,28},{8,16},{12,20},{16,8},{20,12},{24,0},{28,4},{1,25},{... | collective-permute-start | bytes 196616 | tf_op jit(solution)/shard_map/ppermute | solution.py:51
  47.9 1.2 %collective-permute-start.20 = (bf16[64,512]{1,0:T(8,128)(2,1)S(1)}, bf16[64,512]{1,0:T(8,128)(2,1)S(1)}, u32[]{:S(2)}, u32[]{:S(2)}) collective-permute-start(bf16[64,512]{1,0:T(8,128)(2,1)S(1)} %get-tuple-element.65.refs_5_), channel_id=1, source_target_pairs={{0,8},{4,12},{8,0},{12,4},{16,24},{20,28},{24,16},{28,20},{1,9},{5... | collective-permute-start | bytes 196616 | tf_op jit(solution)/shard_map/ppermute | solution.py:35
  49.3 1.2 %shard_map.82 = (f32[256,512]{1,0:T(8,128)S(1)}, f32[160,128]{1,0:T(8,128)S(1)}, f32[160,128]{1,0:T(8,128)S(1)}) custom-call(s32[2]{0:T(128)S(1)} %pad_add_fusion.2.meta.refs_0_, f32[64,512]{1,0:T(8,128)S(1)} %copy-done, f32[64,512]{1,0:T(8,128)S(1)} %copy-done.1, f32[64,512]{1,0:T(8,128)S(1)} %get-tuple-element.66.j_ref, ...), custom_call_target="tpu_custom_call" | custom-call | flops 1000000000 | tf_op jit(solution)/shard_map/pallas_call | solution.py:432
  50.5 1.7 %collective-permute-done.22.refs_9_ = bf16[64,512]{1,0:T(8,128)(2,1)S(1)} collective-permute-done((bf16[64,512]{1,0:T(8,128)(2,1)S(1)}, bf16[64,512]{1,0:T(8,128)(2,1)S(1)}, u32[]{:S(2)}, u32[]{:S(2)}) %collective-permute-start.22) | collective-permute-done | bytes 65568 | tf_op jit(solution)/shard_map/ppermute | solution.py:51
  53.6 3.4 %shard_map.83 = (f32[64,512]{1,0:T(8,128)S(1)}, bf16[64,512]{1,0:T(8,128)(2,1)S(1)}, bf16[64,512]{1,0:T(8,128)(2,1)S(1)}, bf16[64,512]{1,0:T(8,128)(2,1)S(1)}) custom-call(s32[2]{0:T(128)S(1)} %pad_add_fusion.2.meta.refs_0_, s32[137]{0:T(256)S(1)} %select_reduce_fusion.1.items.refs_1_, s32[265]{0:T(512)S(1)} %select_reduce_fusion.refs_2_, ...), custom_call_target="tpu_custom_call" | custom-call | flops 3000000000 | tf_op jit(solution)/shard_map/pallas_call | solution.py:432
  57.1 1.8 %collective-permute-start.28 = (bf16[64,512]{1,0:T(8,128)(2,1)S(1)}, bf16[64,512]{1,0:T(8,128)(2,1)S(1)}, u32[]{:S(2)}, u32[]{:S(2)}) collective-permute-start(bf16[64,512]{1,0:T(8,128)(2,1)S(1)} %get-tuple-element.80), channel_id=1, source_target_pairs={{0,2},{1,3},{2,0},{3,1},{4,6},{5,7},{6,4},{7,5},{8,10},{9,11},{10,... | collective-permute-start | bytes 196616 | tf_op jit(solution)/shard_map/ppermute | solution.py:40
  58.9 2.0 %collective-permute-start.29 = (bf16[64,512]{1,0:T(8,128)(2,1)S(1)}, bf16[64,512]{1,0:T(8,128)(2,1)S(1)}, u32[]{:S(2)}, u32[]{:S(2)}) collective-permute-start(bf16[64,512]{1,0:T(8,128)(2,1)S(1)} %get-tuple-element.81), channel_id=1, source_target_pairs={{0,3},{1,0},{2,1},{3,2},{4,7},{5,4},{6,5},{7,6},{8,11},{9,8},{10,9... | collective-permute-start | bytes 196616 | tf_op jit(solution)/shard_map/ppermute | solution.py:40
  60.9 3.0 %collective-permute-done.24.refs_1_ = bf16[64,512]{1,0:T(8,128)(2,1)S(1)} collective-permute-done((bf16[64,512]{1,0:T(8,128)(2,1)S(1)}, bf16[64,512]{1,0:T(8,128)(2,1)S(1)}, u32[]{:S(2)}, u32[]{:S(2)}) %collective-permute-start.24) | collective-permute-done | bytes 65568 | tf_op jit(solution)/shard_map/ppermute | solution.py:40
  63.9 1.4 %collective-permute-done.28.refs_2_ = bf16[64,512]{1,0:T(8,128)(2,1)S(1)} collective-permute-done((bf16[64,512]{1,0:T(8,128)(2,1)S(1)}, bf16[64,512]{1,0:T(8,128)(2,1)S(1)}, u32[]{:S(2)}, u32[]{:S(2)}) %collective-permute-start.28) | collective-permute-done | bytes 65568 | tf_op jit(solution)/shard_map/ppermute | solution.py:40
  67.6 2.1 %collective-permute-start.27 = (f32[160,128]{1,0:T(8,128)S(1)}, f32[160,128]{1,0:T(8,128)S(1)}, u32[]{:S(2)}, u32[]{:S(2)}) collective-permute-start(f32[160,128]{1,0:T(8,128)S(1)} %add.180), channel_id=1, source_target_pairs={{0,24},{4,28},{8,16},{12,20},{16,8},{20,12},{24,0},{28,4},{1,25},{... | collective-permute-start | bytes 245768 | tf_op jit(solution)/shard_map/ppermute | solution.py:35
  71.5 1.8 %collective-permute-start.37 = (f32[160,128]{1,0:T(8,128)S(1)}, f32[160,128]{1,0:T(8,128)S(1)}, u32[]{:S(2)}, u32[]{:S(2)}) collective-permute-start(f32[160,128]{1,0:T(8,128)S(1)} %add.184), channel_id=1, source_target_pairs={{0,24},{1,25},{2,26},{3,27},{4,7},{5,4},{6,5},{7,6},{8,16},{9,17},... | collective-permute-start | bytes 245768 | tf_op jit(solution)/shard_map/ppermute | solution.py:92
  73.4 1.5 %collective-permute-start.31 = (f32[160,128]{1,0:T(8,128)S(1)}, f32[160,128]{1,0:T(8,128)S(1)}, u32[]{:S(2)}, u32[]{:S(2)}) collective-permute-start(f32[160,128]{1,0:T(8,128)S(1)} %add_add_fusion.3), channel_id=1, source_target_pairs={{0,1},{1,2},{2,3},{3,0},{4,5},{5,6},{6,7},{7,4},{8,9},{9,10},{10,1... | collective-permute-start | bytes 245768 | tf_op jit(solution)/shard_map/ppermute | solution.py:40
  74.9 1.4 %collective-permute-start.32 = (f32[160,128]{1,0:T(8,128)S(1)}, f32[160,128]{1,0:T(8,128)S(1)}, u32[]{:S(2)}, u32[]{:S(2)}) collective-permute-start(f32[160,128]{1,0:T(8,128)S(1)} %add_add_fusion.3), channel_id=1, source_target_pairs={{0,2},{1,3},{2,0},{3,1},{4,6},{5,7},{6,4},{7,5},{8,10},{9,11},{10,... | collective-permute-start | bytes 245768 | tf_op jit(solution)/shard_map/ppermute | solution.py:40
  78.4 1.6 %collective-permute-start.39 = (f32[160,128]{1,0:T(8,128)S(1)}, f32[160,128]{1,0:T(8,128)S(1)}, u32[]{:S(2)}, u32[]{:S(2)}) collective-permute-start(f32[160,128]{1,0:T(8,128)S(1)} %add_add_fusion.1), channel_id=1, source_target_pairs={{0,2},{1,3},{2,0},{3,1},{4,20},{5,21},{6,22},{7,23},{8,10},{9,11},... | collective-permute-start | bytes 245768 | tf_op jit(solution)/shard_map/ppermute | solution.py:92
  80.7 1.6 %collective-permute-start.40 = (f32[160,128]{1,0:T(8,128)S(1)}, f32[160,128]{1,0:T(8,128)S(1)}, u32[]{:S(2)}, u32[]{:S(2)}) collective-permute-start(f32[160,128]{1,0:T(8,128)S(1)} %add_add_fusion.1), channel_id=1, source_target_pairs={{0,3},{1,0},{2,1},{3,2},{4,28},{5,29},{6,30},{7,31},{8,11},{9,8},{... | collective-permute-start | bytes 245768 | tf_op jit(solution)/shard_map/ppermute | solution.py:92
  84.1 2.4 %shard_map.85 = (f32[128,512]{1,0:T(8,128)S(1)}, f32[64,512]{1,0:T(8,128)S(1)}, f32[128,192]{1,0:T(8,128)S(1)}, f32[128,128]{1,0:T(8,128)S(1)}, f32[64,256]{1,0:T(8,128)S(1)}) custom-call(s32[2]{0:T(128)S(1)} %pad_add_fusion.2.meta.refs_0_, f32[192,64]{1,0:T(8,128)S(1)} %bitcast.12, f32[256,512]{1,0:T(8,128)S(1)} %get-tuple-element.70.rows, ...), custom_call_target="tpu_custom_call" | custom-call | tf_op jit(solution)/shard_map/pallas_call | solution.py:432
  87.1 2.1 %shard_map.87 = (f32[64,512]{1,0:T(8,128)}, f32[64,512]{1,0:T(8,128)}) custom-call(f32[192,64]{1,0:T(8,128)S(1)} %bitcast.13, f32[128,512]{1,0:T(8,128)S(1)} %get-tuple-element.84.new, f32[64,512]{1,0:T(8,128)S(1)} %shard_map.86.j_ref, f32[128,192]{1,0:T(8,128)S(1)} %get-tuple-element.86.coef.coef_ref, f32[128,128]{1,0:T(8,128)S(1)} %get-tuple-element.88.g_ref, ...), custom_call_target="tpu_custom_call" | custom-call | flops 2500000000 | tf_op jit(solution)/shard_map/pallas_call | solution.py:432
  (106 shorter events, 18.9 us)
Async XLA Ops:
  3.0 4.7 %collective-permute-start = (bf16[512,256]{1,0:T(8,128)(2,1)S(1)}, bf16[512,256]{1,0:T(8,128)(2,1)S(1)}, u32[]{:S(2)}, u32[]{:S(2)}) collective-permute-start(bf16[512,256]{1,0:T(8,128)(2,1)S(1)} %get-tuple-element.47), channel_id=1, source_target_pairs={{0,4},{4,0},{8,12},{12,8},{16,20},{20,16},{24,28},{28,24},{1,5},{5... | collective-permute-start | bytes 786440 | tf_op jit(solution)/shard_map/ppermute | solution.py:35
  3.6 18.8 %collective-permute-start.5 = (bf16[512,256]{1,0:T(8,128)(2,1)S(1)}, bf16[512,256]{1,0:T(8,128)(2,1)S(1)}, u32[]{:S(2)}, u32[]{:S(2)}) collective-permute-start(bf16[512,256]{1,0:T(8,128)(2,1)S(1)} %get-tuple-element.47), channel_id=1, source_target_pairs={{0,24},{4,28},{8,16},{12,20},{16,8},{20,12},{24,0},{28,4},{1,25},{... | collective-permute-start | bytes 786440 | tf_op jit(solution)/shard_map/ppermute | solution.py:51
  7.1 15.3 %collective-permute-start.3 = (bf16[512,256]{1,0:T(8,128)(2,1)S(1)}, bf16[512,256]{1,0:T(8,128)(2,1)S(1)}, u32[]{:S(2)}, u32[]{:S(2)}) collective-permute-start(bf16[512,256]{1,0:T(8,128)(2,1)S(1)} %get-tuple-element.47), channel_id=1, source_target_pairs={{0,8},{4,12},{8,0},{12,4},{16,24},{20,28},{24,16},{28,20},{1,9},{5... | collective-permute-start | bytes 786440 | tf_op jit(solution)/shard_map/ppermute | solution.py:35
  9.4 13.6 %collective-permute-start.10 = (bf16[128,512]{1,0:T(8,128)(2,1)S(1)}, bf16[128,512]{1,0:T(8,128)(2,1)S(1)}, u32[]{:S(2)}, u32[]{:S(2)}) collective-permute-start(bf16[128,512]{1,0:T(8,128)(2,1)S(1)} %get-tuple-element.55.refs_9_), channel_id=1, source_target_pairs={{0,24},{4,28},{8,16},{12,20},{16,8},{20,12},{24,0},{28,4},{1,25},{... | collective-permute-start | bytes 393224 | tf_op jit(solution)/shard_map/ppermute | solution.py:51
  10.9 14.6 %collective-permute-start.8 = (bf16[128,512]{1,0:T(8,128)(2,1)S(1)}, bf16[128,512]{1,0:T(8,128)(2,1)S(1)}, u32[]{:S(2)}, u32[]{:S(2)}) collective-permute-start(bf16[128,512]{1,0:T(8,128)(2,1)S(1)} %get-tuple-element.55.refs_9_), channel_id=1, source_target_pairs={{0,8},{4,12},{8,0},{12,4},{16,24},{20,28},{24,16},{28,20},{1,9},{5... | collective-permute-start | bytes 393224 | tf_op jit(solution)/shard_map/ppermute | solution.py:35
  11.6 5.3 %collective-permute-start.2 = (s32[16,24]{1,0:T(8,128)S(1)}, s32[16,24]{1,0:T(8,128)S(1)}, u32[]{:S(2)}, u32[]{:S(2)}) collective-permute-start(s32[16,24]{1,0:T(8,128)S(1)} %pad_add_fusion), channel_id=1, source_target_pairs={{0,2},{1,3},{2,0},{3,1},{4,6},{5,7},{6,4},{7,5},{8,10},{9,11},{10,... | collective-permute-start | bytes 4616 | tf_op jit(solution)/shard_map/ppermute | solution.py:35
  16.9 9.2 %collective-permute-start.7 = (bf16[128,512]{1,0:T(8,128)(2,1)S(1)}, bf16[128,512]{1,0:T(8,128)(2,1)S(1)}, u32[]{:S(2)}, u32[]{:S(2)}) collective-permute-start(bf16[128,512]{1,0:T(8,128)(2,1)S(1)} %get-tuple-element.55.refs_9_), channel_id=1, source_target_pairs={{0,4},{4,0},{8,12},{12,8},{16,20},{20,16},{24,28},{28,24},{1,5},{5... | collective-permute-start | bytes 393224 | tf_op jit(solution)/shard_map/ppermute | solution.py:35
  22.3 4.5 %collective-permute-start.6 = (bf16[512,256]{1,0:T(8,128)(2,1)S(1)}, bf16[512,256]{1,0:T(8,128)(2,1)S(1)}, u32[]{:S(2)}, u32[]{:S(2)}) collective-permute-start(bf16[512,256]{1,0:T(8,128)(2,1)S(1)} %collective-permute-done.5.refs_7_), channel_id=1, source_target_pairs={{0,4},{4,0},{8,12},{12,8},{16,20},{20,16},{24,28},{28,24},{1,5},{5... | collective-permute-start | bytes 786440 | tf_op jit(solution)/shard_map/ppermute | solution.py:35
  32.7 6.3 %collective-permute-start.12 = (bf16[64,512]{1,0:T(8,128)(2,1)S(1)}, bf16[64,512]{1,0:T(8,128)(2,1)S(1)}, u32[]{:S(2)}, u32[]{:S(2)}) collective-permute-start(bf16[64,512]{1,0:T(8,128)(2,1)S(1)} %get-tuple-element.59), channel_id=1, source_target_pairs={{0,1},{1,2},{2,3},{3,0},{4,5},{5,6},{6,7},{7,4},{8,9},{9,10},{10,1... | collective-permute-start | bytes 196616 | tf_op jit(solution)/shard_map/ppermute | solution.py:40
  33.6 6.8 %collective-permute-start.13 = (bf16[64,512]{1,0:T(8,128)(2,1)S(1)}, bf16[64,512]{1,0:T(8,128)(2,1)S(1)}, u32[]{:S(2)}, u32[]{:S(2)}) collective-permute-start(bf16[64,512]{1,0:T(8,128)(2,1)S(1)} %get-tuple-element.61), channel_id=1, source_target_pairs={{0,1},{1,2},{2,3},{3,0},{4,5},{5,6},{6,7},{7,4},{8,9},{9,10},{10,1... | collective-permute-start | bytes 196616 | tf_op jit(solution)/shard_map/ppermute | solution.py:40
  35.0 7.3 %collective-permute-start.14 = (bf16[64,512]{1,0:T(8,128)(2,1)S(1)}, bf16[64,512]{1,0:T(8,128)(2,1)S(1)}, u32[]{:S(2)}, u32[]{:S(2)}) collective-permute-start(bf16[64,512]{1,0:T(8,128)(2,1)S(1)} %get-tuple-element.62), channel_id=1, source_target_pairs={{0,2},{1,3},{2,0},{3,1},{4,6},{5,7},{6,4},{7,5},{8,10},{9,11},{10,... | collective-permute-start | bytes 196616 | tf_op jit(solution)/shard_map/ppermute | solution.py:40
  37.1 5.2 %collective-permute-start.15 = (bf16[64,512]{1,0:T(8,128)(2,1)S(1)}, bf16[64,512]{1,0:T(8,128)(2,1)S(1)}, u32[]{:S(2)}, u32[]{:S(2)}) collective-permute-start(bf16[64,512]{1,0:T(8,128)(2,1)S(1)} %get-tuple-element.63), channel_id=1, source_target_pairs={{0,3},{1,0},{2,1},{3,2},{4,7},{5,4},{6,5},{7,6},{8,11},{9,8},{10,9... | collective-permute-start | bytes 196616 | tf_op jit(solution)/shard_map/ppermute | solution.py:40
  42.4 6.7 %collective-permute-start.16 = (bf16[64,512]{1,0:T(8,128)(2,1)S(1)}, bf16[64,512]{1,0:T(8,128)(2,1)S(1)}, u32[]{:S(2)}, u32[]{:S(2)}) collective-permute-start(bf16[64,512]{1,0:T(8,128)(2,1)S(1)} %get-tuple-element.65.refs_5_), channel_id=1, source_target_pairs={{0,4},{4,0},{8,12},{12,8},{16,20},{20,16},{24,28},{28,24},{1,5},{5... | collective-permute-start | bytes 196616 | tf_op jit(solution)/shard_map/ppermute | solution.py:35
  42.4 6.7 %collective-permute-start.17 = (bf16[64,512]{1,0:T(8,128)(2,1)S(1)}, bf16[64,512]{1,0:T(8,128)(2,1)S(1)}, u32[]{:S(2)}, u32[]{:S(2)}) collective-permute-start(bf16[64,512]{1,0:T(8,128)(2,1)S(1)} %get-tuple-element.68), channel_id=1, source_target_pairs={{0,2},{1,3},{2,0},{3,1},{4,6},{5,7},{6,4},{7,5},{8,10},{9,11},{10,... | collective-permute-start | bytes 196616 | tf_op jit(solution)/shard_map/ppermute | solution.py:40
  43.3 6.0 %collective-permute-start.18 = (bf16[64,512]{1,0:T(8,128)(2,1)S(1)}, bf16[64,512]{1,0:T(8,128)(2,1)S(1)}, u32[]{:S(2)}, u32[]{:S(2)}) collective-permute-start(bf16[64,512]{1,0:T(8,128)(2,1)S(1)} %get-tuple-element.69), channel_id=1, source_target_pairs={{0,3},{1,0},{2,1},{3,2},{4,7},{5,4},{6,5},{7,6},{8,11},{9,8},{10,9... | collective-permute-start | bytes 196616 | tf_op jit(solution)/shard_map/ppermute | solution.py:40
  46.7 5.5 %collective-permute-start.22 = (bf16[64,512]{1,0:T(8,128)(2,1)S(1)}, bf16[64,512]{1,0:T(8,128)(2,1)S(1)}, u32[]{:S(2)}, u32[]{:S(2)}) collective-permute-start(bf16[64,512]{1,0:T(8,128)(2,1)S(1)} %get-tuple-element.65.refs_5_), channel_id=1, source_target_pairs={{0,24},{4,28},{8,16},{12,20},{16,8},{20,12},{24,0},{28,4},{1,25},{... | collective-permute-start | bytes 196616 | tf_op jit(solution)/shard_map/ppermute | solution.py:51
  52.7 8.2 %collective-permute-start.19 = (f32[160,128]{1,0:T(8,128)S(1)}, f32[160,128]{1,0:T(8,128)S(1)}, u32[]{:S(2)}, u32[]{:S(2)}) collective-permute-start(f32[160,128]{1,0:T(8,128)S(1)} %get-tuple-element.72), channel_id=1, source_target_pairs={{0,4},{4,0},{8,12},{12,8},{16,20},{20,16},{24,28},{28,24},{1,5},{5... | collective-permute-start | bytes 245768 | tf_op jit(solution)/shard_map/ppermute | solution.py:35
  57.0 6.8 %collective-permute-start.24 = (bf16[64,512]{1,0:T(8,128)(2,1)S(1)}, bf16[64,512]{1,0:T(8,128)(2,1)S(1)}, u32[]{:S(2)}, u32[]{:S(2)}) collective-permute-start(bf16[64,512]{1,0:T(8,128)(2,1)S(1)} %get-tuple-element.77), channel_id=1, source_target_pairs={{0,1},{1,2},{2,3},{3,0},{4,5},{5,6},{6,7},{7,4},{8,9},{9,10},{10,1... | collective-permute-start | bytes 196616 | tf_op jit(solution)/shard_map/ppermute | solution.py:40
  57.1 8.2 %collective-permute-start.28 = (bf16[64,512]{1,0:T(8,128)(2,1)S(1)}, bf16[64,512]{1,0:T(8,128)(2,1)S(1)}, u32[]{:S(2)}, u32[]{:S(2)}) collective-permute-start(bf16[64,512]{1,0:T(8,128)(2,1)S(1)} %get-tuple-element.80), channel_id=1, source_target_pairs={{0,2},{1,3},{2,0},{3,1},{4,6},{5,7},{6,4},{7,5},{8,10},{9,11},{10,... | collective-permute-start | bytes 196616 | tf_op jit(solution)/shard_map/ppermute | solution.py:40
  58.9 6.5 %collective-permute-start.29 = (bf16[64,512]{1,0:T(8,128)(2,1)S(1)}, bf16[64,512]{1,0:T(8,128)(2,1)S(1)}, u32[]{:S(2)}, u32[]{:S(2)}) collective-permute-start(bf16[64,512]{1,0:T(8,128)(2,1)S(1)} %get-tuple-element.81), channel_id=1, source_target_pairs={{0,3},{1,0},{2,1},{3,2},{4,7},{5,4},{6,5},{7,6},{8,11},{9,8},{10,9... | collective-permute-start | bytes 196616 | tf_op jit(solution)/shard_map/ppermute | solution.py:40
  66.2 5.3 %collective-permute-start.25 = (f32[160,128]{1,0:T(8,128)S(1)}, f32[160,128]{1,0:T(8,128)S(1)}, u32[]{:S(2)}, u32[]{:S(2)}) collective-permute-start(f32[160,128]{1,0:T(8,128)S(1)} %add.180), channel_id=1, source_target_pairs={{0,8},{4,12},{8,0},{12,4},{16,24},{20,28},{24,16},{28,20},{1,9},{5... | collective-permute-start | bytes 245768 | tf_op jit(solution)/shard_map/ppermute | solution.py:35
  66.5 6.8 %collective-permute-start.26 = (f32[160,128]{1,0:T(8,128)S(1)}, f32[160,128]{1,0:T(8,128)S(1)}, u32[]{:S(2)}, u32[]{:S(2)}) collective-permute-start(f32[160,128]{1,0:T(8,128)S(1)} %add.180), channel_id=1, source_target_pairs={{0,16},{4,20},{8,24},{12,28},{16,0},{20,4},{24,8},{28,12},{1,17},{... | collective-permute-start | bytes 245768 | tf_op jit(solution)/shard_map/ppermute | solution.py:35
  67.6 5.7 %collective-permute-start.27 = (f32[160,128]{1,0:T(8,128)S(1)}, f32[160,128]{1,0:T(8,128)S(1)}, u32[]{:S(2)}, u32[]{:S(2)}) collective-permute-start(f32[160,128]{1,0:T(8,128)S(1)} %add.180), channel_id=1, source_target_pairs={{0,24},{4,28},{8,16},{12,20},{16,8},{20,12},{24,0},{28,4},{1,25},{... | collective-permute-start | bytes 245768 | tf_op jit(solution)/shard_map/ppermute | solution.py:35
  69.7 6.5 %collective-permute-start.35 = (f32[160,128]{1,0:T(8,128)S(1)}, f32[160,128]{1,0:T(8,128)S(1)}, u32[]{:S(2)}, u32[]{:S(2)}) collective-permute-start(f32[160,128]{1,0:T(8,128)S(1)} %add.184), channel_id=1, source_target_pairs={{0,8},{1,9},{2,10},{3,11},{4,5},{5,6},{6,7},{7,4},{8,0},{9,1},{10,... | collective-permute-start | bytes 245768 | tf_op jit(solution)/shard_map/ppermute | solution.py:92
  70.0 7.3 %collective-permute-start.36 = (f32[160,128]{1,0:T(8,128)S(1)}, f32[160,128]{1,0:T(8,128)S(1)}, u32[]{:S(2)}, u32[]{:S(2)}) collective-permute-start(f32[160,128]{1,0:T(8,128)S(1)} %add.184), channel_id=1, source_target_pairs={{0,16},{1,17},{2,18},{3,19},{4,6},{5,7},{6,4},{7,5},{8,24},{9,25},... | collective-permute-start | bytes 245768 | tf_op jit(solution)/shard_map/ppermute | solution.py:92
  71.5 5.9 %collective-permute-start.37 = (f32[160,128]{1,0:T(8,128)S(1)}, f32[160,128]{1,0:T(8,128)S(1)}, u32[]{:S(2)}, u32[]{:S(2)}) collective-permute-start(f32[160,128]{1,0:T(8,128)S(1)} %add.184), channel_id=1, source_target_pairs={{0,24},{1,25},{2,26},{3,27},{4,7},{5,4},{6,5},{7,6},{8,16},{9,17},... | collective-permute-start | bytes 245768 | tf_op jit(solution)/shard_map/ppermute | solution.py:92
  73.4 7.3 %collective-permute-start.31 = (f32[160,128]{1,0:T(8,128)S(1)}, f32[160,128]{1,0:T(8,128)S(1)}, u32[]{:S(2)}, u32[]{:S(2)}) collective-permute-start(f32[160,128]{1,0:T(8,128)S(1)} %add_add_fusion.3), channel_id=1, source_target_pairs={{0,1},{1,2},{2,3},{3,0},{4,5},{5,6},{6,7},{7,4},{8,9},{9,10},{10,1... | collective-permute-start | bytes 245768 | tf_op jit(solution)/shard_map/ppermute | solution.py:40
  74.9 7.8 %collective-permute-start.32 = (f32[160,128]{1,0:T(8,128)S(1)}, f32[160,128]{1,0:T(8,128)S(1)}, u32[]{:S(2)}, u32[]{:S(2)}) collective-permute-start(f32[160,128]{1,0:T(8,128)S(1)} %add_add_fusion.3), channel_id=1, source_target_pairs={{0,2},{1,3},{2,0},{3,1},{4,6},{5,7},{6,4},{7,5},{8,10},{9,11},{10,... | collective-permute-start | bytes 245768 | tf_op jit(solution)/shard_map/ppermute | solution.py:40
  76.3 6.5 %collective-permute-start.33 = (f32[160,128]{1,0:T(8,128)S(1)}, f32[160,128]{1,0:T(8,128)S(1)}, u32[]{:S(2)}, u32[]{:S(2)}) collective-permute-start(f32[160,128]{1,0:T(8,128)S(1)} %add_add_fusion.3), channel_id=1, source_target_pairs={{0,3},{1,0},{2,1},{3,2},{4,7},{5,4},{6,5},{7,6},{8,11},{9,8},{10,9... | collective-permute-start | bytes 245768 | tf_op jit(solution)/shard_map/ppermute | solution.py:40
  77.4 9.4 %collective-permute-start.38 = (f32[160,128]{1,0:T(8,128)S(1)}, f32[160,128]{1,0:T(8,128)S(1)}, u32[]{:S(2)}, u32[]{:S(2)}) collective-permute-start(f32[160,128]{1,0:T(8,128)S(1)} %add_add_fusion.1), channel_id=1, source_target_pairs={{0,1},{1,2},{2,3},{3,0},{4,12},{5,13},{6,14},{7,15},{8,9},{9,10},{... | collective-permute-start | bytes 245768 | tf_op jit(solution)/shard_map/ppermute | solution.py:92
  78.4 8.7 %collective-permute-start.39 = (f32[160,128]{1,0:T(8,128)S(1)}, f32[160,128]{1,0:T(8,128)S(1)}, u32[]{:S(2)}, u32[]{:S(2)}) collective-permute-start(f32[160,128]{1,0:T(8,128)S(1)} %add_add_fusion.1), channel_id=1, source_target_pairs={{0,2},{1,3},{2,0},{3,1},{4,20},{5,21},{6,22},{7,23},{8,10},{9,11},... | collective-permute-start | bytes 245768 | tf_op jit(solution)/shard_map/ppermute | solution.py:92
  80.7 6.4 %collective-permute-start.40 = (f32[160,128]{1,0:T(8,128)S(1)}, f32[160,128]{1,0:T(8,128)S(1)}, u32[]{:S(2)}, u32[]{:S(2)}) collective-permute-start(f32[160,128]{1,0:T(8,128)S(1)} %add_add_fusion.1), channel_id=1, source_target_pairs={{0,3},{1,0},{2,1},{3,2},{4,28},{5,29},{6,30},{7,31},{8,11},{9,8},{... | collective-permute-start | bytes 245768 | tf_op jit(solution)/shard_map/ppermute | solution.py:92
  (14 other events, 94.2 us)

commit v4 on v3

--- a/solution.py
+++ b/solution.py
@@ -22,7 +22,7 @@
 WEIGHT = 1.0 / (BR * MAXT)
 SIGMA = math.exp(TAU) * WEIGHT
 EXP2 = TAU / EMB * math.log2(math.e)
-GROUP = 8
+GROUP = 16
 SHARDS = 6
 F32 = jnp.float32
 BF16 = jnp.bfloat16
@@ -40,14 +40,14 @@
     return lax.ppermute(value, axis, [(i, (i + steps) % count) for i in range(count)])
 
 
-def other_side(value):
+def other_side(value, core_0_too=True):
     count = lax.axis_size("rows")
     chips = count // 2
     pairs = []
     for r in range(count):
         chip, core = divmod(r, 2)
         to = (chip + 1) % chips if chip % 2 else (chip - 1) % chips
-        pairs.append((r, to * 2 + core))
+        pairs.append((r, to * 2 + core if core or core_0_too else r ^ 2))
     return lax.ppermute(value, "rows", pairs)
 
 
@@ -63,24 +63,17 @@
     return [side_a, swapped(side_a, "rows", 1), side_b, swapped(side_b, "rows", 1)]
 
 
-def sum_tiles(value):
-    return value + sum(rotated(value, "tiles", n) for n in range(1, lax.axis_size("tiles")))
-
-
-def sum_rows(value):
-    rows, bits = lax.axis_size("rows"), 2
-    while bits < rows:
-        span = min(4, rows // bits)
-        value = value + sum(swapped(value, "rows", k * bits) for k in range(1, span))
-        bits *= span
+def sum_along(value, axis, bits):
+    while bits < lax.axis_size(axis):
+        value = value + swapped(value, axis, bits)
+        bits *= 2
     return value
 
 
 def sum_chips(value, part):
     rows, tiles = lax.axis_size("rows"), lax.axis_size("tiles")
     if rows // 2 != tiles or tiles != 4:
-        total = (sum_tiles if part else sum_rows)(value)
-        return total, total
+        return sum_along(value, "tiles", 1) if part else sum_along(value, "rows", 2)
     parts = [value]
     for step in range(1, 4):
         pairs = []
@@ -90,11 +83,7 @@
                 to = (r ^ (2 * step), t) if along_rows else (r, (t + step) % tiles)
                 pairs.append((r * tiles + t, to[0] * tiles + to[1]))
         parts.append(lax.ppermute(value, ("rows", "tiles"), pairs))
-    return sum(parts), parts[1]
-
-
-def after_list(values, other):
-    return [after(values[0], other), *values[1:]]
+    return sum(parts)
 
 
 def dot_t(a, b):
@@ -113,7 +102,7 @@
     return (values * lax.rsqrt(mean + EPS)).astype(BF16)
 
 
-def pack_kernel(meta, emb, block, step, cols, emb_out, vec_out, cols_out, block_buf, step_buf, sems):
+def pack_kernel(meta, emb, block, step, emb_out, vec_out, block_buf, step_buf, sems):
     here, width = meta[0], emb_out.shape[0]
     copies = [
         pltpu.make_async_copy(emb.at[pl.ds(here * width, width), :], emb_out, sems.at[0]),
@@ -122,7 +111,6 @@
     ]
     for copy in copies:
         copy.start()
-    cols_out[...] = cols[...]
     copies[1].wait()
     vec_out[:K, :] = block_buf[...].astype(BF16)
     copies[2].wait()
@@ -196,10 +184,7 @@
     copy.wait()
 
 
-def apply_tiles(blocks, share, devices, here, items, tiles, vec, outs, vec_ext, acc):
-    for j, ref in enumerate(vec):
-        for i in range(share):
-            vec_ext[j * share + i] = ref[:, pl.ds(i * BR, BR)]
+def apply_tiles(blocks, share, devices, here, items, tiles, outs, vec_ext, acc):
     acc[...] = jnp.zeros_like(acc)
     for i in range(share):
         acc[here * share + i] = jnp.dot(vec_ext[i], tiles[0][i], preferred_element_type=F32)
@@ -248,13 +233,24 @@
     build_tiles(blocks, 0, items[1], unit_own, unit_ext, far)
     copy.wait()
     group_copies(count, share, stored, near, sems, lambda copy: copy.wait())
-    apply_tiles(blocks, share, devices, meta[0], items, (near, far), vec, outs, vec_ext, acc)
+    for j, ref in enumerate(vec):
+        for i in range(share):
+            vec_ext[j * share + i] = ref[:, pl.ds(i * BR, BR)]
+    apply_tiles(blocks, share, devices, meta[0], items, (near, far), outs, vec_ext, acc)
 
 
 def apply_kernel(blocks, share, devices, *refs):
     meta, items, tiles = refs[0], refs[1:3], refs[3:5]
-    vec, outs, (vec_ext, acc) = refs[5 : 5 + SHARDS], refs[5 + SHARDS : -2], refs[-2:]
-    apply_tiles(blocks, share, devices, meta[0], items, tiles, vec, outs, vec_ext, acc)
+    own, core, mine, other = refs[5:9]
+    outs, (vec_ext, acc) = refs[9:-2], refs[-2:]
+    odd = meta[1]
+    slots = [(own, 0, 0), (core, 0, 1)]
+    slots += [(mine, 0, 2 + 2 * odd), (mine, 1, 3 + 2 * odd)]
+    slots += [(other, 0, 5 - 2 * odd), (other, 1, 4 - 2 * odd)]
+    for ref, half, slot in slots:
+        for i in range(share):
+            vec_ext[slot * share + i] = ref[pl.ds(half * K, K), pl.ds(i * BR, BR)]
+    apply_tiles(blocks, share, devices, meta[0], items, tiles, outs, vec_ext, acc)
 
 
 def summed(parts, diag, vectors):
@@ -275,6 +271,28 @@
     return jnp.dot(a, b, precision=PRECISE, preferred_element_type=F32)
 
 
+def halves_of(value):
+    high = value.astype(BF16)
+    return high, (value - high.astype(F32)).astype(BF16)
+
+
+def mul3(a, b):
+    (a_high, a_low), (b_high, b_low) = halves_of(a), halves_of(b)
+    return jnp.dot(
+        jnp.concatenate([a_high, a_high, a_low], axis=1),
+        jnp.concatenate([b_high, b_low, b_high], axis=0),
+        preferred_element_type=F32,
+    )
+
+
+def dot3(a, b):
+    (a_high, a_low), (b_high, b_low) = halves_of(a), halves_of(b)
+    return dot_t(
+        jnp.concatenate([a_high, a_high, a_low], axis=1),
+        jnp.concatenate([b_high, b_low, b_high], axis=1),
+    )
+
+
 def eye_mask(n):
     shape = (n, n)
     return lax.broadcasted_iota(jnp.int32, shape, 0) == lax.broadcasted_iota(jnp.int32, shape, 1)
@@ -286,15 +304,15 @@
 
 def step_coefficients(g_vv, g_vs, g_ss, g_jv, g_js, g_jj, rotation, total):
     m_t = g_jv * (1.0 / total) + SIGMA * (g_vv * (1.0 / total) - eye_mask(K).astype(F32))
-    resid_sq = (
-        jnp.sum(jnp.where(eye_mask(K), g_jj, 0.0), axis=1, keepdims=True)
-        - 2.0 * jnp.sum(m_t * g_jv, axis=1, keepdims=True)
-        + jnp.sum(m_t * mul(m_t, g_vv), axis=1, keepdims=True)
+    resid_sq = jnp.sum(
+        jnp.where(eye_mask(K), g_jj, 0.0) + m_t * (mul(m_t, g_vv) - 2.0 * g_jv),
+        axis=1,
+        keepdims=True,
     )
     resid_inv = 1.0 / jnp.sqrt(jnp.maximum(resid_sq, 0.0) * (1.0 / total) + EPS)
-    on_v, on_resid, on_s = rotation[:K].T, rotation[K : 2 * K].T, rotation[2 * K :].T
+    on_v, on_resid, on_s = rotation[:, :K], rotation[:, K : 2 * K], rotation[:, 2 * K :]
     p_j = on_resid * as_row(resid_inv)
-    p_step = -mul(p_j, m_t)
+    p_step = -mul3(p_j, m_t)
     coef = jnp.concatenate(
         [
             jnp.concatenate([on_v + p_step, on_s, p_j], axis=1),
@@ -310,45 +328,43 @@
         ],
         axis=0,
     )
-    on_gram = mul(coef, gram)
+    on_gram = mul3(coef, gram)
     comb_sq = jnp.sum(on_gram[:K] * coef[:K], axis=1, keepdims=True)
     scale = 1.0 / jnp.sqrt(jnp.maximum(comb_sq, 0.0) * (1.0 / total) + EPS)
     return coef, on_gram, jnp.concatenate([scale, scale], axis=0)
 
 
-def gram_kernel(devices, meta, x_ref, y_ref, j_ref, diag, *refs):
-    parts, (rows, keep, send) = refs[:devices], refs[devices:]
+def split_by_core(core, value, keep, send):
+    half = keep.shape[0]
+    keep[...] = jnp.where(core == 0, value[:half], value[half:])
+    send[...] = jnp.where(core == 0, value[half:], value[:half])
+
+
+def joined(core, mine, other):
+    return jnp.concatenate(
+        [
+            jnp.where(core == 0, mine[...], other[...]),
+            jnp.where(core == 0, other[...], mine[...]),
+        ],
+        axis=0,
+    )
+
+
+def gram_kernel(x_ref, y_ref, j_ref, rows, out):
     rows[:K, :] = x_ref[...]
     rows[K : 2 * K, :] = y_ref[...]
-    rows[2 * K : 3 * K, :] = j_ref[...]
-    rows[3 * K :, :] = summed(parts, diag, y_ref[...])
+    rows[2 * K :, :] = j_ref[...]
     g = dot_exact(rows[...], rows[...])
-    packed = jnp.concatenate(
-        [
-            g[:K, : 2 * K],
-            jnp.concatenate([g[K : 2 * K, K : 2 * K], g[3 * K :, 3 * K :]], axis=1),
-            g[: 3 * K, 2 * K :],
-        ],
-        axis=0,
-    )
-    half = keep.shape[0]
-    keep[...] = jnp.where(meta[1] == 0, packed[:half], packed[half:])
-    send[...] = jnp.where(meta[1] == 0, packed[half:], packed[:half])
-
-
-def first_kernel(total, meta, rot_ref, rows, mine, other, new_out, part_out, coef_out, g_out, l_out):
-    packed = jnp.concatenate(
-        [
-            jnp.where(meta[1] == 0, mine[...], other[...]),
-            jnp.where(meta[1] == 0, other[...], mine[...]),
-        ],
-        axis=0,
-    )
+    out[:K, :] = g[:K, : 2 * K]
+    out[K : 2 * K, :K] = g[K : 2 * K, K : 2 * K]
+    out[K : 2 * K, K:] = g[2 * K :, 2 * K :]
+    out[2 * K :, :] = g[2 * K :, : 2 * K]
+
+
+def first_step(packed, rotation, total):
     xx, xy = packed[:K, :K], packed[:K, K:]
-    yy, tt = packed[K : 2 * K, :K], packed[K : 2 * K, K:]
-    xj, xt = packed[2 * K : 3 * K, :K], packed[2 * K : 3 * K, K:]
-    yj, yt = packed[3 * K : 4 * K, :K], packed[3 * K : 4 * K, K:]
-    jj, jt = packed[4 * K :, :K], packed[4 * K :, K:]
+    yy, jj = packed[K : 2 * K, :K], packed[K : 2 * K, K:]
+    jx, jy = packed[2 * K :, :K], packed[2 * K :, K:]
 
     def inv_rms(square):
         picked = jnp.sum(jnp.where(eye_mask(K), square, 0.0), axis=1, keepdims=True)
@@ -360,66 +376,79 @@
         xx * x_col * x_row,
         xy * x_col * y_row,
         yy * y_col * y_row,
-        xj.T * x_col * x_row,
-        yj.T * x_col * y_row,
+        jx * x_col * x_row,
+        jy * x_col * y_row,
         jj * x_col * x_row,
-        rot_ref[...],
+        rotation,
         total,
     )
     coef = scale * coef
-    g_out[...] = dot_exact(scale * on_gram, coef)
+    gram = dot3(scale * on_gram, coef)
     coef = coef * jnp.concatenate([x_row, y_row, x_row], axis=1)
-    coef_out[...] = coef
-    new_out[...] = mul(coef, rows[: 3 * K, :])
-    known = coef[:K, : 2 * K]
-    part_out[...] = mul(known, rows[2 * K :, :])
-    j_t = jnp.concatenate(
+    return coef, gram, mul3(coef[:K, :K], jnp.concatenate([jx, jy, jj], axis=1))
+
+
+def twice_kernel(devices, meta, rows, gram, step, diag, *refs):
+    t_parts, q_parts = refs[:devices], refs[devices : 2 * devices]
+    t_out, q_out, keep, send = refs[2 * devices :]
+    t = summed(t_parts, diag, step[...])
+    q = summed(q_parts, diag, rows[2 * K :, :])
+    t_out[...] = t
+    q_out[...] = q
+    both = jnp.concatenate([t, q], axis=0)
+    on_rows = dot3(both, rows[...])
+    on_both = dot3(both, both)
+    half = K // 2
+    packed = jnp.concatenate(
         [
-            jnp.concatenate([xj.T, yj.T, jj, jt], axis=1),
-            jnp.concatenate([xt.T, yt.T, jt.T, tt], axis=1),
+            gram[...],
+            on_rows[:, : 2 * K],
+            jnp.concatenate([on_rows[:K, 2 * K :], on_rows[K:, 2 * K :]], axis=1),
+            on_both[K:],
+            jnp.concatenate([on_both[:half, :K], on_both[half:K, :K]], axis=1),
         ],
         axis=0,
     )
-    l_out[...] = mul(known, j_t)
-
-
-def twice_kernel(devices, rows, diag, *refs):
-    parts, (q_out, out) = refs[:devices], refs[devices:]
-    q = summed(parts, diag, rows[2 * K : 3 * K, :])
-    q_out[...] = q
-    g = dot_exact(q, rows[...])
-    out[:K, :] = g[:, : 2 * K]
-    out[K : 2 * K, :] = g[:, 2 * K :]
-    qq = dot_exact(q, q)
-    out[2 * K :, :K] = qq[: K // 2]
-    out[2 * K :, K:] = qq[K // 2 :]
-
-
-def image_again_kernel(part, coef, q, out):
-    out[...] = part[...] + mul(coef[:K, 2 * K :], q[...])
-
-
-def last_kernel(total, rot_ref, new, j_ref, coef_ref, g_ref, l_ref, h_ref, v_out, s_out):
-    coef, gram = coef_ref[...], g_ref[...]
-    q_xy, q_jt = h_ref[:K, :], h_ref[K : 2 * K, :]
-    qq = jnp.concatenate([h_ref[2 * K :, :K], h_ref[2 * K :, K:]], axis=0)
-    q_all = jnp.concatenate([q_xy, q_jt, qq], axis=1)
-    image = mul(coef[:K, 2 * K :], q_all)
-    on_rows = l_ref[...] + image[:, : 4 * K]
-    on_q = dot_exact(coef[:K, : 2 * K], q_jt) + image[:, 4 * K :]
-    j_new = dot_exact(on_rows[:, : 3 * K], coef)
-    g_jj = dot_exact(jnp.concatenate([on_rows[:, 2 * K :], on_q], axis=1), coef[:K])
-    coef, _, scale = step_coefficients(
+    split_by_core(meta[1], packed, keep, send)
+
+
+def last_kernel(total, meta, rot_ref, rows, t_ref, q_ref, mine, other, v_out, s_out):
+    packed = joined(meta[1], mine, other)
+    coef, gram, known = first_step(packed[: 3 * K], rot_ref[0], total)
+    packed = packed[3 * K :]
+    on_xy, on_j, on_both = packed[: 2 * K], packed[2 * K : 3 * K], packed[3 * K :]
+    tq_j = jnp.concatenate([on_j[:, :K], on_j[:, K:]], axis=0)
+    qt, qq = on_both[:K, :K], on_both[:K, K:]
+    tt = jnp.concatenate([on_both[K:, :K], on_both[K:, K:]], axis=0)
+    on_tq = jnp.concatenate(
+        [jnp.concatenate([tt, qt.T], axis=1), jnp.concatenate([qt, qq], axis=1)], axis=0
+    )
+    image = mul3(coef[:K, K:], jnp.concatenate([on_xy, tq_j, on_tq], axis=1))
+    on_rows = known + image[:, : 3 * K]
+    on_tq = dot3(coef[:K, :K], tq_j) + image[:, 3 * K :]
+    j_new = dot3(on_rows, coef)
+    g_jj = dot3(jnp.concatenate([on_rows[:, 2 * K :], on_tq], axis=1), coef[:K])
+    again, _, scale = step_coefficients(
         gram[:K, :K],
         gram[:K, K:],
         gram[K:, K:],
         j_new[:, :K],
         j_new[:, K:],
         g_jj,
-        rot_ref[...],
+        rot_ref[1],
         total,
     )
-    both = scale * mul(coef, jnp.concatenate([new[...], j_ref[...]], axis=0))
+    on_new = mul3(again[:, : 2 * K], coef)
+    on_image = mul3(again[:, 2 * K :], coef[:K])
+    both = jnp.concatenate(
+        [
+            on_new[:, : 2 * K],
+            on_new[:, 2 * K :] + on_image[:, :K],
+            on_image[:, K:],
+        ],
+        axis=1,
+    )
+    both = scale * mul3(both, jnp.concatenate([rows[...], t_ref[...], q_ref[...]], axis=0))
     v_out[...], s_out[...] = both[:K], both[K:]
 
 
@@ -487,14 +516,13 @@
     here, row = lax.axis_index("tiles"), lax.axis_index("rows")
 
     meta = jnp.stack([here, row % 2])
-    own_emb, own_vec, cols = call(
+    own_emb, own_vec = call(
         pack_kernel,
-        [((width, EMB), BF16), ((2 * K, width), BF16), (neighbour_cols.shape, jnp.int32)],
+        [((width, EMB), BF16), ((2 * K, width), BF16)],
         meta,
         embedding,
         start_block,
         start_step,
-        neighbour_cols,
         smem=1,
         hbm=3,
         scratch=[
@@ -505,7 +533,7 @@
         us=1.0,
     )
     emb_a, emb_b, emb_core = across(own_emb)
-    lists = after(cols, emb_core)
+    lists = after(neighbour_cols, emb_core)
     bits = 1
     while bits < devices:
         lists = jnp.concatenate([lists, swapped(lists, "tiles", bits)], axis=1)
@@ -584,74 +612,55 @@
     def gathered(parts):
         return [parts[0]] + [rotated(part, "tiles", n + 1) for n, part in enumerate(parts[1:])]
 
-    parts, step_parts = gathered(parts[:devices]), gathered(parts[devices:])
+    parts, step_out = gathered(parts[:devices]), parts[devices:]
     image, image_half = call(
         functools.partial(image_kernel, devices),
         [((K, width), F32), ((K, width), BF16)],
-        *after_list(parts, step_parts[1]),
+        *parts,
         diag,
         start_block,
         us=0.1,
     )
-    image_a, image_b, image_core = across(image_half)
-    half = 5 * K // 2
-    rows, keep, send = call(
-        functools.partial(gram_kernel, devices),
-        [((4 * K, width), F32)] + [((half, 2 * K), F32)] * 2,
-        meta,
+    image_core = swapped(image_half, "rows", 1)
+    image_side = other_side(jnp.concatenate([image_half, image_core], axis=0), False)
+    rows, gram = call(
+        gram_kernel,
+        [((3 * K, width), F32), ((3 * K, 2 * K), F32)],
         start_block,
         start_step,
         after(image, image_core),
+        us=0.8,
+    )
+    step_parts = gathered([after(part, gram) for part in step_out])
+    image_side = after(image_side, *step_parts[1:2])
+    image_vec = [image_half, image_core, image_side, swapped(image_side, "rows", 1)]
+    parts = gathered(applied(image_vec))
+    step_image, twice, keep, send = call(
+        functools.partial(twice_kernel, devices),
+        [((K, width), F32)] * 2 + [((15 * K // 4, 2 * K), F32)] * 2,
+        meta,
+        rows,
+        gram,
+        start_step,
         diag,
         *step_parts,
+        *parts,
         smem=1,
-        us=1.0,
-    )
-    image_vec = [image_half, image_core, *by_core(after(image_a, keep), after(image_b, keep))]
-    gram = keep + swapped(send, "rows", 1)
-    parts = gathered(applied(image_vec))
-    gram = sum_rows(after(gram, parts[1]))
-    twice, products = call(
-        functools.partial(twice_kernel, devices),
-        [((K, width), F32), ((half, 2 * K), F32)],
-        rows,
-        diag,
-        *parts,
-        us=0.8,
-    )
-    products = products + swapped(products, "rows", 1)
-    gram = sum_tiles(after(gram, products))
-    products, _ = sum_chips(products, 0)
-    products, _ = sum_chips(products, 1)
-    new, part, coef, gram, known = call(
-        functools.partial(first_kernel, total),
-        [
-            ((2 * K, width), F32),
-            ((K, width), F32),
-            ((2 * K, 3 * K), F32),
-            ((2 * K, 2 * K), F32),
-            ((K, 4 * K), F32),
-        ],
-        meta,
-        rotations[0],
-        rows,
-        gram,
-        swapped(gram, "rows", 1),
-        smem=1,
-        us=0.0,
-    )
-    (image,) = call(image_again_kernel, [((K, width), F32)], part, coef, twice, us=0.0)
+        us=1.3,
+    )
+    products = sum_chips(sum_chips(keep + swapped(send, "rows", 1), 0), 1)
     return call(
         functools.partial(last_kernel, total),
         [((K, width), F32)] * 2,
-        rotations[1],
-        new,
-        image,
-        coef,
-        gram,
-        known,
+        meta,
+        rotations.swapaxes(1, 2),
+        rows,
+        step_image,
+        twice,
         products,
-        us=2.5,
+        swapped(products, "rows", 1),
+        smem=1,
+        us=3.2,
     )
 
 

time: 90.3 us -> 87.4 us (0.968); the launches traced: 89.2 us -> 87.7 us
  waiting for transfers between devices: 16.6 us -> 31.9 us
  starting transfers between devices: 44 us -> 34.1 us
  Pallas kernels: 24.5 us -> 17.9 us
    ppermute x6, waiting for transfers between devices: 0.25 us -> 11.5 us  [sum_chips(): parts.append(lax.ppermute(value, ('rows', 'tiles'), pairs))]
    pallas_call x11 -> x9, Pallas kernels: 24.5 us -> 17.9 us  [call(): pl.pallas_call(kernel, out_shape=tuple((pltpu.HBM(*out[:2]) if len(out) >...]
    ppermute x20 -> x14, starting transfers between devices: 12.1 us -> 6.66 us  [swapped(): return lax.ppermute(value, axis, [(i, i ^ bits) for i in range(count)])]
    ppermute x12 -> x9, starting transfers between devices: 18.3 us -> 13.4 us  [rotated(): lax.ppermute(value, axis, [(i, (i + steps) % count) for i in range(count)])]
    ppermute x12 -> x9, waiting for transfers between devices: 9.08 us -> 13.2 us  [rotated(): lax.ppermute(value, axis, [(i, (i + steps) % count) for i in range(count)])]
    ppermute x3, waiting for transfers between devices: 1.72 us -> 0.01 us  [other_side(): return lax.ppermute(value, 'rows', pairs)]
    ppermute x20 -> x14, waiting for transfers between devices: 5.57 us -> 7.22 us  [swapped(): return lax.ppermute(value, axis, [(i, i ^ bits) for i in range(count)])]
    ppermute x3, starting transfers between devices: 6.15 us -> 7.61 us  [other_side(): return lax.ppermute(value, 'rows', pairs)]
  transfers between devices with their start and end apart: 41 -> 32, of which waited for: 18 -> 19; matrix products, arithmetic and copies ran while one was open for 2% -> 3% of each run, Pallas kernels for 16% -> 9%
where the time goes in v4:
time: 87.4 us; the launch traced here: 87.7 us
  starting transfers between devices  34.1 us (39%)
  waiting for transfers between devices  31.9 us (36%)
  Pallas kernels  17.9 us (20%)
  other arithmetic  2.17 us (2%)
  between operations  0.94 us (1%)
    pallas_call x9, Pallas kernels, call(): pl.pallas_call(kernel, out_shape=tuple((pltpu.HBM(*out[:2]) if len(out) >...  17.9 us
    ppermute x9, starting transfers between devices, rotated(): lax.ppermute(value, axis, [(i, (i + steps) % count) for i in range(count)])  13.4 us
    ppermute x9, waiting for transfers between devices, rotated(): lax.ppermute(value, axis, [(i, (i + steps) % count) for i in range(count)])  13.2 us
    ppermute x6, waiting for transfers between devices, sum_chips(): parts.append(lax.ppermute(value, ('rows', 'tiles'), pairs))  11.5 us
    ppermute x3, starting transfers between devices, other_side(): return lax.ppermute(value, 'rows', pairs)  7.61 us
    ppermute x14, waiting for transfers between devices, swapped(): return lax.ppermute(value, axis, [(i, i ^ bits) for i in range(count)])  7.22 us
    ppermute x14, starting transfers between devices, swapped(): return lax.ppermute(value, axis, [(i, i ^ bits) for i in range(count)])  6.66 us
    ppermute x6, starting transfers between devices, sum_chips(): parts.append(lax.ppermute(value, ('rows', 'tiles'), pairs))  6.42 us
  transfers between devices with their start and end apart: 32, of which 19 were waited for; matrix products, arithmetic and copies ran while one was open for 3% of the time, Pallas kernels for 9%

profile of v4, /device:TPU:0, one launch (start us, length us, event | category | flops | bytes accessed | tf_op | source)
XLA Modules:
  0.0 87.7 jit_solution(1171876783436855262)
XLA Ops:
  0.7 1.6 %shard_map.77 = (bf16[512,256]{1,0:T(8,128)(2,1)S(1)}, bf16[128,512]{1,0:T(8,128)(2,1)S(1)}) custom-call(s32[2]{0:T(128)S(1)} %pad_add_fusion.2.meta.refs_0_, bf16[2048,256]{1,0:T(8,128)(2,1)} %emb.1, f32[64,512]{1,0:T(8,128)} %x_ref.1, f32[64,512]{1,0:T(8,128)} %step.3), custom_call_target="tpu_custom_call" | custom-call | flops 1000000000 | tf_op jit(solution)/shard_map/pallas_call | solution.py:461
  2.4 4.0 %collective-permute-start.5 = (bf16[512,256]{1,0:T(8,128)(2,1)S(1)}, bf16[512,256]{1,0:T(8,128)(2,1)S(1)}, u32[]{:S(2)}, u32[]{:S(2)}) collective-permute-start(bf16[512,256]{1,0:T(8,128)(2,1)S(1)} %get-tuple-element.41), channel_id=1, source_target_pairs={{0,24},{4,28},{8,16},{12,20},{16,8},{20,12},{24,0},{28,4},{1,25},{... | collective-permute-start | bytes 786440 | tf_op jit(solution)/shard_map/ppermute | solution.py:51
  7.0 1.4 %collective-permute-done.emb_core = bf16[512,256]{1,0:T(8,128)(2,1)S(1)} collective-permute-done((bf16[512,256]{1,0:T(8,128)(2,1)S(1)}, bf16[512,256]{1,0:T(8,128)(2,1)S(1)}, u32[]{:S(2)}, u32[]{:S(2)}) %collective-permute-start) | collective-permute-done | bytes 262176 | tf_op jit(solution)/shard_map/ppermute | solution.py:35
  8.4 1.6 %collective-permute-start.1 = (s32[16,12]{1,0:T(8,128)}, s32[16,12]{1,0:T(8,128)S(1)}, u32[]{:S(2)}, u32[]{:S(2)}) collective-permute-start(s32[16,12]{1,0:T(8,128)} %param.10), channel_id=1, source_target_pairs={{0,1},{1,0},{2,3},{3,2},{4,5},{5,4},{6,7},{7,6},{8,9},{9,8},{10,11... | collective-permute-start | bytes 2312 | tf_op jit(solution)/shard_map/ppermute | solution.py:35
  10.0 1.4 %collective-permute-start.10 = (bf16[128,512]{1,0:T(8,128)(2,1)S(1)}, bf16[128,512]{1,0:T(8,128)(2,1)S(1)}, u32[]{:S(2)}, u32[]{:S(2)}) collective-permute-start(bf16[128,512]{1,0:T(8,128)(2,1)S(1)} %get-tuple-element.49.refs_9_), channel_id=1, source_target_pairs={{0,24},{4,28},{8,16},{12,20},{16,8},{20,12},{24,0},{28,4},{1,25},{... | collective-permute-start | bytes 393224 | tf_op jit(solution)/shard_map/ppermute | solution.py:51
  13.0 2.6 %collective-permute-start.2 = (s32[16,24]{1,0:T(8,128)S(1)}, s32[16,24]{1,0:T(8,128)S(1)}, u32[]{:S(2)}, u32[]{:S(2)}) collective-permute-start(s32[16,24]{1,0:T(8,128)S(1)} %pad_add_fusion), channel_id=1, source_target_pairs={{0,2},{1,3},{2,0},{3,1},{4,6},{5,7},{6,4},{7,5},{8,10},{9,11},{10,... | collective-permute-start | bytes 4616 | tf_op jit(solution)/shard_map/ppermute | solution.py:35
  15.6 2.7 %shard_map.78.unit_own.refs_4_ = bf16[16,128,256]{2,1,0:T(8,128)(2,1)S(1)} custom-call(bf16[16,128,256]{2,1,0:T(8,128)(2,1)} %bitcast.13), custom_call_target="tpu_custom_call" | custom-call | flops 2600000000 | tf_op jit(solution)/shard_map/pallas_call | solution.py:461
  19.7 2.7 %shard_map.79 = (f32[1,512]{1,0:T(1,128)S(1)}, bf16[148,128,128]{2,1,0:T(8,128)(2,1)}) custom-call(s32[2]{0:T(128)S(1)} %pad_add_fusion.2.meta.refs_0_, s32[145]{0:T(256)S(1)} %select_reduce_fusion.1.items.refs_1_, bf16[16,128,256]{2,1,0:T(8,128)(2,1)S(1)} %shard_map.78.unit_own.refs_4_, bf16[512,256]{1,0:T(8,128)(2,1)S(1)} %collective-permute-done.emb_core), custom_call_target="tpu_custom_call" | custom-call | flops 2000000000 | tf_op jit(solution)/shard_map/pallas_call | solution.py:461
  25.7 3.4 %shard_map.80 = (f32[64,512]{1,0:T(8,128)S(1)}, bf16[64,512]{1,0:T(8,128)(2,1)S(1)}, bf16[64,512]{1,0:T(8,128)(2,1)S(1)}, bf16[64,512]{1,0:T(8,128)(2,1)S(1)}, f...) custom-call(s32[2]{0:T(128)S(1)} %pad_add_fusion.2.meta.refs_0_, ...), custom_call_target="tpu_custom_call" | custom-call | flops 5000000000 | tf_op jit(solution)/shard_map/pallas_call | solution.py:461
  29.1 1.6 %collective-permute-start.12 = (bf16[64,512]{1,0:T(8,128)(2,1)S(1)}, bf16[64,512]{1,0:T(8,128)(2,1)S(1)}, u32[]{:S(2)}, u32[]{:S(2)}) collective-permute-start(bf16[64,512]{1,0:T(8,128)(2,1)S(1)} %get-tuple-element.53), channel_id=1, source_target_pairs={{0,1},{1,2},{2,3},{3,0},{4,5},{5,6},{6,7},{7,4},{8,9},{9,10},{10,1... | collective-permute-start | bytes 196616 | tf_op jit(solution)/shard_map/ppermute | solution.py:40
  30.7 2.6 %collective-permute-start.13 = (bf16[64,512]{1,0:T(8,128)(2,1)S(1)}, bf16[64,512]{1,0:T(8,128)(2,1)S(1)}, u32[]{:S(2)}, u32[]{:S(2)}) collective-permute-start(bf16[64,512]{1,0:T(8,128)(2,1)S(1)} %get-tuple-element.54), channel_id=1, source_target_pairs={{0,2},{1,3},{2,0},{3,1},{4,6},{5,7},{6,4},{7,5},{8,10},{9,11},{10,... | collective-permute-start | bytes 196616 | tf_op jit(solution)/shard_map/ppermute | solution.py:40
  33.3 1.4 %collective-permute-start.14 = (bf16[64,512]{1,0:T(8,128)(2,1)S(1)}, bf16[64,512]{1,0:T(8,128)(2,1)S(1)}, u32[]{:S(2)}, u32[]{:S(2)}) collective-permute-start(bf16[64,512]{1,0:T(8,128)(2,1)S(1)} %get-tuple-element.55), channel_id=1, source_target_pairs={{0,3},{1,0},{2,1},{3,2},{4,7},{5,4},{6,5},{7,6},{8,11},{9,8},{10,9... | collective-permute-start | bytes 196616 | tf_op jit(solution)/shard_map/ppermute | solution.py:40
  34.6 1.3 %collective-permute-done.12.refs_1_ = bf16[64,512]{1,0:T(8,128)(2,1)S(1)} collective-permute-done((bf16[64,512]{1,0:T(8,128)(2,1)S(1)}, bf16[64,512]{1,0:T(8,128)(2,1)S(1)}, u32[]{:S(2)}, u32[]{:S(2)}) %collective-permute-start.12) | collective-permute-done | bytes 65568 | tf_op jit(solution)/shard_map/ppermute | solution.py:40
  36.0 2.6 %collective-permute-done.13.refs_2_ = bf16[64,512]{1,0:T(8,128)(2,1)S(1)} collective-permute-done((bf16[64,512]{1,0:T(8,128)(2,1)S(1)}, bf16[64,512]{1,0:T(8,128)(2,1)S(1)}, u32[]{:S(2)}, u32[]{:S(2)}) %collective-permute-start.13) | collective-permute-done | bytes 65568 | tf_op jit(solution)/shard_map/ppermute | solution.py:40
  40.1 2.2 %collective-permute-start.19 = (bf16[128,512]{1,0:T(8,128)(2,1)S(1)}, bf16[128,512]{1,0:T(8,128)(2,1)S(1)}, u32[]{:S(2)}, u32[]{:S(2)}) collective-permute-start(bf16[128,512]{1,0:T(8,128)(2,1)S(1)} %pad_maximum_fusion), channel_id=1, source_target_pairs={{0,8},{4,28},{8,0},{12,20},{16,24},{20,12},{24,16},{28,4},{1,9},{5... | collective-permute-start | bytes 393224 | tf_op jit(solution)/shard_map/ppermute | solution.py:51
  42.9 1.7 %collective-permute-start.16 = (bf16[64,512]{1,0:T(8,128)(2,1)S(1)}, bf16[64,512]{1,0:T(8,128)(2,1)S(1)}, u32[]{:S(2)}, u32[]{:S(2)}) collective-permute-start(bf16[64,512]{1,0:T(8,128)(2,1)S(1)} %get-tuple-element.64), channel_id=1, source_target_pairs={{0,1},{1,2},{2,3},{3,0},{4,5},{5,6},{6,7},{7,4},{8,9},{9,10},{10,1... | collective-permute-start | bytes 196616 | tf_op jit(solution)/shard_map/ppermute | solution.py:40
  44.7 4.4 %collective-permute-done.16.refs_1_ = bf16[64,512]{1,0:T(8,128)(2,1)S(1)} collective-permute-done((bf16[64,512]{1,0:T(8,128)(2,1)S(1)}, bf16[64,512]{1,0:T(8,128)(2,1)S(1)}, u32[]{:S(2)}, u32[]{:S(2)}) %collective-permute-start.16) | collective-permute-done | bytes 65568 | tf_op jit(solution)/shard_map/ppermute | solution.py:40
  49.1 2.2 %collective-permute-start.18 = (bf16[64,512]{1,0:T(8,128)(2,1)S(1)}, bf16[64,512]{1,0:T(8,128)(2,1)S(1)}, u32[]{:S(2)}, u32[]{:S(2)}) collective-permute-start(bf16[64,512]{1,0:T(8,128)(2,1)S(1)} %get-tuple-element.68), channel_id=1, source_target_pairs={{0,3},{1,0},{2,1},{3,2},{4,7},{5,4},{6,5},{7,6},{8,11},{9,8},{10,9... | collective-permute-start | bytes 196616 | tf_op jit(solution)/shard_map/ppermute | solution.py:40
  51.3 1.7 %shard_map.83 = (f32[64,512]{1,0:T(8,128)S(1)}, bf16[64,512]{1,0:T(8,128)(2,1)S(1)}, bf16[64,512]{1,0:T(8,128)(2,1)S(1)}, bf16[64,512]{1,0:T(8,128)(2,1)S(1)}) custom-call(s32[2]{0:T(128)S(1)} %pad_add_fusion.2.meta.refs_0_, s32[145]{0:T(256)S(1)} %select_reduce_fusion.1.items.refs_1_, s32[273]{0:T(512)S(1)} %select_reduce_fusion.refs_2_, ...), custom_call_target="tpu_custom_call" | custom-call | flops 3000000000 | tf_op jit(solution)/shard_map/pallas_call | solution.py:461
  53.1 2.7 %collective-permute-start.22 = (bf16[64,512]{1,0:T(8,128)(2,1)S(1)}, bf16[64,512]{1,0:T(8,128)(2,1)S(1)}, u32[]{:S(2)}, u32[]{:S(2)}) collective-permute-start(bf16[64,512]{1,0:T(8,128)(2,1)S(1)} %get-tuple-element.74), channel_id=1, source_target_pairs={{0,2},{1,3},{2,0},{3,1},{4,6},{5,7},{6,4},{7,5},{8,10},{9,11},{10,... | collective-permute-start | bytes 196616 | tf_op jit(solution)/shard_map/ppermute | solution.py:40
  57.0 3.0 %collective-permute-done.21.refs_5_ = bf16[64,512]{1,0:T(8,128)(2,1)S(1)} collective-permute-done((bf16[64,512]{1,0:T(8,128)(2,1)S(1)}, bf16[64,512]{1,0:T(8,128)(2,1)S(1)}, u32[]{:S(2)}, u32[]{:S(2)}) %collective-permute-start.21) | collective-permute-done | bytes 65568 | tf_op jit(solution)/shard_map/ppermute | solution.py:40
  59.9 1.7 %collective-permute-done.22.refs_6_ = bf16[64,512]{1,0:T(8,128)(2,1)S(1)} collective-permute-done((bf16[64,512]{1,0:T(8,128)(2,1)S(1)}, bf16[64,512]{1,0:T(8,128)(2,1)S(1)}, u32[]{:S(2)}, u32[]{:S(2)}) %collective-permute-start.22) | collective-permute-done | bytes 65568 | tf_op jit(solution)/shard_map/ppermute | solution.py:40
  62.8 1.3 %collective-permute-done.24 = f32[240,128]{1,0:T(8,128)S(1)} collective-permute-done((f32[240,128]{1,0:T(8,128)S(1)}, f32[240,128]{1,0:T(8,128)S(1)}, u32[]{:S(2)}, u32[]{:S(2)}) %collective-permute-start.24) | collective-permute-done | bytes 122912 | tf_op jit(solution)/shard_map/ppermute | solution.py:35
  64.2 1.7 %collective-permute-start.27 = (f32[240,128]{1,0:T(8,128)S(1)}, f32[240,128]{1,0:T(8,128)S(1)}, u32[]{:S(2)}, u32[]{:S(2)}) collective-permute-start(f32[240,128]{1,0:T(8,128)S(1)} %add.159), channel_id=1, source_target_pairs={{0,24},{1,25},{2,26},{3,27},{4,7},{5,4},{6,5},{7,6},{8,16},{9,17},... | collective-permute-start | bytes 368648 | tf_op jit(solution)/shard_map/ppermute | solution.py:85
  65.9 1.4 %collective-permute-start.26 = (f32[240,128]{1,0:T(8,128)S(1)}, f32[240,128]{1,0:T(8,128)S(1)}, u32[]{:S(2)}, u32[]{:S(2)}) collective-permute-start(f32[240,128]{1,0:T(8,128)S(1)} %add.159), channel_id=1, source_target_pairs={{0,16},{1,17},{2,18},{3,19},{4,6},{5,7},{6,4},{7,5},{8,24},{9,25},... | collective-permute-start | bytes 368648 | tf_op jit(solution)/shard_map/ppermute | solution.py:85
  67.7 2.3 %collective-permute-done.27 = f32[240,128]{1,0:T(8,128)S(1)} collective-permute-done((f32[240,128]{1,0:T(8,128)S(1)}, f32[240,128]{1,0:T(8,128)S(1)}, u32[]{:S(2)}, u32[]{:S(2)}) %collective-permute-start.27) | collective-permute-done | bytes 122912 | tf_op jit(solution)/shard_map/ppermute | solution.py:85
  70.1 1.3 %collective-permute-done.26 = f32[240,128]{1,0:T(8,128)S(1)} collective-permute-done((f32[240,128]{1,0:T(8,128)S(1)}, f32[240,128]{1,0:T(8,128)S(1)}, u32[]{:S(2)}, u32[]{:S(2)}) %collective-permute-start.26) | collective-permute-done | bytes 122912 | tf_op jit(solution)/shard_map/ppermute | solution.py:85
  72.2 1.8 %collective-permute-start.30 = (f32[240,128]{1,0:T(8,128)S(1)}, f32[240,128]{1,0:T(8,128)S(1)}, u32[]{:S(2)}, u32[]{:S(2)}) collective-permute-start(f32[240,128]{1,0:T(8,128)S(1)} %add_add_fusion.1), channel_id=1, source_target_pairs={{0,3},{1,0},{2,1},{3,2},{4,28},{5,29},{6,30},{7,31},{8,11},{9,8},{... | collective-permute-start | bytes 368648 | tf_op jit(solution)/shard_map/ppermute | solution.py:85
  75.0 2.1 %collective-permute-done.30 = f32[240,128]{1,0:T(8,128)S(1)} collective-permute-done((f32[240,128]{1,0:T(8,128)S(1)}, f32[240,128]{1,0:T(8,128)S(1)}, u32[]{:S(2)}, u32[]{:S(2)}) %collective-permute-start.30) | collective-permute-done | bytes 122912 | tf_op jit(solution)/shard_map/ppermute | solution.py:85
  77.1 5.0 %collective-permute-done.29 = f32[240,128]{1,0:T(8,128)S(1)} collective-permute-done((f32[240,128]{1,0:T(8,128)S(1)}, f32[240,128]{1,0:T(8,128)S(1)}, u32[]{:S(2)}, u32[]{:S(2)}) %collective-permute-start.29) | collective-permute-done | bytes 122912 | tf_op jit(solution)/shard_map/ppermute | solution.py:85
  82.2 1.3 %collective-permute-done.31.other = f32[240,128]{1,0:T(8,128)S(1)} collective-permute-done((f32[240,128]{1,0:T(8,128)S(1)}, f32[240,128]{1,0:T(8,128)S(1)}, u32[]{:S(2)}, u32[]{:S(2)}) %collective-permute-start.31) | collective-permute-done | bytes 122912 | tf_op jit(solution)/shard_map/ppermute | solution.py:35
  83.5 4.2 %shard_map.85 = (f32[64,512]{1,0:T(8,128)}, f32[64,512]{1,0:T(8,128)}) custom-call(s32[2]{0:T(128)S(1)} %pad_add_fusion.2.meta.refs_0_, f32[2,64,192]{2,1,0:T(8,128)S(1)} %bitcast.11, f32[192,512]{1,0:T(8,128)S(1)} %get-tuple-element.59.rows, f32[64,512]{1,0:T(8,128)S(1)} %get-tuple-element.76.t_ref, f32[64,512]{1,0:T(8,128)S(1)} %get-tuple-element.77.q_ref, ...), custom_call_target="tpu_custom_call" | custom-call | flops 3200000000 | tf_op jit(solution)/shard_map/pallas_call | solution.py:461
  (81 shorter events, 13.9 us)
Async XLA Ops:
  2.4 20.0 %collective-permute-start.5 = (bf16[512,256]{1,0:T(8,128)(2,1)S(1)}, bf16[512,256]{1,0:T(8,128)(2,1)S(1)}, u32[]{:S(2)}, u32[]{:S(2)}) collective-permute-start(bf16[512,256]{1,0:T(8,128)(2,1)S(1)} %get-tuple-element.41), channel_id=1, source_target_pairs={{0,24},{4,28},{8,16},{12,20},{16,8},{20,12},{24,0},{28,4},{1,25},{... | collective-permute-start | bytes 786440 | tf_op jit(solution)/shard_map/ppermute | solution.py:51
  6.3 16.0 %collective-permute-start.3 = (bf16[512,256]{1,0:T(8,128)(2,1)S(1)}, bf16[512,256]{1,0:T(8,128)(2,1)S(1)}, u32[]{:S(2)}, u32[]{:S(2)}) collective-permute-start(bf16[512,256]{1,0:T(8,128)(2,1)S(1)} %get-tuple-element.41), channel_id=1, source_target_pairs={{0,8},{4,12},{8,0},{12,4},{16,24},{20,28},{24,16},{28,20},{1,9},{5... | collective-permute-start | bytes 786440 | tf_op jit(solution)/shard_map/ppermute | solution.py:35
  6.8 1.5 %collective-permute-start = (bf16[512,256]{1,0:T(8,128)(2,1)S(1)}, bf16[512,256]{1,0:T(8,128)(2,1)S(1)}, u32[]{:S(2)}, u32[]{:S(2)}) collective-permute-start(bf16[512,256]{1,0:T(8,128)(2,1)S(1)} %get-tuple-element.41), channel_id=1, source_target_pairs={{0,4},{4,0},{8,12},{12,8},{16,20},{20,16},{24,28},{28,24},{1,5},{5... | collective-permute-start | bytes 786440 | tf_op jit(solution)/shard_map/ppermute | solution.py:35
  8.4 3.9 %collective-permute-start.1 = (s32[16,12]{1,0:T(8,128)}, s32[16,12]{1,0:T(8,128)S(1)}, u32[]{:S(2)}, u32[]{:S(2)}) collective-permute-start(s32[16,12]{1,0:T(8,128)} %param.10), channel_id=1, source_target_pairs={{0,1},{1,0},{2,3},{3,2},{4,5},{5,4},{6,7},{7,6},{8,9},{9,8},{10,11... | collective-permute-start | bytes 2312 | tf_op jit(solution)/shard_map/ppermute | solution.py:35
  10.0 13.0 %collective-permute-start.10 = (bf16[128,512]{1,0:T(8,128)(2,1)S(1)}, bf16[128,512]{1,0:T(8,128)(2,1)S(1)}, u32[]{:S(2)}, u32[]{:S(2)}) collective-permute-start(bf16[128,512]{1,0:T(8,128)(2,1)S(1)} %get-tuple-element.49.refs_9_), channel_id=1, source_target_pairs={{0,24},{4,28},{8,16},{12,20},{16,8},{20,12},{24,0},{28,4},{1,25},{... | collective-permute-start | bytes 393224 | tf_op jit(solution)/shard_map/ppermute | solution.py:51
  11.4 12.7 %collective-permute-start.8 = (bf16[128,512]{1,0:T(8,128)(2,1)S(1)}, bf16[128,512]{1,0:T(8,128)(2,1)S(1)}, u32[]{:S(2)}, u32[]{:S(2)}) collective-permute-start(bf16[128,512]{1,0:T(8,128)(2,1)S(1)} %get-tuple-element.49.refs_9_), channel_id=1, source_target_pairs={{0,8},{4,12},{8,0},{12,4},{16,24},{20,28},{24,16},{28,20},{1,9},{5... | collective-permute-start | bytes 393224 | tf_op jit(solution)/shard_map/ppermute | solution.py:35
  13.0 5.3 %collective-permute-start.2 = (s32[16,24]{1,0:T(8,128)S(1)}, s32[16,24]{1,0:T(8,128)S(1)}, u32[]{:S(2)}, u32[]{:S(2)}) collective-permute-start(s32[16,24]{1,0:T(8,128)S(1)} %pad_add_fusion), channel_id=1, source_target_pairs={{0,2},{1,3},{2,0},{3,1},{4,6},{5,7},{6,4},{7,5},{8,10},{9,11},{10,... | collective-permute-start | bytes 4616 | tf_op jit(solution)/shard_map/ppermute | solution.py:35
  18.3 6.8 %collective-permute-start.7 = (bf16[128,512]{1,0:T(8,128)(2,1)S(1)}, bf16[128,512]{1,0:T(8,128)(2,1)S(1)}, u32[]{:S(2)}, u32[]{:S(2)}) collective-permute-start(bf16[128,512]{1,0:T(8,128)(2,1)S(1)} %get-tuple-element.49.refs_9_), channel_id=1, source_target_pairs={{0,4},{4,0},{8,12},{12,8},{16,20},{20,16},{24,28},{28,24},{1,5},{5... | collective-permute-start | bytes 393224 | tf_op jit(solution)/shard_map/ppermute | solution.py:35
  22.3 3.3 %collective-permute-start.4 = (bf16[512,256]{1,0:T(8,128)(2,1)S(1)}, bf16[512,256]{1,0:T(8,128)(2,1)S(1)}, u32[]{:S(2)}, u32[]{:S(2)}) collective-permute-start(bf16[512,256]{1,0:T(8,128)(2,1)S(1)} %collective-permute-done.3.refs_5_), channel_id=1, source_target_pairs={{0,4},{4,0},{8,12},{12,8},{16,20},{20,16},{24,28},{28,24},{1,5},{5... | collective-permute-start | bytes 786440 | tf_op jit(solution)/shard_map/ppermute | solution.py:35
  22.9 2.8 %collective-permute-start.6 = (bf16[512,256]{1,0:T(8,128)(2,1)S(1)}, bf16[512,256]{1,0:T(8,128)(2,1)S(1)}, u32[]{:S(2)}, u32[]{:S(2)}) collective-permute-start(bf16[512,256]{1,0:T(8,128)(2,1)S(1)} %collective-permute-done.5.refs_7_), channel_id=1, source_target_pairs={{0,4},{4,0},{8,12},{12,8},{16,20},{20,16},{24,28},{28,24},{1,5},{5... | collective-permute-start | bytes 786440 | tf_op jit(solution)/shard_map/ppermute | solution.py:35
  24.1 1.3 %collective-permute-start.9 = (bf16[128,512]{1,0:T(8,128)(2,1)S(1)}, bf16[128,512]{1,0:T(8,128)(2,1)S(1)}, u32[]{:S(2)}, u32[]{:S(2)}) collective-permute-start(bf16[128,512]{1,0:T(8,128)(2,1)S(1)} %collective-permute-done.8.refs_11_), channel_id=1, source_target_pairs={{0,4},{4,0},{8,12},{12,8},{16,20},{20,16},{24,28},{28,24},{1,5},{5... | collective-permute-start | bytes 393224 | tf_op jit(solution)/shard_map/ppermute | solution.py:35
  24.1 1.5 %collective-permute-start.11 = (bf16[128,512]{1,0:T(8,128)(2,1)S(1)}, bf16[128,512]{1,0:T(8,128)(2,1)S(1)}, u32[]{:S(2)}, u32[]{:S(2)}) collective-permute-start(bf16[128,512]{1,0:T(8,128)(2,1)S(1)} %collective-permute-done.10.refs_13_), channel_id=1, source_target_pairs={{0,4},{4,0},{8,12},{12,8},{16,20},{20,16},{24,28},{28,24},{1,5},{5... | collective-permute-start | bytes 393224 | tf_op jit(solution)/shard_map/ppermute | solution.py:35
  29.1 6.9 %collective-permute-start.12 = (bf16[64,512]{1,0:T(8,128)(2,1)S(1)}, bf16[64,512]{1,0:T(8,128)(2,1)S(1)}, u32[]{:S(2)}, u32[]{:S(2)}) collective-permute-start(bf16[64,512]{1,0:T(8,128)(2,1)S(1)} %get-tuple-element.53), channel_id=1, source_target_pairs={{0,1},{1,2},{2,3},{3,0},{4,5},{5,6},{6,7},{7,4},{8,9},{9,10},{10,1... | collective-permute-start | bytes 196616 | tf_op jit(solution)/shard_map/ppermute | solution.py:40
  30.7 7.8 %collective-permute-start.13 = (bf16[64,512]{1,0:T(8,128)(2,1)S(1)}, bf16[64,512]{1,0:T(8,128)(2,1)S(1)}, u32[]{:S(2)}, u32[]{:S(2)}) collective-permute-start(bf16[64,512]{1,0:T(8,128)(2,1)S(1)} %get-tuple-element.54), channel_id=1, source_target_pairs={{0,2},{1,3},{2,0},{3,1},{4,6},{5,7},{6,4},{7,5},{8,10},{9,11},{10,... | collective-permute-start | bytes 196616 | tf_op jit(solution)/shard_map/ppermute | solution.py:40
  33.3 5.4 %collective-permute-start.14 = (bf16[64,512]{1,0:T(8,128)(2,1)S(1)}, bf16[64,512]{1,0:T(8,128)(2,1)S(1)}, u32[]{:S(2)}, u32[]{:S(2)}) collective-permute-start(bf16[64,512]{1,0:T(8,128)(2,1)S(1)} %get-tuple-element.55), channel_id=1, source_target_pairs={{0,3},{1,0},{2,1},{3,2},{4,7},{5,4},{6,5},{7,6},{8,11},{9,8},{10,9... | collective-permute-start | bytes 196616 | tf_op jit(solution)/shard_map/ppermute | solution.py:40
  38.8 1.3 %collective-permute-start.15 = (bf16[64,512]{1,0:T(8,128)(2,1)S(1)}, bf16[64,512]{1,0:T(8,128)(2,1)S(1)}, u32[]{:S(2)}, u32[]{:S(2)}) collective-permute-start(bf16[64,512]{1,0:T(8,128)(2,1)S(1)} %get-tuple-element.57.refs_5_), channel_id=1, source_target_pairs={{0,4},{4,0},{8,12},{12,8},{16,20},{20,16},{24,28},{28,24},{1,5},{5... | collective-permute-start | bytes 196616 | tf_op jit(solution)/shard_map/ppermute | solution.py:35
  40.1 8.9 %collective-permute-start.19 = (bf16[128,512]{1,0:T(8,128)(2,1)S(1)}, bf16[128,512]{1,0:T(8,128)(2,1)S(1)}, u32[]{:S(2)}, u32[]{:S(2)}) collective-permute-start(bf16[128,512]{1,0:T(8,128)(2,1)S(1)} %pad_maximum_fusion), channel_id=1, source_target_pairs={{0,8},{4,28},{8,0},{12,20},{16,24},{20,12},{24,16},{28,4},{1,9},{5... | collective-permute-start | bytes 393224 | tf_op jit(solution)/shard_map/ppermute | solution.py:51
  42.9 6.1 %collective-permute-start.16 = (bf16[64,512]{1,0:T(8,128)(2,1)S(1)}, bf16[64,512]{1,0:T(8,128)(2,1)S(1)}, u32[]{:S(2)}, u32[]{:S(2)}) collective-permute-start(bf16[64,512]{1,0:T(8,128)(2,1)S(1)} %get-tuple-element.64), channel_id=1, source_target_pairs={{0,1},{1,2},{2,3},{3,0},{4,5},{5,6},{6,7},{7,4},{8,9},{9,10},{10,1... | collective-permute-start | bytes 196616 | tf_op jit(solution)/shard_map/ppermute | solution.py:40
  49.0 2.3 %collective-permute-start.20 = (bf16[128,512]{1,0:T(8,128)(2,1)S(1)}, bf16[128,512]{1,0:T(8,128)(2,1)S(1)}, u32[]{:S(2)}, u32[]{:S(2)}) collective-permute-start(bf16[128,512]{1,0:T(8,128)(2,1)S(1)} %collective-permute-done.19.refs_7_), channel_id=1, source_target_pairs={{0,4},{4,0},{8,12},{12,8},{16,20},{20,16},{24,28},{28,24},{1,5},{5... | collective-permute-start | bytes 393224 | tf_op jit(solution)/shard_map/ppermute | solution.py:35
  49.0 7.9 %collective-permute-start.17 = (bf16[64,512]{1,0:T(8,128)(2,1)S(1)}, bf16[64,512]{1,0:T(8,128)(2,1)S(1)}, u32[]{:S(2)}, u32[]{:S(2)}) collective-permute-start(bf16[64,512]{1,0:T(8,128)(2,1)S(1)} %get-tuple-element.66), channel_id=1, source_target_pairs={{0,2},{1,3},{2,0},{3,1},{4,6},{5,7},{6,4},{7,5},{8,10},{9,11},{10,... | collective-permute-start | bytes 196616 | tf_op jit(solution)/shard_map/ppermute | solution.py:40
  49.1 7.9 %collective-permute-start.18 = (bf16[64,512]{1,0:T(8,128)(2,1)S(1)}, bf16[64,512]{1,0:T(8,128)(2,1)S(1)}, u32[]{:S(2)}, u32[]{:S(2)}) collective-permute-start(bf16[64,512]{1,0:T(8,128)(2,1)S(1)} %get-tuple-element.68), channel_id=1, source_target_pairs={{0,3},{1,0},{2,1},{3,2},{4,7},{5,4},{6,5},{7,6},{8,11},{9,8},{10,9... | collective-permute-start | bytes 196616 | tf_op jit(solution)/shard_map/ppermute | solution.py:40
  53.1 6.9 %collective-permute-start.21 = (bf16[64,512]{1,0:T(8,128)(2,1)S(1)}, bf16[64,512]{1,0:T(8,128)(2,1)S(1)}, u32[]{:S(2)}, u32[]{:S(2)}) collective-permute-start(bf16[64,512]{1,0:T(8,128)(2,1)S(1)} %get-tuple-element.73), channel_id=1, source_target_pairs={{0,1},{1,2},{2,3},{3,0},{4,5},{5,6},{6,7},{7,4},{8,9},{9,10},{10,1... | collective-permute-start | bytes 196616 | tf_op jit(solution)/shard_map/ppermute | solution.py:40
  53.1 8.6 %collective-permute-start.22 = (bf16[64,512]{1,0:T(8,128)(2,1)S(1)}, bf16[64,512]{1,0:T(8,128)(2,1)S(1)}, u32[]{:S(2)}, u32[]{:S(2)}) collective-permute-start(bf16[64,512]{1,0:T(8,128)(2,1)S(1)} %get-tuple-element.74), channel_id=1, source_target_pairs={{0,2},{1,3},{2,0},{3,1},{4,6},{5,7},{6,4},{7,5},{8,10},{9,11},{10,... | collective-permute-start | bytes 196616 | tf_op jit(solution)/shard_map/ppermute | solution.py:40
  55.8 5.9 %collective-permute-start.23 = (bf16[64,512]{1,0:T(8,128)(2,1)S(1)}, bf16[64,512]{1,0:T(8,128)(2,1)S(1)}, u32[]{:S(2)}, u32[]{:S(2)}) collective-permute-start(bf16[64,512]{1,0:T(8,128)(2,1)S(1)} %get-tuple-element.75), channel_id=1, source_target_pairs={{0,3},{1,0},{2,1},{3,2},{4,7},{5,4},{6,5},{7,6},{8,11},{9,8},{10,9... | collective-permute-start | bytes 196616 | tf_op jit(solution)/shard_map/ppermute | solution.py:40
  62.8 1.4 %collective-permute-start.24 = (f32[240,128]{1,0:T(8,128)S(1)}, f32[240,128]{1,0:T(8,128)S(1)}, u32[]{:S(2)}, u32[]{:S(2)}) collective-permute-start(f32[240,128]{1,0:T(8,128)S(1)} %get-tuple-element.79), channel_id=1, source_target_pairs={{0,4},{4,0},{8,12},{12,8},{16,20},{20,16},{24,28},{28,24},{1,5},{5... | collective-permute-start | bytes 368648 | tf_op jit(solution)/shard_map/ppermute | solution.py:35
  64.2 5.9 %collective-permute-start.27 = (f32[240,128]{1,0:T(8,128)S(1)}, f32[240,128]{1,0:T(8,128)S(1)}, u32[]{:S(2)}, u32[]{:S(2)}) collective-permute-start(f32[240,128]{1,0:T(8,128)S(1)} %add.159), channel_id=1, source_target_pairs={{0,24},{1,25},{2,26},{3,27},{4,7},{5,4},{6,5},{7,6},{8,16},{9,17},... | collective-permute-start | bytes 368648 | tf_op jit(solution)/shard_map/ppermute | solution.py:85
  65.9 5.4 %collective-permute-start.26 = (f32[240,128]{1,0:T(8,128)S(1)}, f32[240,128]{1,0:T(8,128)S(1)}, u32[]{:S(2)}, u32[]{:S(2)}) collective-permute-start(f32[240,128]{1,0:T(8,128)S(1)} %add.159), channel_id=1, source_target_pairs={{0,16},{1,17},{2,18},{3,19},{4,6},{5,7},{6,4},{7,5},{8,24},{9,25},... | collective-permute-start | bytes 368648 | tf_op jit(solution)/shard_map/ppermute | solution.py:85
  67.2 4.9 %collective-permute-start.25 = (f32[240,128]{1,0:T(8,128)S(1)}, f32[240,128]{1,0:T(8,128)S(1)}, u32[]{:S(2)}, u32[]{:S(2)}) collective-permute-start(f32[240,128]{1,0:T(8,128)S(1)} %add.159), channel_id=1, source_target_pairs={{0,8},{1,9},{2,10},{3,11},{4,5},{5,6},{6,7},{7,4},{8,0},{9,1},{10,... | collective-permute-start | bytes 368648 | tf_op jit(solution)/shard_map/ppermute | solution.py:85
  72.2 4.9 %collective-permute-start.30 = (f32[240,128]{1,0:T(8,128)S(1)}, f32[240,128]{1,0:T(8,128)S(1)}, u32[]{:S(2)}, u32[]{:S(2)}) collective-permute-start(f32[240,128]{1,0:T(8,128)S(1)} %add_add_fusion.1), channel_id=1, source_target_pairs={{0,3},{1,0},{2,1},{3,2},{4,28},{5,29},{6,30},{7,31},{8,11},{9,8},{... | collective-permute-start | bytes 368648 | tf_op jit(solution)/shard_map/ppermute | solution.py:85
  74.0 8.1 %collective-permute-start.29 = (f32[240,128]{1,0:T(8,128)S(1)}, f32[240,128]{1,0:T(8,128)S(1)}, u32[]{:S(2)}, u32[]{:S(2)}) collective-permute-start(f32[240,128]{1,0:T(8,128)S(1)} %add_add_fusion.1), channel_id=1, source_target_pairs={{0,2},{1,3},{2,0},{3,1},{4,20},{5,21},{6,22},{7,23},{8,10},{9,11},... | collective-permute-start | bytes 368648 | tf_op jit(solution)/shard_map/ppermute | solution.py:85
  75.0 7.1 %collective-permute-start.28 = (f32[240,128]{1,0:T(8,128)S(1)}, f32[240,128]{1,0:T(8,128)S(1)}, u32[]{:S(2)}, u32[]{:S(2)}) collective-permute-start(f32[240,128]{1,0:T(8,128)S(1)} %add_add_fusion.1), channel_id=1, source_target_pairs={{0,1},{1,2},{2,3},{3,0},{4,12},{5,13},{6,14},{7,15},{8,9},{9,10},{... | collective-permute-start | bytes 368648 | tf_op jit(solution)/shard_map/ppermute | solution.py:85
  82.1 1.4 %collective-permute-start.31 = (f32[240,128]{1,0:T(8,128)S(1)}, f32[240,128]{1,0:T(8,128)S(1)}, u32[]{:S(2)}, u32[]{:S(2)}) collective-permute-start(f32[240,128]{1,0:T(8,128)S(1)} %add_add_fusion.mine), channel_id=1, source_target_pairs={{0,4},{4,0},{8,12},{12,8},{16,20},{20,16},{24,28},{28,24},{1,5},{5... | collective-permute-start | bytes 368648 | tf_op jit(solution)/shard_map/ppermute | solution.py:35
  (5 other events, 83.2 us)

commit v5 on v4

--- a/solution.py
+++ b/solution.py
@@ -98,7 +98,7 @@
 
 def unit_of(rows):
     values = rows.astype(F32)
-    mean = jnp.sum(values * values, axis=1, keepdims=True) * (1.0 / EMB)
+    mean = jnp.sum(values * values, axis=-1, keepdims=True) * (1.0 / EMB)
     return (values * lax.rsqrt(mean + EPS)).astype(BF16)
 
 
@@ -152,10 +152,8 @@
         copy.start()
     for n, copy in enumerate(copies):
         copy.wait()
-
-        @pl.loop(n * each, (n + 1) * each)
-        def _(b):
-            unit[b] = unit_of(buf[b])
+        at = pl.ds(n * each, each)
+        unit[at] = unit_of(buf[at])
 
 
 def near_kernel(
@@ -412,7 +410,15 @@
     split_by_core(meta[1], packed, keep, send)
 
 
-def last_kernel(total, meta, rot_ref, rows, t_ref, q_ref, mine, other, v_out, s_out):
+def deep_kernel(rows, t_ref, q_ref, out):
+    high, low = halves_of(jnp.concatenate([rows[...], t_ref[...], q_ref[...]], axis=0))
+    depth = high.shape[0]
+    out[:depth, :] = high
+    out[depth : 2 * depth, :] = low
+    out[2 * depth :, :] = high
+
+
+def last_kernel(total, meta, rot_ref, deep, mine, other, v_out, s_out):
     packed = joined(meta[1], mine, other)
     coef, gram, known = first_step(packed[: 3 * K], rot_ref[0], total)
     packed = packed[3 * K :]
@@ -448,7 +454,10 @@
         ],
         axis=1,
     )
-    both = scale * mul3(both, jnp.concatenate([rows[...], t_ref[...], q_ref[...]], axis=0))
+    high, low = halves_of(both)
+    both = scale * jnp.dot(
+        jnp.concatenate([high, high, low], axis=1), deep[...], preferred_element_type=F32
+    )
     v_out[...], s_out[...] = both[:K], both[K:]
 
 
@@ -648,15 +657,16 @@
         smem=1,
         us=1.3,
     )
+    (deep,) = call(
+        deep_kernel, [((15 * K, width), BF16)], rows, step_image, twice, us=0.5
+    )
     products = sum_chips(sum_chips(keep + swapped(send, "rows", 1), 0), 1)
     return call(
         functools.partial(last_kernel, total),
         [((K, width), F32)] * 2,
         meta,
         rotations.swapaxes(1, 2),
-        rows,
-        step_image,
-        twice,
+        deep,
         products,
         swapped(products, "rows", 1),
         smem=1,

time: 87.4 us -> 86.6 us (level)
  Pallas kernels: 17.9 us -> 17 us
    ppermute x6, waiting for transfers between devices: 11.5 us -> 10.1 us  [sum_chips(): parts.append(lax.ppermute(value, ('rows', 'tiles'), pairs))]
    ppermute x14, waiting for transfers between devices: 7.22 us -> 8.2 us  [swapped(): return lax.ppermute(value, axis, [(i, i ^ bits) for i in range(count)])]
    pallas_call x9 -> x10, Pallas kernels: 17.9 us -> 17 us  [call(): pl.pallas_call(kernel, out_shape=tuple((pltpu.HBM(*out[:2]) if len(out) >...]
  transfers between devices with their start and end apart: 32 -> 32, of which waited for: 19 -> 20; matrix products, arithmetic and copies ran while one was open for 3% -> 3% of each run, Pallas kernels for 9% -> 8%
where the time goes in v5:
time: 86.6 us
  starting transfers between devices  34.5 us (40%)
  waiting for transfers between devices  31.4 us (36%)
  Pallas kernels  17 us (20%)
  other arithmetic  2.16 us (2%)
  between operations  0.93 us (1%)
    pallas_call x10, Pallas kernels, call(): pl.pallas_call(kernel, out_shape=tuple((pltpu.HBM(*out[:2]) if len(out) >...  17 us
    ppermute x9, starting transfers between devices, rotated(): lax.ppermute(value, axis, [(i, (i + steps) % count) for i in range(count)])  14 us
    ppermute x9, waiting for transfers between devices, rotated(): lax.ppermute(value, axis, [(i, (i + steps) % count) for i in range(count)])  13 us
    ppermute x6, waiting for transfers between devices, sum_chips(): parts.append(lax.ppermute(value, ('rows', 'tiles'), pairs))  10.1 us
    ppermute x14, waiting for transfers between devices, swapped(): return lax.ppermute(value, axis, [(i, i ^ bits) for i in range(count)])  8.2 us
    ppermute x3, starting transfers between devices, other_side(): return lax.ppermute(value, 'rows', pairs)  7.22 us
    ppermute x6, starting transfers between devices, sum_chips(): parts.append(lax.ppermute(value, ('rows', 'tiles'), pairs))  6.69 us
    ppermute x14, starting transfers between devices, swapped(): return lax.ppermute(value, axis, [(i, i ^ bits) for i in range(count)])  6.61 us
  transfers between devices with their start and end apart: 32, of which 20 were waited for; matrix products, arithmetic and copies ran while one was open for 3% of the time, Pallas kernels for 8%

profile of v5, /device:TPU:0, one launch (start us, length us, event | category | flops | bytes accessed | tf_op | source)
XLA Modules:
  0.0 86.6 jit_solution(9870053443216549580)
XLA Ops:
  0.7 1.6 %shard_map.77 = (bf16[512,256]{1,0:T(8,128)(2,1)S(1)}, bf16[128,512]{1,0:T(8,128)(2,1)S(1)}) custom-call(s32[2]{0:T(128)S(1)} %pad_add_fusion.2.meta.refs_0_, bf16[2048,256]{1,0:T(8,128)(2,1)} %emb.1, f32[64,512]{1,0:T(8,128)} %x_ref.1, f32[64,512]{1,0:T(8,128)} %step.3), custom_call_target="tpu_custom_call" | custom-call | flops 1000000000 | tf_op jit(solution)/shard_map/pallas_call | solution.py:470
  2.4 4.0 %collective-permute-start.5 = (bf16[512,256]{1,0:T(8,128)(2,1)S(1)}, bf16[512,256]{1,0:T(8,128)(2,1)S(1)}, u32[]{:S(2)}, u32[]{:S(2)}) collective-permute-start(bf16[512,256]{1,0:T(8,128)(2,1)S(1)} %get-tuple-element.41), channel_id=1, source_target_pairs={{0,24},{4,28},{8,16},{12,20},{16,8},{20,12},{24,0},{28,4},{1,25},{... | collective-permute-start | bytes 786440 | tf_op jit(solution)/shard_map/ppermute | solution.py:51
  7.0 1.4 %collective-permute-done.emb_core = bf16[512,256]{1,0:T(8,128)(2,1)S(1)} collective-permute-done((bf16[512,256]{1,0:T(8,128)(2,1)S(1)}, bf16[512,256]{1,0:T(8,128)(2,1)S(1)}, u32[]{:S(2)}, u32[]{:S(2)}) %collective-permute-start) | collective-permute-done | bytes 262176 | tf_op jit(solution)/shard_map/ppermute | solution.py:35
  8.4 1.6 %collective-permute-start.1 = (s32[16,12]{1,0:T(8,128)}, s32[16,12]{1,0:T(8,128)S(1)}, u32[]{:S(2)}, u32[]{:S(2)}) collective-permute-start(s32[16,12]{1,0:T(8,128)} %param.10), channel_id=1, source_target_pairs={{0,1},{1,0},{2,3},{3,2},{4,5},{5,4},{6,7},{7,6},{8,9},{9,8},{10,11... | collective-permute-start | bytes 2312 | tf_op jit(solution)/shard_map/ppermute | solution.py:35
  10.0 1.4 %collective-permute-start.10 = (bf16[128,512]{1,0:T(8,128)(2,1)S(1)}, bf16[128,512]{1,0:T(8,128)(2,1)S(1)}, u32[]{:S(2)}, u32[]{:S(2)}) collective-permute-start(bf16[128,512]{1,0:T(8,128)(2,1)S(1)} %get-tuple-element.49.refs_9_), channel_id=1, source_target_pairs={{0,24},{4,28},{8,16},{12,20},{16,8},{20,12},{24,0},{28,4},{1,25},{... | collective-permute-start | bytes 393224 | tf_op jit(solution)/shard_map/ppermute | solution.py:51
  13.0 2.6 %collective-permute-start.2 = (s32[16,24]{1,0:T(8,128)S(1)}, s32[16,24]{1,0:T(8,128)S(1)}, u32[]{:S(2)}, u32[]{:S(2)}) collective-permute-start(s32[16,24]{1,0:T(8,128)S(1)} %pad_add_fusion), channel_id=1, source_target_pairs={{0,2},{1,3},{2,0},{3,1},{4,6},{5,7},{6,4},{7,5},{8,10},{9,11},{10,... | collective-permute-start | bytes 4616 | tf_op jit(solution)/shard_map/ppermute | solution.py:35
  15.6 1.6 %shard_map.78.unit_own.refs_4_ = bf16[16,128,256]{2,1,0:T(8,128)(2,1)S(1)} custom-call(bf16[16,128,256]{2,1,0:T(8,128)(2,1)} %bitcast.13), custom_call_target="tpu_custom_call" | custom-call | flops 2600000000 | tf_op jit(solution)/shard_map/pallas_call | solution.py:470
  18.9 2.6 %shard_map.79 = (f32[1,512]{1,0:T(1,128)S(1)}, bf16[148,128,128]{2,1,0:T(8,128)(2,1)}) custom-call(s32[2]{0:T(128)S(1)} %pad_add_fusion.2.meta.refs_0_, s32[145]{0:T(256)S(1)} %select_reduce_fusion.1.items.refs_1_, bf16[16,128,256]{2,1,0:T(8,128)(2,1)S(1)} %shard_map.78.unit_own.refs_4_, bf16[512,256]{1,0:T(8,128)(2,1)S(1)} %collective-permute-done.emb_core), custom_call_target="tpu_custom_call" | custom-call | flops 2000000000 | tf_op jit(solution)/shard_map/pallas_call | solution.py:470
  22.2 1.9 %collective-permute-done.8.refs_11_ = bf16[128,512]{1,0:T(8,128)(2,1)S(1)} collective-permute-done((bf16[128,512]{1,0:T(8,128)(2,1)S(1)}, bf16[128,512]{1,0:T(8,128)(2,1)S(1)}, u32[]{:S(2)}, u32[]{:S(2)}) %collective-permute-start.8) | collective-permute-done | bytes 131104 | tf_op jit(solution)/shard_map/ppermute | solution.py:35
  25.7 3.4 %shard_map.80 = (f32[64,512]{1,0:T(8,128)S(1)}, bf16[64,512]{1,0:T(8,128)(2,1)S(1)}, bf16[64,512]{1,0:T(8,128)(2,1)S(1)}, bf16[64,512]{1,0:T(8,128)(2,1)S(1)}, f...) custom-call(s32[2]{0:T(128)S(1)} %pad_add_fusion.2.meta.refs_0_, ...), custom_call_target="tpu_custom_call" | custom-call | flops 5000000000 | tf_op jit(solution)/shard_map/pallas_call | solution.py:470
  29.1 1.6 %collective-permute-start.12 = (bf16[64,512]{1,0:T(8,128)(2,1)S(1)}, bf16[64,512]{1,0:T(8,128)(2,1)S(1)}, u32[]{:S(2)}, u32[]{:S(2)}) collective-permute-start(bf16[64,512]{1,0:T(8,128)(2,1)S(1)} %get-tuple-element.53), channel_id=1, source_target_pairs={{0,1},{1,2},{2,3},{3,0},{4,5},{5,6},{6,7},{7,4},{8,9},{9,10},{10,1... | collective-permute-start | bytes 196616 | tf_op jit(solution)/shard_map/ppermute | solution.py:40
  30.7 2.6 %collective-permute-start.13 = (bf16[64,512]{1,0:T(8,128)(2,1)S(1)}, bf16[64,512]{1,0:T(8,128)(2,1)S(1)}, u32[]{:S(2)}, u32[]{:S(2)}) collective-permute-start(bf16[64,512]{1,0:T(8,128)(2,1)S(1)} %get-tuple-element.54), channel_id=1, source_target_pairs={{0,2},{1,3},{2,0},{3,1},{4,6},{5,7},{6,4},{7,5},{8,10},{9,11},{10,... | collective-permute-start | bytes 196616 | tf_op jit(solution)/shard_map/ppermute | solution.py:40
  33.3 1.4 %collective-permute-start.14 = (bf16[64,512]{1,0:T(8,128)(2,1)S(1)}, bf16[64,512]{1,0:T(8,128)(2,1)S(1)}, u32[]{:S(2)}, u32[]{:S(2)}) collective-permute-start(bf16[64,512]{1,0:T(8,128)(2,1)S(1)} %get-tuple-element.55), channel_id=1, source_target_pairs={{0,3},{1,0},{2,1},{3,2},{4,7},{5,4},{6,5},{7,6},{8,11},{9,8},{10,9... | collective-permute-start | bytes 196616 | tf_op jit(solution)/shard_map/ppermute | solution.py:40
  35.7 2.8 %collective-permute-done.13.refs_2_ = bf16[64,512]{1,0:T(8,128)(2,1)S(1)} collective-permute-done((bf16[64,512]{1,0:T(8,128)(2,1)S(1)}, bf16[64,512]{1,0:T(8,128)(2,1)S(1)}, u32[]{:S(2)}, u32[]{:S(2)}) %collective-permute-start.13) | collective-permute-done | bytes 65568 | tf_op jit(solution)/shard_map/ppermute | solution.py:40
  38.9 1.2 %collective-permute-done.15.refs_6_ = bf16[64,512]{1,0:T(8,128)(2,1)S(1)} collective-permute-done((bf16[64,512]{1,0:T(8,128)(2,1)S(1)}, bf16[64,512]{1,0:T(8,128)(2,1)S(1)}, u32[]{:S(2)}, u32[]{:S(2)}) %collective-permute-start.15) | collective-permute-done | bytes 65568 | tf_op jit(solution)/shard_map/ppermute | solution.py:35
  40.2 1.8 %collective-permute-start.19 = (bf16[128,512]{1,0:T(8,128)(2,1)S(1)}, bf16[128,512]{1,0:T(8,128)(2,1)S(1)}, u32[]{:S(2)}, u32[]{:S(2)}) collective-permute-start(bf16[128,512]{1,0:T(8,128)(2,1)S(1)} %pad_maximum_fusion), channel_id=1, source_target_pairs={{0,8},{4,28},{8,0},{12,20},{16,24},{20,12},{24,16},{28,4},{1,9},{5... | collective-permute-start | bytes 393224 | tf_op jit(solution)/shard_map/ppermute | solution.py:51
  42.6 2.0 %collective-permute-start.16 = (bf16[64,512]{1,0:T(8,128)(2,1)S(1)}, bf16[64,512]{1,0:T(8,128)(2,1)S(1)}, u32[]{:S(2)}, u32[]{:S(2)}) collective-permute-start(bf16[64,512]{1,0:T(8,128)(2,1)S(1)} %get-tuple-element.64), channel_id=1, source_target_pairs={{0,1},{1,2},{2,3},{3,0},{4,5},{5,6},{6,7},{7,4},{8,9},{9,10},{10,1... | collective-permute-start | bytes 196616 | tf_op jit(solution)/shard_map/ppermute | solution.py:40
  44.6 4.1 %collective-permute-done.16.refs_1_ = bf16[64,512]{1,0:T(8,128)(2,1)S(1)} collective-permute-done((bf16[64,512]{1,0:T(8,128)(2,1)S(1)}, bf16[64,512]{1,0:T(8,128)(2,1)S(1)}, u32[]{:S(2)}, u32[]{:S(2)}) %collective-permute-start.16) | collective-permute-done | bytes 65568 | tf_op jit(solution)/shard_map/ppermute | solution.py:40
  48.7 2.5 %collective-permute-start.18 = (bf16[64,512]{1,0:T(8,128)(2,1)S(1)}, bf16[64,512]{1,0:T(8,128)(2,1)S(1)}, u32[]{:S(2)}, u32[]{:S(2)}) collective-permute-start(bf16[64,512]{1,0:T(8,128)(2,1)S(1)} %get-tuple-element.68), channel_id=1, source_target_pairs={{0,3},{1,0},{2,1},{3,2},{4,7},{5,4},{6,5},{7,6},{8,11},{9,8},{10,9... | collective-permute-start | bytes 196616 | tf_op jit(solution)/shard_map/ppermute | solution.py:40
  51.3 1.7 %shard_map.83 = (f32[64,512]{1,0:T(8,128)S(1)}, bf16[64,512]{1,0:T(8,128)(2,1)S(1)}, bf16[64,512]{1,0:T(8,128)(2,1)S(1)}, bf16[64,512]{1,0:T(8,128)(2,1)S(1)}) custom-call(s32[2]{0:T(128)S(1)} %pad_add_fusion.2.meta.refs_0_, s32[145]{0:T(256)S(1)} %select_reduce_fusion.1.items.refs_1_, s32[273]{0:T(512)S(1)} %select_reduce_fusion.refs_2_, ...), custom_call_target="tpu_custom_call" | custom-call | flops 3000000000 | tf_op jit(solution)/shard_map/pallas_call | solution.py:470
  53.1 2.4 %collective-permute-start.22 = (bf16[64,512]{1,0:T(8,128)(2,1)S(1)}, bf16[64,512]{1,0:T(8,128)(2,1)S(1)}, u32[]{:S(2)}, u32[]{:S(2)}) collective-permute-start(bf16[64,512]{1,0:T(8,128)(2,1)S(1)} %get-tuple-element.74), channel_id=1, source_target_pairs={{0,2},{1,3},{2,0},{3,1},{4,6},{5,7},{6,4},{7,5},{8,10},{9,11},{10,... | collective-permute-start | bytes 196616 | tf_op jit(solution)/shard_map/ppermute | solution.py:40
  55.5 1.4 %collective-permute-start.23 = (bf16[64,512]{1,0:T(8,128)(2,1)S(1)}, bf16[64,512]{1,0:T(8,128)(2,1)S(1)}, u32[]{:S(2)}, u32[]{:S(2)}) collective-permute-start(bf16[64,512]{1,0:T(8,128)(2,1)S(1)} %get-tuple-element.75), channel_id=1, source_target_pairs={{0,3},{1,0},{2,1},{3,2},{4,7},{5,4},{6,5},{7,6},{8,11},{9,8},{10,9... | collective-permute-start | bytes 196616 | tf_op jit(solution)/shard_map/ppermute | solution.py:40
  56.9 3.0 %collective-permute-done.21.refs_5_ = bf16[64,512]{1,0:T(8,128)(2,1)S(1)} collective-permute-done((bf16[64,512]{1,0:T(8,128)(2,1)S(1)}, bf16[64,512]{1,0:T(8,128)(2,1)S(1)}, u32[]{:S(2)}, u32[]{:S(2)}) %collective-permute-start.21) | collective-permute-done | bytes 65568 | tf_op jit(solution)/shard_map/ppermute | solution.py:40
  59.9 1.7 %collective-permute-done.22.refs_6_ = bf16[64,512]{1,0:T(8,128)(2,1)S(1)} collective-permute-done((bf16[64,512]{1,0:T(8,128)(2,1)S(1)}, bf16[64,512]{1,0:T(8,128)(2,1)S(1)}, u32[]{:S(2)}, u32[]{:S(2)}) %collective-permute-start.22) | collective-permute-done | bytes 65568 | tf_op jit(solution)/shard_map/ppermute | solution.py:40
  62.8 1.3 %collective-permute-done.24 = f32[240,128]{1,0:T(8,128)S(1)} collective-permute-done((f32[240,128]{1,0:T(8,128)S(1)}, f32[240,128]{1,0:T(8,128)S(1)}, u32[]{:S(2)}, u32[]{:S(2)}) %collective-permute-start.24) | collective-permute-done | bytes 122912 | tf_op jit(solution)/shard_map/ppermute | solution.py:35
  64.5 1.7 %collective-permute-start.26 = (f32[240,128]{1,0:T(8,128)S(1)}, f32[240,128]{1,0:T(8,128)S(1)}, u32[]{:S(2)}, u32[]{:S(2)}) collective-permute-start(f32[240,128]{1,0:T(8,128)S(1)} %add.159), channel_id=1, source_target_pairs={{0,16},{1,17},{2,18},{3,19},{4,6},{5,7},{6,4},{7,5},{8,24},{9,25},... | collective-permute-start | bytes 368648 | tf_op jit(solution)/shard_map/ppermute | solution.py:85
  66.1 1.5 %collective-permute-start.25 = (f32[240,128]{1,0:T(8,128)S(1)}, f32[240,128]{1,0:T(8,128)S(1)}, u32[]{:S(2)}, u32[]{:S(2)}) collective-permute-start(f32[240,128]{1,0:T(8,128)S(1)} %add.159), channel_id=1, source_target_pairs={{0,8},{1,9},{2,10},{3,11},{4,5},{5,6},{6,7},{7,4},{8,0},{9,1},{10,... | collective-permute-start | bytes 368648 | tf_op jit(solution)/shard_map/ppermute | solution.py:85
  67.7 2.4 %collective-permute-done.27 = f32[240,128]{1,0:T(8,128)S(1)} collective-permute-done((f32[240,128]{1,0:T(8,128)S(1)}, f32[240,128]{1,0:T(8,128)S(1)}, u32[]{:S(2)}, u32[]{:S(2)}) %collective-permute-start.27) | collective-permute-done | bytes 122912 | tf_op jit(solution)/shard_map/ppermute | solution.py:85
  71.1 2.5 %collective-permute-start.30 = (f32[240,128]{1,0:T(8,128)S(1)}, f32[240,128]{1,0:T(8,128)S(1)}, u32[]{:S(2)}, u32[]{:S(2)}) collective-permute-start(f32[240,128]{1,0:T(8,128)S(1)} %add_add_fusion.1), channel_id=1, source_target_pairs={{0,3},{1,0},{2,1},{3,2},{4,28},{5,29},{6,30},{7,31},{8,11},{9,8},{... | collective-permute-start | bytes 368648 | tf_op jit(solution)/shard_map/ppermute | solution.py:85
  74.2 1.8 %collective-permute-done.30 = f32[240,128]{1,0:T(8,128)S(1)} collective-permute-done((f32[240,128]{1,0:T(8,128)S(1)}, f32[240,128]{1,0:T(8,128)S(1)}, u32[]{:S(2)}, u32[]{:S(2)}) %collective-permute-start.30) | collective-permute-done | bytes 122912 | tf_op jit(solution)/shard_map/ppermute | solution.py:85
  76.0 5.0 %collective-permute-done.29 = f32[240,128]{1,0:T(8,128)S(1)} collective-permute-done((f32[240,128]{1,0:T(8,128)S(1)}, f32[240,128]{1,0:T(8,128)S(1)}, u32[]{:S(2)}, u32[]{:S(2)}) %collective-permute-start.29) | collective-permute-done | bytes 122912 | tf_op jit(solution)/shard_map/ppermute | solution.py:85
  82.4 4.1 %shard_map.86 = (f32[64,512]{1,0:T(8,128)}, f32[64,512]{1,0:T(8,128)}) custom-call(s32[2]{0:T(128)S(1)} %pad_add_fusion.2.meta.refs_0_, f32[2,64,192]{2,1,0:T(8,128)S(1)} %bitcast.11, bf16[960,512]{1,0:T(8,128)(2,1)S(1)} %shard_map.85.deep, f32[240,128]{1,0:T(8,128)S(1)} %add_add_fusion.mine, f32[240,128]{1,0:T(8,128)S(1)} %collective-permute-done.31.other), custom_call_target="tpu_custom_call" | custom-call | flops 3200000000 | tf_op jit(solution)/shard_map/pallas_call | solution.py:470
  (82 shorter events, 12.8 us)
Async XLA Ops:
  2.4 19.2 %collective-permute-start.5 = (bf16[512,256]{1,0:T(8,128)(2,1)S(1)}, bf16[512,256]{1,0:T(8,128)(2,1)S(1)}, u32[]{:S(2)}, u32[]{:S(2)}) collective-permute-start(bf16[512,256]{1,0:T(8,128)(2,1)S(1)} %get-tuple-element.41), channel_id=1, source_target_pairs={{0,24},{4,28},{8,16},{12,20},{16,8},{20,12},{24,0},{28,4},{1,25},{... | collective-permute-start | bytes 786440 | tf_op jit(solution)/shard_map/ppermute | solution.py:51
  6.3 15.2 %collective-permute-start.3 = (bf16[512,256]{1,0:T(8,128)(2,1)S(1)}, bf16[512,256]{1,0:T(8,128)(2,1)S(1)}, u32[]{:S(2)}, u32[]{:S(2)}) collective-permute-start(bf16[512,256]{1,0:T(8,128)(2,1)S(1)} %get-tuple-element.41), channel_id=1, source_target_pairs={{0,8},{4,12},{8,0},{12,4},{16,24},{20,28},{24,16},{28,20},{1,9},{5... | collective-permute-start | bytes 786440 | tf_op jit(solution)/shard_map/ppermute | solution.py:35
  6.8 1.5 %collective-permute-start = (bf16[512,256]{1,0:T(8,128)(2,1)S(1)}, bf16[512,256]{1,0:T(8,128)(2,1)S(1)}, u32[]{:S(2)}, u32[]{:S(2)}) collective-permute-start(bf16[512,256]{1,0:T(8,128)(2,1)S(1)} %get-tuple-element.41), channel_id=1, source_target_pairs={{0,4},{4,0},{8,12},{12,8},{16,20},{20,16},{24,28},{28,24},{1,5},{5... | collective-permute-start | bytes 786440 | tf_op jit(solution)/shard_map/ppermute | solution.py:35
  8.4 3.9 %collective-permute-start.1 = (s32[16,12]{1,0:T(8,128)}, s32[16,12]{1,0:T(8,128)S(1)}, u32[]{:S(2)}, u32[]{:S(2)}) collective-permute-start(s32[16,12]{1,0:T(8,128)} %param.10), channel_id=1, source_target_pairs={{0,1},{1,0},{2,3},{3,2},{4,5},{5,4},{6,7},{7,6},{8,9},{9,8},{10,11... | collective-permute-start | bytes 2312 | tf_op jit(solution)/shard_map/ppermute | solution.py:35
  10.0 12.2 %collective-permute-start.10 = (bf16[128,512]{1,0:T(8,128)(2,1)S(1)}, bf16[128,512]{1,0:T(8,128)(2,1)S(1)}, u32[]{:S(2)}, u32[]{:S(2)}) collective-permute-start(bf16[128,512]{1,0:T(8,128)(2,1)S(1)} %get-tuple-element.49.refs_9_), channel_id=1, source_target_pairs={{0,24},{4,28},{8,16},{12,20},{16,8},{20,12},{24,0},{28,4},{1,25},{... | collective-permute-start | bytes 393224 | tf_op jit(solution)/shard_map/ppermute | solution.py:51
  11.4 12.7 %collective-permute-start.8 = (bf16[128,512]{1,0:T(8,128)(2,1)S(1)}, bf16[128,512]{1,0:T(8,128)(2,1)S(1)}, u32[]{:S(2)}, u32[]{:S(2)}) collective-permute-start(bf16[128,512]{1,0:T(8,128)(2,1)S(1)} %get-tuple-element.49.refs_9_), channel_id=1, source_target_pairs={{0,8},{4,12},{8,0},{12,4},{16,24},{20,28},{24,16},{28,20},{1,9},{5... | collective-permute-start | bytes 393224 | tf_op jit(solution)/shard_map/ppermute | solution.py:35
  13.0 4.6 %collective-permute-start.2 = (s32[16,24]{1,0:T(8,128)S(1)}, s32[16,24]{1,0:T(8,128)S(1)}, u32[]{:S(2)}, u32[]{:S(2)}) collective-permute-start(s32[16,24]{1,0:T(8,128)S(1)} %pad_add_fusion), channel_id=1, source_target_pairs={{0,2},{1,3},{2,0},{3,1},{4,6},{5,7},{6,4},{7,5},{8,10},{9,11},{10,... | collective-permute-start | bytes 4616 | tf_op jit(solution)/shard_map/ppermute | solution.py:35
  17.6 7.6 %collective-permute-start.7 = (bf16[128,512]{1,0:T(8,128)(2,1)S(1)}, bf16[128,512]{1,0:T(8,128)(2,1)S(1)}, u32[]{:S(2)}, u32[]{:S(2)}) collective-permute-start(bf16[128,512]{1,0:T(8,128)(2,1)S(1)} %get-tuple-element.49.refs_9_), channel_id=1, source_target_pairs={{0,4},{4,0},{8,12},{12,8},{16,20},{20,16},{24,28},{28,24},{1,5},{5... | collective-permute-start | bytes 393224 | tf_op jit(solution)/shard_map/ppermute | solution.py:35
  21.5 4.1 %collective-permute-start.4 = (bf16[512,256]{1,0:T(8,128)(2,1)S(1)}, bf16[512,256]{1,0:T(8,128)(2,1)S(1)}, u32[]{:S(2)}, u32[]{:S(2)}) collective-permute-start(bf16[512,256]{1,0:T(8,128)(2,1)S(1)} %collective-permute-done.3.refs_5_), channel_id=1, source_target_pairs={{0,4},{4,0},{8,12},{12,8},{16,20},{20,16},{24,28},{28,24},{1,5},{5... | collective-permute-start | bytes 786440 | tf_op jit(solution)/shard_map/ppermute | solution.py:35
  22.1 3.5 %collective-permute-start.6 = (bf16[512,256]{1,0:T(8,128)(2,1)S(1)}, bf16[512,256]{1,0:T(8,128)(2,1)S(1)}, u32[]{:S(2)}, u32[]{:S(2)}) collective-permute-start(bf16[512,256]{1,0:T(8,128)(2,1)S(1)} %collective-permute-done.5.refs_7_), channel_id=1, source_target_pairs={{0,4},{4,0},{8,12},{12,8},{16,20},{20,16},{24,28},{28,24},{1,5},{5... | collective-permute-start | bytes 786440 | tf_op jit(solution)/shard_map/ppermute | solution.py:35
  24.1 1.3 %collective-permute-start.9 = (bf16[128,512]{1,0:T(8,128)(2,1)S(1)}, bf16[128,512]{1,0:T(8,128)(2,1)S(1)}, u32[]{:S(2)}, u32[]{:S(2)}) collective-permute-start(bf16[128,512]{1,0:T(8,128)(2,1)S(1)} %collective-permute-done.8.refs_11_), channel_id=1, source_target_pairs={{0,4},{4,0},{8,12},{12,8},{16,20},{20,16},{24,28},{28,24},{1,5},{5... | collective-permute-start | bytes 393224 | tf_op jit(solution)/shard_map/ppermute | solution.py:35
  24.1 1.5 %collective-permute-start.11 = (bf16[128,512]{1,0:T(8,128)(2,1)S(1)}, bf16[128,512]{1,0:T(8,128)(2,1)S(1)}, u32[]{:S(2)}, u32[]{:S(2)}) collective-permute-start(bf16[128,512]{1,0:T(8,128)(2,1)S(1)} %collective-permute-done.10.refs_13_), channel_id=1, source_target_pairs={{0,4},{4,0},{8,12},{12,8},{16,20},{20,16},{24,28},{28,24},{1,5},{5... | collective-permute-start | bytes 393224 | tf_op jit(solution)/shard_map/ppermute | solution.py:35
  29.1 6.6 %collective-permute-start.12 = (bf16[64,512]{1,0:T(8,128)(2,1)S(1)}, bf16[64,512]{1,0:T(8,128)(2,1)S(1)}, u32[]{:S(2)}, u32[]{:S(2)}) collective-permute-start(bf16[64,512]{1,0:T(8,128)(2,1)S(1)} %get-tuple-element.53), channel_id=1, source_target_pairs={{0,1},{1,2},{2,3},{3,0},{4,5},{5,6},{6,7},{7,4},{8,9},{9,10},{10,1... | collective-permute-start | bytes 196616 | tf_op jit(solution)/shard_map/ppermute | solution.py:40
  30.7 7.8 %collective-permute-start.13 = (bf16[64,512]{1,0:T(8,128)(2,1)S(1)}, bf16[64,512]{1,0:T(8,128)(2,1)S(1)}, u32[]{:S(2)}, u32[]{:S(2)}) collective-permute-start(bf16[64,512]{1,0:T(8,128)(2,1)S(1)} %get-tuple-element.54), channel_id=1, source_target_pairs={{0,2},{1,3},{2,0},{3,1},{4,6},{5,7},{6,4},{7,5},{8,10},{9,11},{10,... | collective-permute-start | bytes 196616 | tf_op jit(solution)/shard_map/ppermute | solution.py:40
  33.3 5.5 %collective-permute-start.14 = (bf16[64,512]{1,0:T(8,128)(2,1)S(1)}, bf16[64,512]{1,0:T(8,128)(2,1)S(1)}, u32[]{:S(2)}, u32[]{:S(2)}) collective-permute-start(bf16[64,512]{1,0:T(8,128)(2,1)S(1)} %get-tuple-element.55), channel_id=1, source_target_pairs={{0,3},{1,0},{2,1},{3,2},{4,7},{5,4},{6,5},{7,6},{8,11},{9,8},{10,9... | collective-permute-start | bytes 196616 | tf_op jit(solution)/shard_map/ppermute | solution.py:40
  38.9 1.3 %collective-permute-start.15 = (bf16[64,512]{1,0:T(8,128)(2,1)S(1)}, bf16[64,512]{1,0:T(8,128)(2,1)S(1)}, u32[]{:S(2)}, u32[]{:S(2)}) collective-permute-start(bf16[64,512]{1,0:T(8,128)(2,1)S(1)} %get-tuple-element.57.refs_5_), channel_id=1, source_target_pairs={{0,4},{4,0},{8,12},{12,8},{16,20},{20,16},{24,28},{28,24},{1,5},{5... | collective-permute-start | bytes 196616 | tf_op jit(solution)/shard_map/ppermute | solution.py:35
  40.2 8.5 %collective-permute-start.19 = (bf16[128,512]{1,0:T(8,128)(2,1)S(1)}, bf16[128,512]{1,0:T(8,128)(2,1)S(1)}, u32[]{:S(2)}, u32[]{:S(2)}) collective-permute-start(bf16[128,512]{1,0:T(8,128)(2,1)S(1)} %pad_maximum_fusion), channel_id=1, source_target_pairs={{0,8},{4,28},{8,0},{12,20},{16,24},{20,12},{24,16},{28,4},{1,9},{5... | collective-permute-start | bytes 393224 | tf_op jit(solution)/shard_map/ppermute | solution.py:51
  42.6 6.1 %collective-permute-start.16 = (bf16[64,512]{1,0:T(8,128)(2,1)S(1)}, bf16[64,512]{1,0:T(8,128)(2,1)S(1)}, u32[]{:S(2)}, u32[]{:S(2)}) collective-permute-start(bf16[64,512]{1,0:T(8,128)(2,1)S(1)} %get-tuple-element.64), channel_id=1, source_target_pairs={{0,1},{1,2},{2,3},{3,0},{4,5},{5,6},{6,7},{7,4},{8,9},{9,10},{10,1... | collective-permute-start | bytes 196616 | tf_op jit(solution)/shard_map/ppermute | solution.py:40
  48.7 2.5 %collective-permute-start.20 = (bf16[128,512]{1,0:T(8,128)(2,1)S(1)}, bf16[128,512]{1,0:T(8,128)(2,1)S(1)}, u32[]{:S(2)}, u32[]{:S(2)}) collective-permute-start(bf16[128,512]{1,0:T(8,128)(2,1)S(1)} %collective-permute-done.19.refs_7_), channel_id=1, source_target_pairs={{0,4},{4,0},{8,12},{12,8},{16,20},{20,16},{24,28},{28,24},{1,5},{5... | collective-permute-start | bytes 393224 | tf_op jit(solution)/shard_map/ppermute | solution.py:35
  48.7 8.2 %collective-permute-start.17 = (bf16[64,512]{1,0:T(8,128)(2,1)S(1)}, bf16[64,512]{1,0:T(8,128)(2,1)S(1)}, u32[]{:S(2)}, u32[]{:S(2)}) collective-permute-start(bf16[64,512]{1,0:T(8,128)(2,1)S(1)} %get-tuple-element.66), channel_id=1, source_target_pairs={{0,2},{1,3},{2,0},{3,1},{4,6},{5,7},{6,4},{7,5},{8,10},{9,11},{10,... | collective-permute-start | bytes 196616 | tf_op jit(solution)/shard_map/ppermute | solution.py:40
  48.7 8.2 %collective-permute-start.18 = (bf16[64,512]{1,0:T(8,128)(2,1)S(1)}, bf16[64,512]{1,0:T(8,128)(2,1)S(1)}, u32[]{:S(2)}, u32[]{:S(2)}) collective-permute-start(bf16[64,512]{1,0:T(8,128)(2,1)S(1)} %get-tuple-element.68), channel_id=1, source_target_pairs={{0,3},{1,0},{2,1},{3,2},{4,7},{5,4},{6,5},{7,6},{8,11},{9,8},{10,9... | collective-permute-start | bytes 196616 | tf_op jit(solution)/shard_map/ppermute | solution.py:40
  53.0 6.9 %collective-permute-start.21 = (bf16[64,512]{1,0:T(8,128)(2,1)S(1)}, bf16[64,512]{1,0:T(8,128)(2,1)S(1)}, u32[]{:S(2)}, u32[]{:S(2)}) collective-permute-start(bf16[64,512]{1,0:T(8,128)(2,1)S(1)} %get-tuple-element.73), channel_id=1, source_target_pairs={{0,1},{1,2},{2,3},{3,0},{4,5},{5,6},{6,7},{7,4},{8,9},{9,10},{10,1... | collective-permute-start | bytes 196616 | tf_op jit(solution)/shard_map/ppermute | solution.py:40
  53.1 8.6 %collective-permute-start.22 = (bf16[64,512]{1,0:T(8,128)(2,1)S(1)}, bf16[64,512]{1,0:T(8,128)(2,1)S(1)}, u32[]{:S(2)}, u32[]{:S(2)}) collective-permute-start(bf16[64,512]{1,0:T(8,128)(2,1)S(1)} %get-tuple-element.74), channel_id=1, source_target_pairs={{0,2},{1,3},{2,0},{3,1},{4,6},{5,7},{6,4},{7,5},{8,10},{9,11},{10,... | collective-permute-start | bytes 196616 | tf_op jit(solution)/shard_map/ppermute | solution.py:40
  55.5 6.1 %collective-permute-start.23 = (bf16[64,512]{1,0:T(8,128)(2,1)S(1)}, bf16[64,512]{1,0:T(8,128)(2,1)S(1)}, u32[]{:S(2)}, u32[]{:S(2)}) collective-permute-start(bf16[64,512]{1,0:T(8,128)(2,1)S(1)} %get-tuple-element.75), channel_id=1, source_target_pairs={{0,3},{1,0},{2,1},{3,2},{4,7},{5,4},{6,5},{7,6},{8,11},{9,8},{10,9... | collective-permute-start | bytes 196616 | tf_op jit(solution)/shard_map/ppermute | solution.py:40
  62.7 1.4 %collective-permute-start.24 = (f32[240,128]{1,0:T(8,128)S(1)}, f32[240,128]{1,0:T(8,128)S(1)}, u32[]{:S(2)}, u32[]{:S(2)}) collective-permute-start(f32[240,128]{1,0:T(8,128)S(1)} %get-tuple-element.79), channel_id=1, source_target_pairs={{0,4},{4,0},{8,12},{12,8},{16,20},{20,16},{24,28},{28,24},{1,5},{5... | collective-permute-start | bytes 368648 | tf_op jit(solution)/shard_map/ppermute | solution.py:35
  64.1 5.9 %collective-permute-start.27 = (f32[240,128]{1,0:T(8,128)S(1)}, f32[240,128]{1,0:T(8,128)S(1)}, u32[]{:S(2)}, u32[]{:S(2)}) collective-permute-start(f32[240,128]{1,0:T(8,128)S(1)} %add.159), channel_id=1, source_target_pairs={{0,24},{1,25},{2,26},{3,27},{4,7},{5,4},{6,5},{7,6},{8,16},{9,17},... | collective-permute-start | bytes 368648 | tf_op jit(solution)/shard_map/ppermute | solution.py:85
  64.5 6.2 %collective-permute-start.26 = (f32[240,128]{1,0:T(8,128)S(1)}, f32[240,128]{1,0:T(8,128)S(1)}, u32[]{:S(2)}, u32[]{:S(2)}) collective-permute-start(f32[240,128]{1,0:T(8,128)S(1)} %add.159), channel_id=1, source_target_pairs={{0,16},{1,17},{2,18},{3,19},{4,6},{5,7},{6,4},{7,5},{8,24},{9,25},... | collective-permute-start | bytes 368648 | tf_op jit(solution)/shard_map/ppermute | solution.py:85
  66.1 4.9 %collective-permute-start.25 = (f32[240,128]{1,0:T(8,128)S(1)}, f32[240,128]{1,0:T(8,128)S(1)}, u32[]{:S(2)}, u32[]{:S(2)}) collective-permute-start(f32[240,128]{1,0:T(8,128)S(1)} %add.159), channel_id=1, source_target_pairs={{0,8},{1,9},{2,10},{3,11},{4,5},{5,6},{6,7},{7,4},{8,0},{9,1},{10,... | collective-permute-start | bytes 368648 | tf_op jit(solution)/shard_map/ppermute | solution.py:85
  71.1 5.0 %collective-permute-start.30 = (f32[240,128]{1,0:T(8,128)S(1)}, f32[240,128]{1,0:T(8,128)S(1)}, u32[]{:S(2)}, u32[]{:S(2)}) collective-permute-start(f32[240,128]{1,0:T(8,128)S(1)} %add_add_fusion.1), channel_id=1, source_target_pairs={{0,3},{1,0},{2,1},{3,2},{4,28},{5,29},{6,30},{7,31},{8,11},{9,8},{... | collective-permute-start | bytes 368648 | tf_op jit(solution)/shard_map/ppermute | solution.py:85
  73.6 7.4 %collective-permute-start.29 = (f32[240,128]{1,0:T(8,128)S(1)}, f32[240,128]{1,0:T(8,128)S(1)}, u32[]{:S(2)}, u32[]{:S(2)}) collective-permute-start(f32[240,128]{1,0:T(8,128)S(1)} %add_add_fusion.1), channel_id=1, source_target_pairs={{0,2},{1,3},{2,0},{3,1},{4,20},{5,21},{6,22},{7,23},{8,10},{9,11},... | collective-permute-start | bytes 368648 | tf_op jit(solution)/shard_map/ppermute | solution.py:85
  73.9 7.1 %collective-permute-start.28 = (f32[240,128]{1,0:T(8,128)S(1)}, f32[240,128]{1,0:T(8,128)S(1)}, u32[]{:S(2)}, u32[]{:S(2)}) collective-permute-start(f32[240,128]{1,0:T(8,128)S(1)} %add_add_fusion.1), channel_id=1, source_target_pairs={{0,1},{1,2},{2,3},{3,0},{4,12},{5,13},{6,14},{7,15},{8,9},{9,10},{... | collective-permute-start | bytes 368648 | tf_op jit(solution)/shard_map/ppermute | solution.py:85
  81.0 1.4 %collective-permute-start.31 = (f32[240,128]{1,0:T(8,128)S(1)}, f32[240,128]{1,0:T(8,128)S(1)}, u32[]{:S(2)}, u32[]{:S(2)}) collective-permute-start(f32[240,128]{1,0:T(8,128)S(1)} %add_add_fusion.mine), channel_id=1, source_target_pairs={{0,4},{4,0},{8,12},{12,8},{16,20},{20,16},{24,28},{28,24},{1,5},{5... | collective-permute-start | bytes 368648 | tf_op jit(solution)/shard_map/ppermute | solution.py:35
  (5 other events, 80.4 us)
